TPU v7x, 32 devices: a whole 2x2x4 slice. The times are simulated.
32 devices in a mesh: groups: 2 (over y), tensor: 8 (over z, x), dp: 2 (over core).
Axes of the slice: x: 2, y: 2, z: 4, core: 2. Of those that a mesh axis runs over, the one named last changes fastest.
Arguments:
- tokens: bfloat16 [512, 8192], P(('groups', 'dp'), 'tensor'), parts along dimension 0, may hold values from -6 to 6
- cotangent: bfloat16 [512, 8192], P(('groups', 'dp'), 'tensor'), parts along dimension 0, may hold values from -6 to 6
- fwd_values: bfloat16 [16, 56, 128, 128], P(('groups', 'tensor')), parts along dimension 0, may hold values from -0.15625 to 0.15625
- fwd_ids: int32 [16, 56], P(('groups', 'tensor')), parts along dimension 0, may hold values from 0 to 191, as said below
- fwd_count: int32 [16], P(('groups', 'tensor')), parts along dimension 0, may hold values from 14 to 56
- bwd_ids: int32 [16, 96], P(('groups', 'tensor')), parts along dimension 0, may hold values from 0 to 191, as said below
- bwd_count: int32 [16], P(('groups', 'tensor')), parts along dimension 0, may hold values from 34 to 96, as said below
Outputs:
- input_grad: bfloat16 [512, 8192], P(('groups', 'dp'), 'tensor'), parts along dimension 0
- tile_grads: bfloat16 [16, 96, 128, 128], P(('groups', 'tensor')), parts along dimension 0
There are 2 independent parts, one for each index of `groups`. A program takes and returns all parts, laid end to end along the dimension named above; each array names one. Nothing has to cross between parts.
Inputs may be any that keep to these rules, and one draw needn't show every extreme that they name: `fwd_ids`: each row holds distinct numbers; e names the tile of kind e // 64 (gate, up, down) at feature block e % 64 of the owner's hidden block. Only the first fwd_count entries of a row are live. `bwd_ids`: each row holds distinct numbers, coded as in fwd_ids; the first fwd_count[o] entries of row o equal those of fwd_ids. Only the first bwd_count entries of a row are live. `bwd_count`: at least fwd_count of the same owner.
All inputs are finite; a program needn't handle non-finite values.
Results may differ from a plain program's by a relative error of at most 0.0059.
Values may be sent and summed in bfloat16 or wider, within the bound.
No kernel may reach another device: no remote copies, remote signals or barrier semaphores. Data moves between devices by JAX's collectives and lax.ppermute only.
A program may use at most 64 MiB of HBM per device.

v0:
```python
import jax
import jax.numpy as jnp
from jax import lax
from jax.sharding import PartitionSpec as P


def place_tiles(tile_set, slot_ids, slot_live, block_count):
    tile_edge = tile_set.shape[-1]
    onehot = (
        (slot_ids[:, None] == jnp.arange(3 * block_count, dtype=jnp.int32)[None, :])
        & slot_live[:, None]
    ).astype(jnp.bfloat16)
    dense_cols = jnp.einsum("sm,skn->mkn", onehot, tile_set, preferred_element_type=jnp.float32)
    return dense_cols.astype(jnp.bfloat16).reshape(3, block_count * tile_edge, tile_edge)


def on_device(tokens, cotangent, fwd_values, fwd_ids, fwd_count, bwd_ids, bwd_count):
    values = fwd_values[0]
    slot_ids = fwd_ids[0]
    slot_count = slot_ids.shape[0]
    tile_edge = values.shape[-1]
    whole_x, whole_dy = (
        lax.all_gather(tokens, "tensor", axis=1, tiled=True),
        lax.all_gather(cotangent, "tensor", axis=1, tiled=True),
    )
    row_count, feature_width = whole_x.shape
    block_count = feature_width // tile_edge
    slot_live = jnp.arange(slot_count, dtype=jnp.int32) < fwd_count[0]
    tile_kind = slot_ids // block_count
    tile_set = jnp.where((tile_kind == 2)[:, None, None], jnp.swapaxes(values, 1, 2), values)
    x_blocks_all = whole_x.reshape(row_count, block_count, tile_edge)
    dy_blocks_all = whole_dy.reshape(row_count, block_count, tile_edge)
    dense_cols = place_tiles(tile_set, slot_ids, slot_live, block_count)
    gate_pre = jnp.dot(whole_x, dense_cols[0], preferred_element_type=jnp.float32)
    up_val = jnp.dot(whole_x, dense_cols[1], preferred_element_type=jnp.float32)
    dhidden = jnp.dot(whole_dy, dense_cols[2], preferred_element_type=jnp.float32)
    sigmoid_gate = jax.nn.sigmoid(gate_pre)
    activated = gate_pre * sigmoid_gate
    hidden = (activated * up_val).astype(jnp.bfloat16)
    dgate = (dhidden * up_val * sigmoid_gate * (1.0 + gate_pre * (1.0 - sigmoid_gate))).astype(
        jnp.bfloat16
    )
    up_grad = (dhidden * activated).astype(jnp.bfloat16)
    contract = (((1,), (1,)), ((), ()))
    dx_term = lax.dot_general(dgate, dense_cols[0], contract, preferred_element_type=jnp.float32)
    dx_term = dx_term + lax.dot_general(
        up_grad, dense_cols[1], contract, preferred_element_type=jnp.float32
    )
    input_grad = lax.psum_scatter(dx_term, "tensor", scatter_dimension=1, tiled=True).astype(
        jnp.bfloat16
    )
    back_ids = bwd_ids[0]
    back_count = back_ids.shape[0]
    back_live = jnp.arange(back_count, dtype=jnp.int32) < bwd_count[0]
    back_kind = back_ids // block_count
    back_block = back_ids % block_count
    tok_sel = jnp.take(x_blocks_all, back_block, axis=1)
    dy_sel = jnp.take(dy_blocks_all, back_block, axis=1)
    left_side = jnp.where((back_kind == 2)[None, :, None], hidden[:, None, :], tok_sel)
    right_side = jnp.where(
        (back_kind == 0)[None, :, None],
        dgate[:, None, :],
        jnp.where((back_kind == 1)[None, :, None], up_grad[:, None, :], dy_sel),
    )
    local_grad = jnp.einsum(
        "tbk,tbn->bkn", left_side, right_side, preferred_element_type=jnp.float32
    )
    local_grad = jnp.where(back_live[:, None, None], local_grad, jnp.float32(0.0))
    summed_grad = lax.psum(local_grad.astype(jnp.bfloat16), "dp")
    return (input_grad, summed_grad[None])


def solution(mesh):
    return jax.shard_map(
        on_device,
        mesh=mesh,
        in_specs=(
            P(("groups", "dp"), "tensor"),
            P(("groups", "dp"), "tensor"),
            P(("groups", "tensor"), None, None, None),
            P(("groups", "tensor"), None),
            P(("groups", "tensor")),
            P(("groups", "tensor"), None),
            P(("groups", "tensor")),
        ),
        out_specs=(P(("groups", "dp"), "tensor"), P(("groups", "tensor"), None, None, None)),
        check_vma=False,
    )
```

profile of v0, /device:TPU:0, one launch (start us, length us, event | category | flops | bytes accessed | tf_op | source)
XLA Modules:
  0.0 243.3 jit_solution(8068308312874418487)
XLA Ops:
  7.2 0.0 all-gather.5.cloned.1.call-start
  7.2 1.8 copy.27
  9.0 0.0 all-gather.5.cloned.1.call-update
  9.0 0.0 all-gather.3.cloned.1.call-start
  9.1 1.8 copy.25
  10.9 0.0 copy-start.5
  10.9 0.0 copy-start.4
  10.9 0.0 all-gather.3.cloned.1.call-update
  10.9 0.0 reduce-scatter.2.cloned.1.call-start
  11.0 4.0 %copy.22 = bf16[56,128,128]{1,2,0:T(8,128)(2,1)} copy(bf16[56,128,128]{2,1,0:T(8,128)(2,1)} %bitcast.72) | data formatting | bytes 3670016 | tf_op jit(solution)/shard_map/squeeze | solution.py:18
  15.6 0.0 copy-done.5
  15.7 0.0 copy-done.4
  15.7 1.8 bitcast_select_fusion.3
  17.4 2.0 convolution_convert_fusion
  19.5 1.5 fusion.25
  21.0 1.4 copy.28
  22.3 2.7 %copy.24 = bf16[64,128,128]{2,1,0:T(8,128)(2,1)} copy(bf16[64,128,128]{2,0,1:T(8,128)(2,1)S(1)} %get-tuple-element.9) | data formatting | bytes 4194304 | tf_op jit(solution)/shard_map/slice | solution.py:36
  25.0 2.7 %copy.26 = bf16[64,128,128]{2,1,0:T(8,128)(2,1)} copy(bf16[64,128,128]{2,0,1:T(8,128)(2,1)S(1)} %get-tuple-element.7) | data formatting | bytes 4194304 | tf_op jit(solution)/shard_map/slice | solution.py:35
  27.7 35.0 %all-gather.5.cloned.1.call-done = bf16[128,8192]{0,1:T(8,128)(2,1)} async-done(((bf16[128,1024]{0,1:T(8,128)(2,1)}), bf16[128,8192]{0,1:T(8,128)(2,1)}) %all-gather.5.cloned.1.call-update) | async-done | bytes 2097168 | tf_op jit(solution)/shard_map/all_gather | solution.py:23
  62.7 2.3 convolution_bitcast_fusion
  65.1 47.6 %all-gather.3.cloned.1.call-done = bf16[128,8192]{0,1:T(8,128)(2,1)} async-done(((bf16[128,1024]{0,1:T(8,128)(2,1)}), bf16[128,8192]{0,1:T(8,128)(2,1)}) %all-gather.3.cloned.1.call-update) | async-done | bytes 2097168 | tf_op jit(solution)/shard_map/all_gather | solution.py:24
  112.6 0.0 copy-start
  112.7 0.0 copy-start.1
  112.7 3.1 %convolution_bitcast_fusion.2 = f32[128,128]{0,1:T(8,128)S(1)} fusion(bf16[8192,128]{1,0:T(8,128)(2,1)} %bitcast.71, bf16[128,8192]{0,1:T(8,128)(2,1)} %all-gather.3.cloned.1.call-done), kind=kOutput, calls=%fused_computation.24 | convolution fusion | flops 268435456 | bytes 4259840 | tf_op jit(solution)/shard_map/dot_general | solution.py:36
  115.8 0.0 copy-done
  115.8 0.3 copy-done.1
  116.1 0.8 multiply_convert_fusion
  116.9 0.7 fusion.26
  117.7 2.7 %convolution_add_fusion = f32[128,8192]{1,0:T(8,128)} fusion(f32[128,8192]{1,0:T(8,128)S(1)} %fusion.26, bf16[128,128]{0,1:T(8,128)(2,1)S(1)} %get-tuple-element.12, bf16[8192,128]{1,0:T(8,128)(2,1)S(1)} %bitcast.68), kind=kOutput, calls=%fused_computation.2 | convolution fusion | flops 269484032 | bytes 10518528 | tf_op jit(solution)/shard_map/dot_general | solution.py:46
  120.4 0.0 copy-start.6
  120.4 0.0 reduce-scatter.2.cloned.1.call-update
  120.4 0.0 all-reduce.2.cloned.1.call-start
  121.1 0.0 copy-done.6
  121.2 0.1 copy.32
  121.3 0.1 copy.31
  121.4 0.0 copy-start.2
  121.4 4.4 %copy.33 = bf16[128,64,128]{2,0,1:T(8,128)(2,1)} copy(bf16[128,64,128]{0,2,1:T(8,128)(2,1)} %bitcast.70) | data formatting | bytes 4194304 | tf_op jit(solution)/shard_map/reshape | solution.py:32
  125.8 0.0 copy-done.2
  125.8 2.9 %copy.30 = bf16[128,64,128]{2,0,1:T(8,128)(2,1)} copy(bf16[128,64,128]{0,2,1:T(8,128)(2,1)S(1)} %bitcast.69) | data formatting | bytes 4194304 | tf_op jit(solution)/shard_map/reshape | solution.py:31
  128.7 0.0 copy-start.3
  128.7 4.5 %gather_fusion.1 = bf16[96,128,128]{2,1,0:T(8,128)(2,1)} fusion(bf16[128,64,128]{2,0,1:T(8,128)(2,1)} %copy.33, s32[1024]{0:T(1024)S(1)} %pad_clamp_fusion), kind=kCustom, calls=%fused_computation.1.clone | custom fusion | bytes 6291840 | tf_op jit(solution)/shard_map/jit(_take)/gather | solution.py:58
  133.2 0.0 copy-done.3
  133.2 2.8 %gather_fusion = bf16[96,128,128]{2,1,0:T(8,128)(2,1)} fusion(bf16[128,64,128]{2,0,1:T(8,128)(2,1)S(1)} %copy-done.3, s32[1024]{0:T(1024)S(1)} %pad_clamp_fusion), kind=kCustom, calls=%fused_computation.clone | custom fusion | bytes 6291840 | tf_op jit(solution)/shard_map/jit(_take)/gather | solution.py:57
  135.9 0.1 copy.29
  136.1 6.9 %fusion = bf16[1,96,128,128]{3,2,1,0:T(8,128)(2,1)} fusion(pred[96]{0:T(512)(128)(4,1)S(1)} %iota_compare_fusion.1, bf16[96,128,128]{2,1,0:T(8,128)(2,1)} %gather_fusion.1, pred[96]{0:T(512)(128)(4,1)S(1)} %get-tuple-element.15, pred[96]{0:T(512)(128)(4,1)S(1)} %get-tuple-element.14, pred[96]{0:T(512)(128)(4,1)S(1)} %get-tuple-element.13, ...), kind=kOutput, calls=%fused_computation.5 | convolution fusion | flops 413663232 | bytes 9535968 | tf_op jit(solution)/shard_map/tbk,tbn->bkn/dot_general | solution.py:65
  142.9 0.0 all-reduce.2.cloned.1.call-update
  143.0 64.6 %reduce-scatter.2.cloned.1.call-done = f32[128,1024]{1,0:T(8,128)} async-done(((f32[128,8192]{1,0:T(8,128)}), f32[128,1024]{1,0:T(8,128)}) %reduce-scatter.2.cloned.1.call-update) | async-done | bytes 524304 | tf_op jit(solution)/shard_map/reduce_scatter | solution.py:49
  207.5 1.8 convert_element_type.22
  209.3 23.5 %all-reduce.2.cloned.1.call-done = bf16[1,96,128,128]{3,2,1,0:T(8,128)(2,1)} async-done(((bf16[1,96,128,128]{3,2,1,0:T(8,128)(2,1)}), bf16[1,96,128,128]{3,2,1,0:T(8,128)(2,1)}) %all-reduce.2.cloned.1.call-update) | async-done | bytes 3145744 | tf_op jit(solution)/shard_map/psum | solution.py:69
  232.8 4.0 %copy.41 = bf16[1,96,128,128]{3,2,1,0:T(8,128)(2,1)} copy(bf16[1,96,128,128]{3,2,1,0:T(8,128)(2,1)} %all-reduce.2.cloned.1.call-done) | data formatting | bytes 6291456
  (6 shorter events, 0.1 us)
Async XLA Ops:
  7.2 55.6 %all-gather.5.cloned.1.call-start = ((), (), s32[]{:S(2)}) async-start(), calls=%async_computation.2 | async-start | bytes 2359296 | tf_op jit(solution)/shard_map/all_gather | solution.py:23
  9.0 103.6 %all-gather.3.cloned.1.call-start = ((), (), s32[]{:S(2)}) async-start(), calls=%async_computation.1 | async-start | bytes 2359296 | tf_op jit(solution)/shard_map/all_gather | solution.py:24
  10.9 4.7 %copy-start.5 = (s32[1,56]{1,0:T(1,128)S(1)}, s32[1,56]{1,0:T(1,128)}, u32[]{:S(2)}) copy-start(s32[1,56]{1,0:T(1,128)} %param.12) | copy-start | bytes 676
  10.9 4.8 %copy-start.4 = (bf16[1,56,128,128]{3,2,1,0:T(8,128)(2,1)S(1)}, bf16[1,56,128,128]{3,2,1,0:T(8,128)(2,1)}, u32[]{:S(2)}) copy-start(bf16[1,56,128,128]{3,2,1,0:T(8,128)(2,1)} %param.11) | copy-start | bytes 5505028
  10.9 196.6 %reduce-scatter.2.cloned.1.call-start = ((), (), s32[]{:S(2)}) async-start(), calls=%async_computation.3 | async-start | bytes 4718592 | tf_op jit(solution)/shard_map/reduce_scatter | solution.py:49
  112.6 3.1 %copy-start = (bf16[64,128,128]{2,1,0:T(8,128)(2,1)S(1)}, bf16[64,128,128]{2,1,0:T(8,128)(2,1)}, u32[]{:S(2)}) copy-start(bf16[64,128,128]{2,1,0:T(8,128)(2,1)} %copy.26) | copy-start | bytes 6291460
  112.7 3.5 %copy-start.1 = (bf16[128,8192]{0,1:T(8,128)(2,1)S(1)}, bf16[128,8192]{0,1:T(8,128)(2,1)}, u32[]{:S(2)}) copy-start(bf16[128,8192]{0,1:T(8,128)(2,1)} %all-gather.5.cloned.1.call-done) | copy-start | bytes 6291460
  120.4 0.7 copy-start.6
  120.4 112.5 %all-reduce.2.cloned.1.call-start = ((), (), s32[]{:S(2)}) async-start(), calls=%async_computation.4 | async-start | bytes 6291456 | tf_op jit(solution)/shard_map/psum | solution.py:69
  121.4 4.4 %copy-start.2 = (bf16[128,8192]{0,1:T(8,128)(2,1)S(1)}, bf16[128,8192]{0,1:T(8,128)(2,1)}, u32[]{:S(2)}) copy-start(bf16[128,8192]{0,1:T(8,128)(2,1)} %all-gather.5.cloned.1.call-done) | copy-start | bytes 6291460
  128.7 4.5 %copy-start.3 = (bf16[128,64,128]{2,0,1:T(8,128)(2,1)S(1)}, bf16[128,64,128]{2,0,1:T(8,128)(2,1)}, u32[]{:S(2)}) copy-start(bf16[128,64,128]{2,0,1:T(8,128)(2,1)} %copy.30) | copy-start | bytes 6291460
Sparse Core Ops, SparseCore 0:
  10.7 51.9 all-gather.4
  64.8 47.7 all-gather.2
  120.5 86.9 reduce-scatter.1
  209.8 22.9 all-reduce.1
where the time goes:
time: 244 us; the launch traced here: 243 us
  waiting for transfers between devices  171 us (70%)
  local copies, waits for them, and re-layouts  35 us (14%)
  matrix products  18.6 us (8%)
  between operations  15.2 us (6%)
  other arithmetic  3.59 us (1%)
    reduce_scatter x1, waiting for transfers between devices, on_device(): lax.psum_scatter(dx_term, 'tensor', scatter_dimension=1, tiled=True)  64.6 us
    all_gather x1, waiting for transfers between devices, on_device(): lax.all_gather(cotangent, 'tensor', axis=1, tiled=True)  47.6 us
    all_gather x1, waiting for transfers between devices, on_device(): lax.all_gather(tokens, 'tensor', axis=1, tiled=True)  35 us
    psum x1, waiting for transfers between devices, on_device(): summed_grad = lax.psum(local_grad.astype(jnp.bfloat16), 'dp')  23.5 us
    unnamed x17, local copies, waits for them, and re-layouts  7.93 us
    dot_general x1, matrix products, on_device(): jnp.einsum('tbk,tbn->bkn', left_side, right_side, preferred_element_type=...  6.89 us
  transfers between devices with their start and end apart: 4, of which 4 were waited for; matrix products, arithmetic and copies ran while one was open for 18% of the time, Pallas kernels for 0%

commit v1 on v0

--- a/solution.py
+++ b/solution.py
@@ -1,7 +1,15 @@
+import functools
+
 import jax
 import jax.numpy as jnp
 from jax import lax
+from jax.experimental import pallas as pl
+from jax.experimental.pallas import tpu as pltpu
 from jax.sharding import PartitionSpec as P
+
+BF = jnp.bfloat16
+F32 = jnp.float32
+MIB = 1024 * 1024
 
 
 def place_tiles(tile_set, slot_ids, slot_live, block_count):
@@ -14,7 +22,7 @@
     return dense_cols.astype(jnp.bfloat16).reshape(3, block_count * tile_edge, tile_edge)
 
 
-def on_device(tokens, cotangent, fwd_values, fwd_ids, fwd_count, bwd_ids, bwd_count):
+def gather_plan(tokens, cotangent, fwd_values, fwd_ids, fwd_count, bwd_ids, bwd_count):
     values = fwd_values[0]
     slot_ids = fwd_ids[0]
     slot_count = slot_ids.shape[0]
@@ -34,13 +42,7 @@
     gate_pre = jnp.dot(whole_x, dense_cols[0], preferred_element_type=jnp.float32)
     up_val = jnp.dot(whole_x, dense_cols[1], preferred_element_type=jnp.float32)
     dhidden = jnp.dot(whole_dy, dense_cols[2], preferred_element_type=jnp.float32)
-    sigmoid_gate = jax.nn.sigmoid(gate_pre)
-    activated = gate_pre * sigmoid_gate
-    hidden = (activated * up_val).astype(jnp.bfloat16)
-    dgate = (dhidden * up_val * sigmoid_gate * (1.0 + gate_pre * (1.0 - sigmoid_gate))).astype(
-        jnp.bfloat16
-    )
-    up_grad = (dhidden * activated).astype(jnp.bfloat16)
+    hidden, dgate, up_grad = activations(gate_pre, up_val, dhidden)
     contract = (((1,), (1,)), ((), ()))
     dx_term = lax.dot_general(dgate, dense_cols[0], contract, preferred_element_type=jnp.float32)
     dx_term = dx_term + lax.dot_general(
@@ -70,9 +72,236 @@
     return (input_grad, summed_grad[None])
 
 
+def activations(gate, up, dhidden):
+    sig = jax.nn.sigmoid(gate)
+    act = gate * sig
+    hidden = (act * up).astype(BF)
+    dgate = (dhidden * up * sig * (1.0 + gate * (1.0 - sig))).astype(BF)
+    dup = (dhidden * act).astype(BF)
+    return hidden, dgate, dup
+
+
+def place_kernel(ids_ref, cnt_ref, where_ref, val_ref, gu_ref, d_ref, *, blocks, edge):
+    gu_ref[...] = jnp.zeros_like(gu_ref)
+    d_ref[...] = jnp.zeros_like(d_ref)
+
+    def step(s, carry):
+        e = ids_ref[s]
+        kind = e // blocks
+        row = pl.multiple_of(where_ref[e % blocks] * edge, edge)
+        tile = val_ref[s]
+
+        @pl.when(kind == 0)
+        def _():
+            gu_ref[pl.ds(row, edge), 0:edge] = tile
+
+        @pl.when(kind == 1)
+        def _():
+            gu_ref[pl.ds(row, edge), edge : 2 * edge] = tile
+
+        @pl.when(kind == 2)
+        def _():
+            d_ref[pl.ds(row, edge), :] = tile.T
+
+        return carry
+
+    lax.fori_loop(0, cnt_ref[0], step, 0)
+
+
+def place(ids, count, where, values, blocks):
+    edge = values.shape[-1]
+    width = blocks * edge
+    return pl.pallas_call(
+        functools.partial(place_kernel, blocks=blocks, edge=edge),
+        grid_spec=pltpu.PrefetchScalarGridSpec(
+            num_scalar_prefetch=3,
+            grid=(1,),
+            in_specs=[pl.BlockSpec(values.shape, lambda *_: (0, 0, 0))],
+            out_specs=[
+                pl.BlockSpec((width, 2 * edge), lambda *_: (0, 0)),
+                pl.BlockSpec((width, edge), lambda *_: (0, 0)),
+            ],
+        ),
+        out_shape=[
+            jax.ShapeDtypeStruct((width, 2 * edge), BF),
+            jax.ShapeDtypeStruct((width, edge), BF),
+        ],
+        compiler_params=pltpu.CompilerParams(vmem_limit_bytes=24 * MIB),
+        cost_estimate=pl.CostEstimate(flops=0, bytes_accessed=8 * MIB, transcendentals=0),
+        name="place_weights",
+    )(ids, count, where, values)
+
+
+def grads_kernel(slot_ref, shard_ref, *refs, half, blocks, per, edge, rows):
+    mine = refs[: half + 1]
+    sib = (None,) + refs[half + 1 : 2 * half] + (None,)
+    dgu_m, dgu_s, hid_m, hid_s, out_ref = refs[2 * half :]
+    out_ref[...] = jnp.zeros_like(out_ref)
+    hm_t = hid_m[...].T
+    hs_t = hid_s[...].T
+
+    for d in range(half + 1):
+        base = shard_ref[d] * per
+
+        def step(i, carry, d=d, base=base):
+            lane = pl.ds(pl.multiple_of(i * edge, edge), edge)
+            slots = [slot_ref[k * blocks + base + i] for k in range(3)]
+
+            @pl.when((slots[0] >= 0) | (slots[1] >= 0))
+            def _():
+                g = jnp.dot(mine[d][0:rows, lane].T, dgu_m[...], preferred_element_type=F32)
+                g = g.astype(BF)
+                if sib[d] is not None:
+                    g2 = jnp.dot(sib[d][0:rows, lane].T, dgu_s[...], preferred_element_type=F32)
+                    g = (g.astype(F32) + g2.astype(BF).astype(F32)).astype(BF)
+
+                @pl.when(slots[0] >= 0)
+                def _():
+                    out_ref[slots[0]] = g[:, 0:edge]
+
+                @pl.when(slots[1] >= 0)
+                def _():
+                    out_ref[slots[1]] = g[:, edge : 2 * edge]
+
+            @pl.when(slots[2] >= 0)
+            def _():
+                g = jnp.dot(hm_t, mine[d][rows : 2 * rows, lane], preferred_element_type=F32)
+                g = g.astype(BF)
+                if sib[d] is not None:
+                    g2 = jnp.dot(hs_t, sib[d][rows : 2 * rows, lane], preferred_element_type=F32)
+                    g = (g.astype(F32) + g2.astype(BF).astype(F32)).astype(BF)
+                out_ref[slots[2]] = g
+
+            return carry
+
+        lax.fori_loop(0, per, step, 0)
+
+
+def tile_grads(slot_of, shard_of, mine, sib, dgu_m, dgu_s, hid_m, hid_s, slots, blocks):
+    rows, edge = hid_m.shape
+    half = len(mine) - 1
+    arrays = [*mine, *sib, dgu_m, dgu_s, hid_m, hid_s]
+    return pl.pallas_call(
+        functools.partial(
+            grads_kernel,
+            half=half,
+            blocks=blocks,
+            per=mine[0].shape[1] // edge,
+            edge=edge,
+            rows=rows,
+        ),
+        grid_spec=pltpu.PrefetchScalarGridSpec(
+            num_scalar_prefetch=2,
+            grid=(1,),
+            in_specs=[pl.BlockSpec(a.shape, lambda *_: (0, 0)) for a in arrays],
+            out_specs=pl.BlockSpec((slots, edge, edge), lambda *_: (0, 0, 0)),
+        ),
+        out_shape=jax.ShapeDtypeStruct((slots, edge, edge), BF),
+        compiler_params=pltpu.CompilerParams(vmem_limit_bytes=24 * MIB),
+        cost_estimate=pl.CostEstimate(
+            flops=800_000_000, bytes_accessed=8 * MIB, transcendentals=0
+        ),
+        name="tile_gradients",
+    )(slot_of, shard_of, *arrays)
+
+
+def pick(table, index):
+    n = table.shape[0]
+    hit = index[:, None] == jnp.arange(n, dtype=jnp.int32)[None, :]
+    return jnp.sum(jnp.where(hit, table[None, :], 0), axis=1, dtype=jnp.int32)
+
+
+def ring_plan(tokens, cotangent, fwd_values, fwd_ids, fwd_count, bwd_ids, bwd_count, *, n):
+    half = n // 2
+    ring = [2 * i for i in range(half)] + [2 * i + 1 for i in reversed(range(half))]
+    pos = [ring.index(t) for t in range(n)]
+    perm = []
+    for i in range(n):
+        perm.append((ring[i] * 2, ring[(i + 1) % n] * 2))
+        perm.append((ring[i] * 2 + 1, ring[(i - 1) % n] * 2 + 1))
+    hop = lambda v: lax.ppermute(v, ("tensor", "dp"), perm)
+    swap = lambda v: lax.ppermute(v, "dp", [(0, 1), (1, 0)])
+
+    values = fwd_values[0]
+    edge = values.shape[-1]
+    rows, width = tokens.shape
+    per = width // edge
+    blocks = n * per
+    slots = bwd_ids.shape[1]
+
+    core = lax.axis_index("dp")
+    sign = 1 - 2 * core
+    here = pick(jnp.array(pos, jnp.int32), lax.axis_index("tensor")[None])[0]
+    steps = jnp.arange(n, dtype=jnp.int32)
+    shard_of = pick(jnp.array(ring, jnp.int32), (here - sign * steps) % n)
+    dist_of = ((here - jnp.array(pos, jnp.int32)) * sign) % n
+    where = (dist_of[:, None] * per + jnp.arange(per, dtype=jnp.int32)[None, :]).reshape(blocks)
+    slot_iota = jnp.arange(slots, dtype=jnp.int32)
+    hit = (bwd_ids[0][None, :] == jnp.arange(3 * blocks, dtype=jnp.int32)[:, None]) & (
+        slot_iota < bwd_count[0]
+    )[None, :]
+    slot_of = jnp.max(jnp.where(hit, slot_iota[None, :], -1), axis=1)
+
+    own = jnp.concatenate([tokens, cotangent], axis=0)
+    mine = [own]
+    sib = [swap(own)]
+    for k in range(1, half + 1):
+        mine.append(hop(mine[-1]))
+        if k < half:
+            sib.append(hop(sib[-1]))
+
+    w_gu, w_d = place(fwd_ids[0], fwd_count, where, values, blocks)
+    gu_at = lambda d: w_gu[d * width : (d + 1) * width]
+    d_at = lambda d: w_d[d * width : (d + 1) * width]
+    dot = functools.partial(jnp.dot, preferred_element_type=F32)
+
+    gu_m = dot(mine[0][:rows], gu_at(0))
+    dh_m = dot(mine[0][rows:], d_at(0))
+    gu_s = dh_s = None
+    for d in range(1, half + 1):
+        gu_m = gu_m + dot(mine[d][:rows], gu_at(d))
+        dh_m = dh_m + dot(mine[d][rows:], d_at(d))
+        if d < half:
+            part = dot(sib[d][:rows], gu_at(d))
+            gu_s = part if gu_s is None else gu_s + part
+            part = dot(sib[d][rows:], d_at(d))
+            dh_s = part if dh_s is None else dh_s + part
+    gu_tm, gu_ts = gu_m + swap(gu_s), gu_s + swap(gu_m)
+    dh_tm, dh_ts = dh_m + swap(dh_s), dh_s + swap(dh_m)
+
+    hid_m, dg_m, du_m = activations(gu_tm[:, :edge], gu_tm[:, edge:], dh_tm)
+    hid_s, dg_s, du_s = activations(gu_ts[:, :edge], gu_ts[:, edge:], dh_ts)
+    dgu_m = jnp.concatenate([dg_m, du_m], axis=1)
+    dgu_s = jnp.concatenate([dg_s, du_s], axis=1)
+
+    term = lambda dgu, d: lax.dot_general(
+        dgu, gu_at(d), (((1,), (1,)), ((), ())), preferred_element_type=F32
+    )
+    run_m = hop(term(dgu_m, half).astype(BF))
+    run_s = None
+    for d in range(half + 1, n):
+        part = term(dgu_s, d)
+        run_s = hop((part if run_s is None else part + run_s.astype(F32)).astype(BF))
+        run_m = hop((term(dgu_m, d) + run_m.astype(F32)).astype(BF))
+    dx = term(dgu_m, 0) + run_m.astype(F32) + swap(run_s).astype(F32)
+
+    grads = tile_grads(
+        slot_of, shard_of, mine, sib[1:], dgu_m, dgu_s, hid_m, hid_s, slots, blocks
+    )
+    grads = grads + swap(grads)
+    return dx.astype(BF), grads[None]
+
+
+def on_device(tokens, cotangent, fwd_values, *rest, n, cores):
+    width, edge = tokens.shape[1], fwd_values.shape[-1]
+    if cores == 2 and n % 2 == 0 and 4 <= n <= 16 and width % edge == 0:
+        return ring_plan(tokens, cotangent, fwd_values, *rest, n=n)
+    return gather_plan(tokens, cotangent, fwd_values, *rest)
+
+
 def solution(mesh):
     return jax.shard_map(
-        on_device,
+        functools.partial(on_device, n=mesh.shape["tensor"], cores=mesh.shape["dp"]),
         mesh=mesh,
         in_specs=(
             P(("groups", "dp"), "tensor"),

time: 244 us -> 103 us (0.42)
  waiting for transfers between devices: 171 us -> 40 us
  local copies, waits for them, and re-layouts: 35 us -> 4.19 us
  starting transfers between devices: 0.16 us -> 27.5 us
  Pallas kernels: 0 us -> 13.9 us
  between operations: 15.2 us -> 2.26 us
  matrix products: 18.6 us -> 7.95 us
  other arithmetic: 3.59 us -> 7.25 us
    all_gather x2 -> x0, waiting for transfers between devices: 82.6 us -> none  [the longest x1 47.6 us: on_device(): lax.all_gather(cotangent, 'tensor', axis=1, tiled=True)]
    reduce_scatter x1 -> x0, waiting for transfers between devices: 64.6 us -> none  [on_device(): lax.psum_scatter(dx_term, 'tensor', scatter_dimension=1, tiled=True)]
    ppermute x0 -> x21, waiting for transfers between devices: none -> 40 us  [the longest x14 39.2 us: ring_plan(): hop = lambda v: lax.ppermute(v, ('tensor', 'dp'), perm)]
    ppermute x0 -> x21, starting transfers between devices: none -> 27.5 us  [the longest x14 25.6 us: ring_plan(): hop = lambda v: lax.ppermute(v, ('tensor', 'dp'), perm)]
    psum x1 -> x0, waiting for transfers between devices: 23.5 us -> none  [on_device(): summed_grad = lax.psum(local_grad.astype(jnp.bfloat16), 'dp')]
    pallas_call x0 -> x2, Pallas kernels: none -> 13.9 us  [the longest x1 9.95 us: tile_grads(): pl.pallas_call(functools.partial(grads_kernel, half=half, blocks=blocks,...]
    dot_general x7 -> x24, matrix products: 18.6 us -> 7.95 us  [the longest x8 2.44 us: ring_plan(): lax.dot_general(dgu, gu_at(d), (((1,), (1,)), ((), ())), preferred_elemen...]
    slice x4 -> x0, local copies, waits for them, and re-layouts: 8.22 us -> none  [the longest x2 4.19 us: on_device(): up_val = jnp.dot(whole_x, dense_cols[1], preferred_element_type=jnp.float32)]
  transfers between devices with their start and end apart: 4 -> 21, of which waited for: 4 -> 12; matrix products, arithmetic and copies ran while one was open for 18% -> 13% of each run, Pallas kernels for 0% -> 4%
where the time goes in v1:
time: 103 us
  waiting for transfers between devices  40 us (39%)
  starting transfers between devices  27.5 us (27%)
  Pallas kernels  13.9 us (13%)
  matrix products  7.95 us (8%)
  other arithmetic  7.25 us (7%)
  local copies, waits for them, and re-layouts  4.19 us (4%)
  between operations  2.26 us (2%)
    ppermute x14, waiting for transfers between devices, ring_plan(): hop = lambda v: lax.ppermute(v, ('tensor', 'dp'), perm)  39.2 us
    ppermute x14, starting transfers between devices, ring_plan(): hop = lambda v: lax.ppermute(v, ('tensor', 'dp'), perm)  25.6 us
    pallas_call x1, Pallas kernels, tile_grads(): pl.pallas_call(functools.partial(grads_kernel, half=half, blocks=blocks,...  9.95 us
    pallas_call x1, Pallas kernels, place(): pl.pallas_call(functools.partial(place_kernel, blocks=blocks, edge=edge),...  4 us
    unnamed x7, local copies, waits for them, and re-layouts  3.14 us
    dot_general x8, matrix products, ring_plan(): lax.dot_general(dgu, gu_at(d), (((1,), (1,)), ((), ())), preferred_elemen...  2.44 us
  transfers between devices with their start and end apart: 21, of which 12 were waited for; matrix products, arithmetic and copies ran while one was open for 13% of the time, Pallas kernels for 4%

profile of v1, /device:TPU:0, one launch (start us, length us, event | category | flops | bytes accessed | tf_op | source)
XLA Modules:
  0.0 103.0 jit_solution(12941208341704345543)
XLA Ops:
  0.6 1.0 constant_dynamic-update-slice_fusion.1
  1.6 1.0 constant_dynamic-update-slice_fusion.refs_0_
  2.6 0.5 collective-permute-start.4
  3.1 2.6 %collective-permute-start = (bf16[256,1024]{1,0:T(8,128)(2,1)S(1)}, bf16[256,1024]{1,0:T(8,128)(2,1)S(1)}, u32[]{:S(2)}, u32[]{:S(2)}) collective-permute-start(bf16[256,1024]{1,0:T(8,128)(2,1)S(1)} %constant_dynamic-update-slice_fusion.refs_0_), channel_id=1, source_target_pairs={{0,4},{1,3},{4,8},{5,1},{8,12},{9,5},{12,14},{13,9},{14,10},{15,13... | collective-permute-start | bytes 1572872 | tf_op jit(solution)/shard_map/ppermute | solution.py:222
  6.4 1.3 %fusion.53 = s32[]{:T(128)} fusion(s32[8]{0:T(128)} %constant.44.clone, s32[]{:T(128)S(6)} %axis_index.23), kind=kLoop, calls=%fused_computation.96 | loop fusion | flops 23 | bytes 40 | tf_op jit(solution)/shard_map/reduce_sum | solution.py:211
  7.7 1.3 %fusion.54 = s32[8]{0:T(128)S(1)} fusion(s32[8]{0:T(128)} %constant.51, s32[]{:T(128)S(6)} %sub.25, s32[]{:T(128)} %fusion.53), kind=kLoop, calls=%fused_computation.97 | loop fusion | flops 112 | bytes 72 | tf_op jit(solution)/shard_map/mul | solution.py:238
  9.2 1.5 %copy-done = bf16[1,56,128,128]{3,2,1,0:T(8,128)(2,1)S(1)} copy-done((bf16[1,56,128,128]{3,2,1,0:T(8,128)(2,1)S(1)}, bf16[1,56,128,128]{3,2,1,0:T(8,128)(2,1)}, u32[]{:S(2)}) %copy-start) | copy-done | bytes 1835032
  10.7 0.7 copy-done.1
  11.3 4.0 %place_weights.1 = (bf16[8192,256]{1,0:T(8,128)(2,1)S(1)}, bf16[8192,128]{1,0:T(8,128)(2,1)S(1)}) custom-call(s32[56]{0:T(128)S(1)} %bitcast.14, s32[1]{0:T(128)S(6)} %copy.40.cnt_ref, s32[64]{0:T(128)S(1)} %add.121.where_ref, bf16[56,128,128]{2,1,0:T(8,128)(2,1)S(1)} %bitcast.13), custom_call_target="tpu_custom_call" | custom-call | bytes 8388608 | tf_op jit(solution)/shard_map/place_weights/pallas_call | solution.py:114
  15.3 1.2 %convolution_bitcast_fusion.1 = f32[128,128]{1,0:T(8,128)S(1)} fusion(bf16[128,1024]{1,0:T(8,128)(2,1)} %param.11, bf16[8192,128]{1,0:T(8,128)(2,1)S(1)} %get-tuple-element.4), kind=kOutput, calls=%fused_computation.10 | convolution fusion | flops 33554432 | bytes 589824 | tf_op jit(solution)/shard_map/dot_general | solution.py:259
  16.5 0.7 and_select_fusion
  17.8 0.8 select_reduce_fusion.slot_ref
  18.6 1.2 %convolution_bitcast_fusion = f32[128,256]{1,0:T(8,128)S(1)} fusion(bf16[128,1024]{1,0:T(8,128)(2,1)} %param.10, bf16[8192,256]{1,0:T(8,128)(2,1)S(1)} %get-tuple-element.5), kind=kOutput, calls=%fused_computation.3 | convolution fusion | flops 67108864 | bytes 917504 | tf_op jit(solution)/shard_map/dot_general | solution.py:258
  19.8 1.2 %collective-permute-start.5 = (bf16[256,1024]{1,0:T(8,128)(2,1)S(1)}, bf16[256,1024]{1,0:T(8,128)(2,1)S(1)}, u32[]{:S(2)}, u32[]{:S(2)}) collective-permute-start(bf16[256,1024]{1,0:T(8,128)(2,1)S(1)} %collective-permute-done.4), channel_id=1, source_target_pairs={{0,4},{1,3},{4,8},{5,1},{8,12},{9,5},{12,14},{13,9},{14,10},{15,13... | collective-permute-start | bytes 1572872 | tf_op jit(solution)/shard_map/ppermute | solution.py:222
  21.2 1.3 %collective-permute-start.1 = (bf16[256,1024]{1,0:T(8,128)(2,1)S(1)}, bf16[256,1024]{1,0:T(8,128)(2,1)S(1)}, u32[]{:S(2)}, u32[]{:S(2)}) collective-permute-start(bf16[256,1024]{1,0:T(8,128)(2,1)S(1)} %collective-permute-done.refs_1_), channel_id=1, source_target_pairs={{0,4},{1,3},{4,8},{5,1},{8,12},{9,5},{12,14},{13,9},{14,10},{15,13... | collective-permute-start | bytes 1572872 | tf_op jit(solution)/shard_map/ppermute | solution.py:222
  22.5 0.2 convolution_add_fusion.11
  22.7 0.2 convolution_add_fusion.5
  22.9 6.1 %collective-permute-done.5.refs_5_ = bf16[256,1024]{1,0:T(8,128)(2,1)S(1)} collective-permute-done((bf16[256,1024]{1,0:T(8,128)(2,1)S(1)}, bf16[256,1024]{1,0:T(8,128)(2,1)S(1)}, u32[]{:S(2)}, u32[]{:S(2)}) %collective-permute-start.5) | collective-permute-done | bytes 524320 | tf_op jit(solution)/shard_map/ppermute | solution.py:222
  29.1 1.1 %collective-permute-start.6 = (bf16[256,1024]{1,0:T(8,128)(2,1)S(1)}, bf16[256,1024]{1,0:T(8,128)(2,1)S(1)}, u32[]{:S(2)}, u32[]{:S(2)}) collective-permute-start(bf16[256,1024]{1,0:T(8,128)(2,1)S(1)} %collective-permute-done.5.refs_5_), channel_id=1, source_target_pairs={{0,4},{1,3},{4,8},{5,1},{8,12},{9,5},{12,14},{13,9},{14,10},{15,13... | collective-permute-start | bytes 1572872 | tf_op jit(solution)/shard_map/ppermute | solution.py:222
  30.2 0.2 fusion.21
  30.4 4.2 %collective-permute-done.1.refs_2_ = bf16[256,1024]{1,0:T(8,128)(2,1)S(1)} collective-permute-done((bf16[256,1024]{1,0:T(8,128)(2,1)S(1)}, bf16[256,1024]{1,0:T(8,128)(2,1)S(1)}, u32[]{:S(2)}, u32[]{:S(2)}) %collective-permute-start.1) | collective-permute-done | bytes 524320 | tf_op jit(solution)/shard_map/ppermute | solution.py:222
  34.7 1.1 %collective-permute-start.2 = (bf16[256,1024]{1,0:T(8,128)(2,1)S(1)}, bf16[256,1024]{1,0:T(8,128)(2,1)S(1)}, u32[]{:S(2)}, u32[]{:S(2)}) collective-permute-start(bf16[256,1024]{1,0:T(8,128)(2,1)S(1)} %collective-permute-done.1.refs_2_), channel_id=1, source_target_pairs={{0,4},{1,3},{4,8},{5,1},{8,12},{9,5},{12,14},{13,9},{14,10},{15,13... | collective-permute-start | bytes 1572872 | tf_op jit(solution)/shard_map/ppermute | solution.py:222
  35.8 0.2 convolution_add_fusion.10
  36.0 0.2 fusion.36
  36.2 0.2 convolution_add_fusion.4
  36.5 3.8 %collective-permute-done.6.refs_6_ = bf16[256,1024]{1,0:T(8,128)(2,1)S(1)} collective-permute-done((bf16[256,1024]{1,0:T(8,128)(2,1)S(1)}, bf16[256,1024]{1,0:T(8,128)(2,1)S(1)}, u32[]{:S(2)}, u32[]{:S(2)}) %collective-permute-start.6) | collective-permute-done | bytes 524320 | tf_op jit(solution)/shard_map/ppermute | solution.py:222
  40.3 1.1 %collective-permute-start.7 = (bf16[256,1024]{1,0:T(8,128)(2,1)S(1)}, bf16[256,1024]{1,0:T(8,128)(2,1)S(1)}, u32[]{:S(2)}, u32[]{:S(2)}) collective-permute-start(bf16[256,1024]{1,0:T(8,128)(2,1)S(1)} %collective-permute-done.6.refs_6_), channel_id=1, source_target_pairs={{0,4},{1,3},{4,8},{5,1},{8,12},{9,5},{12,14},{13,9},{14,10},{15,13... | collective-permute-start | bytes 1572872 | tf_op jit(solution)/shard_map/ppermute | solution.py:222
  41.4 0.2 convolution_add_fusion.1
  41.7 4.2 %collective-permute-done.2.refs_3_ = bf16[256,1024]{1,0:T(8,128)(2,1)S(1)} collective-permute-done((bf16[256,1024]{1,0:T(8,128)(2,1)S(1)}, bf16[256,1024]{1,0:T(8,128)(2,1)S(1)}, u32[]{:S(2)}, u32[]{:S(2)}) %collective-permute-start.2) | collective-permute-done | bytes 524320 | tf_op jit(solution)/shard_map/ppermute | solution.py:222
  45.9 1.1 %collective-permute-start.3 = (bf16[256,1024]{1,0:T(8,128)(2,1)S(1)}, bf16[256,1024]{1,0:T(8,128)(2,1)S(1)}, u32[]{:S(2)}, u32[]{:S(2)}) collective-permute-start(bf16[256,1024]{1,0:T(8,128)(2,1)S(1)} %collective-permute-done.2.refs_3_), channel_id=1, source_target_pairs={{0,4},{1,3},{4,8},{5,1},{8,12},{9,5},{12,14},{13,9},{14,10},{15,13... | collective-permute-start | bytes 1572872 | tf_op jit(solution)/shard_map/ppermute | solution.py:222
  47.0 0.2 convolution_add_fusion.7
  47.3 0.2 convolution_add_fusion.9
  47.5 0.2 convolution_add_fusion.3
  47.7 9.4 %collective-permute-done.3.refs_4_ = bf16[256,1024]{1,0:T(8,128)(2,1)S(1)} collective-permute-done((bf16[256,1024]{1,0:T(8,128)(2,1)S(1)}, bf16[256,1024]{1,0:T(8,128)(2,1)S(1)}, u32[]{:S(2)}, u32[]{:S(2)}) %collective-permute-start.3) | collective-permute-done | bytes 524320 | tf_op jit(solution)/shard_map/ppermute | solution.py:222
  57.1 0.2 convolution_add_fusion.2
  57.5 0.2 convolution_add_fusion
  57.7 0.6 collective-permute-start.9
  58.3 0.2 convolution_add_fusion.6
  58.8 0.6 collective-permute-start.14
  59.4 0.4 collective-permute-done.8
  59.9 0.4 collective-permute-done.14
  60.3 9.9 %tile_gradients.1 = bf16[96,128,128]{2,1,0:T(8,128)(2,1)S(1)} custom-call(s32[192]{0:T(256)S(1)} %select_reduce_fusion.slot_ref, s32[8]{0:T(128)S(1)} %select_reduce_fusion.1.shard_ref, bf16[256,1024]{1,0:T(8,128)(2,1)S(1)} %constant_dynamic-update-slice_fusion.refs_0_, bf16[256,1024]{1,0:T(8,128)(2,1)S(1)} %collective-permute-done.refs_1_, ...), custom_call_target="tpu_custom_call" | custom-call | flops 800000000 | bytes 8388608 | tf_op jit(solution)/shard_map/tile_gradients/pallas_call | solution.py:184
  70.4 0.3 convolution_convert_fusion
  70.7 2.6 %collective-permute-start.16 = (bf16[128,1024]{1,0:T(8,128)(2,1)S(1)}, bf16[128,1024]{1,0:T(8,128)(2,1)S(1)}, u32[]{:S(2)}, u32[]{:S(2)}) collective-permute-start(bf16[128,1024]{1,0:T(8,128)(2,1)S(1)} %convolution_convert_fusion), channel_id=1, source_target_pairs={{0,4},{1,3},{4,8},{5,1},{8,12},{9,5},{12,14},{13,9},{14,10},{15,13... | collective-permute-start | bytes 786440 | tf_op jit(solution)/shard_map/ppermute | solution.py:222
  73.3 0.3 convolution_convert_fusion.1
  73.6 0.8 collective-permute-start.10
  74.4 2.8 %collective-permute-done.16 = bf16[128,1024]{1,0:T(8,128)(2,1)S(1)} collective-permute-done((bf16[128,1024]{1,0:T(8,128)(2,1)S(1)}, bf16[128,1024]{1,0:T(8,128)(2,1)S(1)}, u32[]{:S(2)}, u32[]{:S(2)}) %collective-permute-start.16) | collective-permute-done | bytes 262176 | tf_op jit(solution)/shard_map/ppermute | solution.py:222
  77.2 0.3 add_convert_fusion.2
  77.5 2.5 %collective-permute-start.17 = (bf16[128,1024]{1,0:T(8,128)(2,1)S(1)}, bf16[128,1024]{1,0:T(8,128)(2,1)S(1)}, u32[]{:S(2)}, u32[]{:S(2)}) collective-permute-start(bf16[128,1024]{1,0:T(8,128)(2,1)S(1)} %add_convert_fusion.2), channel_id=1, source_target_pairs={{0,4},{1,3},{4,8},{5,1},{8,12},{9,5},{12,14},{13,9},{14,10},{15,13... | collective-permute-start | bytes 786440 | tf_op jit(solution)/shard_map/ppermute | solution.py:222
  80.0 0.3 add_convert_fusion.5
  80.3 2.5 %collective-permute-start.11 = (bf16[128,1024]{1,0:T(8,128)(2,1)S(1)}, bf16[128,1024]{1,0:T(8,128)(2,1)S(1)}, u32[]{:S(2)}, u32[]{:S(2)}) collective-permute-start(bf16[128,1024]{1,0:T(8,128)(2,1)S(1)} %add_convert_fusion.5), channel_id=1, source_target_pairs={{0,4},{1,3},{4,8},{5,1},{8,12},{9,5},{12,14},{13,9},{14,10},{15,13... | collective-permute-start | bytes 786440 | tf_op jit(solution)/shard_map/ppermute | solution.py:222
  82.8 1.1 %collective-permute-done.17 = bf16[128,1024]{1,0:T(8,128)(2,1)S(1)} collective-permute-done((bf16[128,1024]{1,0:T(8,128)(2,1)S(1)}, bf16[128,1024]{1,0:T(8,128)(2,1)S(1)}, u32[]{:S(2)}, u32[]{:S(2)}) %collective-permute-start.17) | collective-permute-done | bytes 262176 | tf_op jit(solution)/shard_map/ppermute | solution.py:222
  83.9 0.3 add_convert_fusion.1
  84.2 2.5 %collective-permute-start.18 = (bf16[128,1024]{1,0:T(8,128)(2,1)S(1)}, bf16[128,1024]{1,0:T(8,128)(2,1)S(1)}, u32[]{:S(2)}, u32[]{:S(2)}) collective-permute-start(bf16[128,1024]{1,0:T(8,128)(2,1)S(1)} %add_convert_fusion.1), channel_id=1, source_target_pairs={{0,4},{1,3},{4,8},{5,1},{8,12},{9,5},{12,14},{13,9},{14,10},{15,13... | collective-permute-start | bytes 786440 | tf_op jit(solution)/shard_map/ppermute | solution.py:222
  86.7 0.3 add_convert_fusion.4
  87.1 2.5 %collective-permute-start.12 = (bf16[128,1024]{1,0:T(8,128)(2,1)S(1)}, bf16[128,1024]{1,0:T(8,128)(2,1)S(1)}, u32[]{:S(2)}, u32[]{:S(2)}) collective-permute-start(bf16[128,1024]{1,0:T(8,128)(2,1)S(1)} %add_convert_fusion.4), channel_id=1, source_target_pairs={{0,4},{1,3},{4,8},{5,1},{8,12},{9,5},{12,14},{13,9},{14,10},{15,13... | collective-permute-start | bytes 786440 | tf_op jit(solution)/shard_map/ppermute | solution.py:222
  89.5 1.1 %collective-permute-done.18 = bf16[128,1024]{1,0:T(8,128)(2,1)S(1)} collective-permute-done((bf16[128,1024]{1,0:T(8,128)(2,1)S(1)}, bf16[128,1024]{1,0:T(8,128)(2,1)S(1)}, u32[]{:S(2)}, u32[]{:S(2)}) %collective-permute-start.18) | collective-permute-done | bytes 262176 | tf_op jit(solution)/shard_map/ppermute | solution.py:222
  90.6 2.8 %collective-permute-done.12 = bf16[128,1024]{1,0:T(8,128)(2,1)S(1)} collective-permute-done((bf16[128,1024]{1,0:T(8,128)(2,1)S(1)}, bf16[128,1024]{1,0:T(8,128)(2,1)S(1)}, u32[]{:S(2)}, u32[]{:S(2)}) %collective-permute-start.12) | collective-permute-done | bytes 262176 | tf_op jit(solution)/shard_map/ppermute | solution.py:222
  93.5 0.3 add_convert_fusion.3
  93.8 2.5 %collective-permute-start.13 = (bf16[128,1024]{1,0:T(8,128)(2,1)S(1)}, bf16[128,1024]{1,0:T(8,128)(2,1)S(1)}, u32[]{:S(2)}, u32[]{:S(2)}) collective-permute-start(bf16[128,1024]{1,0:T(8,128)(2,1)S(1)} %add_convert_fusion.3), channel_id=1, source_target_pairs={{0,4},{1,3},{4,8},{5,1},{8,12},{9,5},{12,14},{13,9},{14,10},{15,13... | collective-permute-start | bytes 786440 | tf_op jit(solution)/shard_map/ppermute | solution.py:222
  96.3 0.3 fusion.24
  96.6 3.6 %collective-permute-done.13 = bf16[128,1024]{1,0:T(8,128)(2,1)S(1)} collective-permute-done((bf16[128,1024]{1,0:T(8,128)(2,1)S(1)}, bf16[128,1024]{1,0:T(8,128)(2,1)S(1)}, u32[]{:S(2)}, u32[]{:S(2)}) %collective-permute-start.13) | collective-permute-done | bytes 262176 | tf_op jit(solution)/shard_map/ppermute | solution.py:222
  100.2 0.8 add_convert_fusion
  101.0 2.0 %add_bitcast_fusion = bf16[1,96,128,128]{3,2,1,0:T(8,128)(2,1)} fusion(bf16[96,128,128]{2,1,0:T(8,128)(2,1)S(1)} %tile_gradients.1, bf16[96,128,128]{2,1,0:T(8,128)(2,1)S(1)} %collective-permute-done.20), kind=kLoop, calls=%fused_computation | loop fusion | flops 1572864 | bytes 9437184 | tf_op jit(solution)/shard_map/broadcast_in_dim | solution.py:292
  (28 shorter events, 1.0 us)
Async XLA Ops:
  0.6 20.4 %copy-start.2 = (s32[8]{0:T(128)S(1)}, s32[8]{0:T(128)}, u32[]{:S(2)}) copy-start(s32[8]{0:T(128)} %constant.45.clone) | copy-start | bytes 100
  2.6 17.2 %collective-permute-start.4 = (bf16[256,1024]{1,0:T(8,128)(2,1)S(1)}, bf16[256,1024]{1,0:T(8,128)(2,1)S(1)}, u32[]{:S(2)}, u32[]{:S(2)}) collective-permute-start(bf16[256,1024]{1,0:T(8,128)(2,1)S(1)} %constant_dynamic-update-slice_fusion.refs_0_), channel_id=1, source_target_pairs={{0,1},{1,0},{2,3},{3,2},{4,5},{5,4},{6,7},{7,6},{8,9},{9,8},{10,11... | collective-permute-start | bytes 1572872 | tf_op jit(solution)/shard_map/ppermute | solution.py:223
  3.1 18.1 %collective-permute-start = (bf16[256,1024]{1,0:T(8,128)(2,1)S(1)}, bf16[256,1024]{1,0:T(8,128)(2,1)S(1)}, u32[]{:S(2)}, u32[]{:S(2)}) collective-permute-start(bf16[256,1024]{1,0:T(8,128)(2,1)S(1)} %constant_dynamic-update-slice_fusion.refs_0_), channel_id=1, source_target_pairs={{0,4},{1,3},{4,8},{5,1},{8,12},{9,5},{12,14},{13,9},{14,10},{15,13... | collective-permute-start | bytes 1572872 | tf_op jit(solution)/shard_map/ppermute | solution.py:222
  9.2 1.5 %copy-start = (bf16[1,56,128,128]{3,2,1,0:T(8,128)(2,1)S(1)}, bf16[1,56,128,128]{3,2,1,0:T(8,128)(2,1)}, u32[]{:S(2)}) copy-start(bf16[1,56,128,128]{3,2,1,0:T(8,128)(2,1)} %param.12) | copy-start | bytes 5505028
  10.7 0.7 copy-start.1
  19.8 9.2 %collective-permute-start.5 = (bf16[256,1024]{1,0:T(8,128)(2,1)S(1)}, bf16[256,1024]{1,0:T(8,128)(2,1)S(1)}, u32[]{:S(2)}, u32[]{:S(2)}) collective-permute-start(bf16[256,1024]{1,0:T(8,128)(2,1)S(1)} %collective-permute-done.4), channel_id=1, source_target_pairs={{0,4},{1,3},{4,8},{5,1},{8,12},{9,5},{12,14},{13,9},{14,10},{15,13... | collective-permute-start | bytes 1572872 | tf_op jit(solution)/shard_map/ppermute | solution.py:222
  21.2 13.5 %collective-permute-start.1 = (bf16[256,1024]{1,0:T(8,128)(2,1)S(1)}, bf16[256,1024]{1,0:T(8,128)(2,1)S(1)}, u32[]{:S(2)}, u32[]{:S(2)}) collective-permute-start(bf16[256,1024]{1,0:T(8,128)(2,1)S(1)} %collective-permute-done.refs_1_), channel_id=1, source_target_pairs={{0,4},{1,3},{4,8},{5,1},{8,12},{9,5},{12,14},{13,9},{14,10},{15,13... | collective-permute-start | bytes 1572872 | tf_op jit(solution)/shard_map/ppermute | solution.py:222
  29.1 11.2 %collective-permute-start.6 = (bf16[256,1024]{1,0:T(8,128)(2,1)S(1)}, bf16[256,1024]{1,0:T(8,128)(2,1)S(1)}, u32[]{:S(2)}, u32[]{:S(2)}) collective-permute-start(bf16[256,1024]{1,0:T(8,128)(2,1)S(1)} %collective-permute-done.5.refs_5_), channel_id=1, source_target_pairs={{0,4},{1,3},{4,8},{5,1},{8,12},{9,5},{12,14},{13,9},{14,10},{15,13... | collective-permute-start | bytes 1572872 | tf_op jit(solution)/shard_map/ppermute | solution.py:222
  34.7 11.2 %collective-permute-start.2 = (bf16[256,1024]{1,0:T(8,128)(2,1)S(1)}, bf16[256,1024]{1,0:T(8,128)(2,1)S(1)}, u32[]{:S(2)}, u32[]{:S(2)}) collective-permute-start(bf16[256,1024]{1,0:T(8,128)(2,1)S(1)} %collective-permute-done.1.refs_2_), channel_id=1, source_target_pairs={{0,4},{1,3},{4,8},{5,1},{8,12},{9,5},{12,14},{13,9},{14,10},{15,13... | collective-permute-start | bytes 1572872 | tf_op jit(solution)/shard_map/ppermute | solution.py:222
  40.3 17.2 %collective-permute-start.7 = (bf16[256,1024]{1,0:T(8,128)(2,1)S(1)}, bf16[256,1024]{1,0:T(8,128)(2,1)S(1)}, u32[]{:S(2)}, u32[]{:S(2)}) collective-permute-start(bf16[256,1024]{1,0:T(8,128)(2,1)S(1)} %collective-permute-done.6.refs_6_), channel_id=1, source_target_pairs={{0,4},{1,3},{4,8},{5,1},{8,12},{9,5},{12,14},{13,9},{14,10},{15,13... | collective-permute-start | bytes 1572872 | tf_op jit(solution)/shard_map/ppermute | solution.py:222
  45.9 11.2 %collective-permute-start.3 = (bf16[256,1024]{1,0:T(8,128)(2,1)S(1)}, bf16[256,1024]{1,0:T(8,128)(2,1)S(1)}, u32[]{:S(2)}, u32[]{:S(2)}) collective-permute-start(bf16[256,1024]{1,0:T(8,128)(2,1)S(1)} %collective-permute-done.2.refs_3_), channel_id=1, source_target_pairs={{0,4},{1,3},{4,8},{5,1},{8,12},{9,5},{12,14},{13,9},{14,10},{15,13... | collective-permute-start | bytes 1572872 | tf_op jit(solution)/shard_map/ppermute | solution.py:222
  57.4 2.0 %collective-permute-start.15 = (f32[128,256]{1,0:T(8,128)S(1)}, f32[128,256]{1,0:T(8,128)S(1)}, u32[]{:S(2)}, u32[]{:S(2)}) collective-permute-start(f32[128,256]{1,0:T(8,128)S(1)} %convolution_add_fusion.2), channel_id=1, source_target_pairs={{0,1},{1,0},{2,3},{3,2},{4,5},{5,4},{6,7},{7,6},{8,9},{9,8},{10,11... | collective-permute-start | bytes 393224 | tf_op jit(solution)/shard_map/ppermute | solution.py:223
  57.7 1.7 %collective-permute-start.9 = (f32[128,256]{1,0:T(8,128)S(1)}, f32[128,256]{1,0:T(8,128)S(1)}, u32[]{:S(2)}, u32[]{:S(2)}) collective-permute-start(f32[128,256]{1,0:T(8,128)S(1)} %convolution_add_fusion), channel_id=1, source_target_pairs={{0,1},{1,0},{2,3},{3,2},{4,5},{5,4},{6,7},{7,6},{8,9},{9,8},{10,11... | collective-permute-start | bytes 393224 | tf_op jit(solution)/shard_map/ppermute | solution.py:223
  58.5 1.3 %collective-permute-start.8 = (f32[128,128]{1,0:T(8,128)S(1)}, f32[128,128]{1,0:T(8,128)S(1)}, u32[]{:S(2)}, u32[]{:S(2)}) collective-permute-start(f32[128,128]{1,0:T(8,128)S(1)} %convolution_add_fusion.6), channel_id=1, source_target_pairs={{0,1},{1,0},{2,3},{3,2},{4,5},{5,4},{6,7},{7,6},{8,9},{9,8},{10,11... | collective-permute-start | bytes 196616 | tf_op jit(solution)/shard_map/ppermute | solution.py:223
  58.8 1.5 %collective-permute-start.14 = (f32[128,128]{1,0:T(8,128)S(1)}, f32[128,128]{1,0:T(8,128)S(1)}, u32[]{:S(2)}, u32[]{:S(2)}) collective-permute-start(f32[128,128]{1,0:T(8,128)S(1)} %convolution_add_fusion.8), channel_id=1, source_target_pairs={{0,1},{1,0},{2,3},{3,2},{4,5},{5,4},{6,7},{7,6},{8,9},{9,8},{10,11... | collective-permute-start | bytes 196616 | tf_op jit(solution)/shard_map/ppermute | solution.py:223
  70.3 30.7 %collective-permute-start.20 = (bf16[96,128,128]{2,1,0:T(8,128)(2,1)S(1)}, bf16[96,128,128]{2,1,0:T(8,128)(2,1)S(1)}, u32[]{:S(2)}, u32[]{:S(2)}) collective-permute-start(bf16[96,128,128]{2,1,0:T(8,128)(2,1)S(1)} %tile_gradients.1), channel_id=1, source_target_pairs={{0,1},{1,0},{2,3},{3,2},{4,5},{5,4},{6,7},{7,6},{8,9},{9,8},{10,11... | collective-permute-start | bytes 9437192 | tf_op jit(solution)/shard_map/ppermute | solution.py:223
  70.7 6.5 %collective-permute-start.16 = (bf16[128,1024]{1,0:T(8,128)(2,1)S(1)}, bf16[128,1024]{1,0:T(8,128)(2,1)S(1)}, u32[]{:S(2)}, u32[]{:S(2)}) collective-permute-start(bf16[128,1024]{1,0:T(8,128)(2,1)S(1)} %convolution_convert_fusion), channel_id=1, source_target_pairs={{0,4},{1,3},{4,8},{5,1},{8,12},{9,5},{12,14},{13,9},{14,10},{15,13... | collective-permute-start | bytes 786440 | tf_op jit(solution)/shard_map/ppermute | solution.py:222
  73.6 6.4 %collective-permute-start.10 = (bf16[128,1024]{1,0:T(8,128)(2,1)S(1)}, bf16[128,1024]{1,0:T(8,128)(2,1)S(1)}, u32[]{:S(2)}, u32[]{:S(2)}) collective-permute-start(bf16[128,1024]{1,0:T(8,128)(2,1)S(1)} %convolution_convert_fusion.1), channel_id=1, source_target_pairs={{0,4},{1,3},{4,8},{5,1},{8,12},{9,5},{12,14},{13,9},{14,10},{15,13... | collective-permute-start | bytes 786440 | tf_op jit(solution)/shard_map/ppermute | solution.py:222
  77.5 6.4 %collective-permute-start.17 = (bf16[128,1024]{1,0:T(8,128)(2,1)S(1)}, bf16[128,1024]{1,0:T(8,128)(2,1)S(1)}, u32[]{:S(2)}, u32[]{:S(2)}) collective-permute-start(bf16[128,1024]{1,0:T(8,128)(2,1)S(1)} %add_convert_fusion.2), channel_id=1, source_target_pairs={{0,4},{1,3},{4,8},{5,1},{8,12},{9,5},{12,14},{13,9},{14,10},{15,13... | collective-permute-start | bytes 786440 | tf_op jit(solution)/shard_map/ppermute | solution.py:222
  80.3 6.4 %collective-permute-start.11 = (bf16[128,1024]{1,0:T(8,128)(2,1)S(1)}, bf16[128,1024]{1,0:T(8,128)(2,1)S(1)}, u32[]{:S(2)}, u32[]{:S(2)}) collective-permute-start(bf16[128,1024]{1,0:T(8,128)(2,1)S(1)} %add_convert_fusion.5), channel_id=1, source_target_pairs={{0,4},{1,3},{4,8},{5,1},{8,12},{9,5},{12,14},{13,9},{14,10},{15,13... | collective-permute-start | bytes 786440 | tf_op jit(solution)/shard_map/ppermute | solution.py:222
  84.2 6.4 %collective-permute-start.18 = (bf16[128,1024]{1,0:T(8,128)(2,1)S(1)}, bf16[128,1024]{1,0:T(8,128)(2,1)S(1)}, u32[]{:S(2)}, u32[]{:S(2)}) collective-permute-start(bf16[128,1024]{1,0:T(8,128)(2,1)S(1)} %add_convert_fusion.1), channel_id=1, source_target_pairs={{0,4},{1,3},{4,8},{5,1},{8,12},{9,5},{12,14},{13,9},{14,10},{15,13... | collective-permute-start | bytes 786440 | tf_op jit(solution)/shard_map/ppermute | solution.py:222
  87.1 6.4 %collective-permute-start.12 = (bf16[128,1024]{1,0:T(8,128)(2,1)S(1)}, bf16[128,1024]{1,0:T(8,128)(2,1)S(1)}, u32[]{:S(2)}, u32[]{:S(2)}) collective-permute-start(bf16[128,1024]{1,0:T(8,128)(2,1)S(1)} %add_convert_fusion.4), channel_id=1, source_target_pairs={{0,4},{1,3},{4,8},{5,1},{8,12},{9,5},{12,14},{13,9},{14,10},{15,13... | collective-permute-start | bytes 786440 | tf_op jit(solution)/shard_map/ppermute | solution.py:222
  90.6 6.0 %collective-permute-start.19 = (bf16[128,1024]{1,0:T(8,128)(2,1)S(1)}, bf16[128,1024]{1,0:T(8,128)(2,1)S(1)}, u32[]{:S(2)}, u32[]{:S(2)}) collective-permute-start(bf16[128,1024]{1,0:T(8,128)(2,1)S(1)} %collective-permute-done.18), channel_id=1, source_target_pairs={{0,1},{1,0},{2,3},{3,2},{4,5},{5,4},{6,7},{7,6},{8,9},{9,8},{10,11... | collective-permute-start | bytes 786440 | tf_op jit(solution)/shard_map/ppermute | solution.py:223
  93.8 6.4 %collective-permute-start.13 = (bf16[128,1024]{1,0:T(8,128)(2,1)S(1)}, bf16[128,1024]{1,0:T(8,128)(2,1)S(1)}, u32[]{:S(2)}, u32[]{:S(2)}) collective-permute-start(bf16[128,1024]{1,0:T(8,128)(2,1)S(1)} %add_convert_fusion.3), channel_id=1, source_target_pairs={{0,4},{1,3},{4,8},{5,1},{8,12},{9,5},{12,14},{13,9},{14,10},{15,13... | collective-permute-start | bytes 786440 | tf_op jit(solution)/shard_map/ppermute | solution.py:222

commit v2 on v1

--- a/solution.py
+++ b/solution.py
@@ -81,7 +81,7 @@
     return hidden, dgate, dup
 
 
-def place_kernel(ids_ref, cnt_ref, where_ref, val_ref, gu_ref, d_ref, *, blocks, edge):
+def place_kernel(ids_ref, cnt_ref, where_ref, val_ref, _, gu_ref, d_ref, *, blocks, edge):
     gu_ref[...] = jnp.zeros_like(gu_ref)
     d_ref[...] = jnp.zeros_like(d_ref)
 
@@ -108,7 +108,7 @@
     lax.fori_loop(0, cnt_ref[0], step, 0)
 
 
-def place(ids, count, where, values, blocks):
+def place(ids, count, where, values, after, blocks):
     edge = values.shape[-1]
     width = blocks * edge
     return pl.pallas_call(
@@ -116,7 +116,10 @@
         grid_spec=pltpu.PrefetchScalarGridSpec(
             num_scalar_prefetch=3,
             grid=(1,),
-            in_specs=[pl.BlockSpec(values.shape, lambda *_: (0, 0, 0))],
+            in_specs=[
+                pl.BlockSpec(values.shape, lambda *_: (0, 0, 0)),
+                pl.BlockSpec(memory_space=pl.ANY),
+            ],
             out_specs=[
                 pl.BlockSpec((width, 2 * edge), lambda *_: (0, 0)),
                 pl.BlockSpec((width, edge), lambda *_: (0, 0)),
@@ -129,80 +132,66 @@
         compiler_params=pltpu.CompilerParams(vmem_limit_bytes=24 * MIB),
         cost_estimate=pl.CostEstimate(flops=0, bytes_accessed=8 * MIB, transcendentals=0),
         name="place_weights",
-    )(ids, count, where, values)
-
-
-def grads_kernel(slot_ref, shard_ref, *refs, half, blocks, per, edge, rows):
-    mine = refs[: half + 1]
-    sib = (None,) + refs[half + 1 : 2 * half] + (None,)
-    dgu_m, dgu_s, hid_m, hid_s, out_ref = refs[2 * half :]
-    out_ref[...] = jnp.zeros_like(out_ref)
-    hm_t = hid_m[...].T
-    hs_t = hid_s[...].T
+    )(ids, count, where, values, after)
+
+
+def grads_kernel(src_ref, *refs, half, edge):
+    refs = list(refs)
+    take = lambda k: [refs.pop(0) for _ in range(k)]
+    x_m, y_m = take(half + 1), take(half + 1)
+    x_s, y_s = take(half - 1), take(half - 1)
+    dgu_m, dgu_s, hid_m, hid_s, _, out_ref, all_ref = take(7)
+    per = x_m[0].shape[1] // edge
+    left = (((0,), (0,)), ((), ()))
+    dot = lambda a, b: lax.dot_general(a, b, left, preferred_element_type=F32).astype(BF)
+    both = lambda a, b: (a.astype(F32) + b.astype(F32)).astype(BF)
+    hm, hs = hid_m[...], hid_s[...]
 
     for d in range(half + 1):
-        base = shard_ref[d] * per
-
-        def step(i, carry, d=d, base=base):
-            lane = pl.ds(pl.multiple_of(i * edge, edge), edge)
-            slots = [slot_ref[k * blocks + base + i] for k in range(3)]
-
-            @pl.when((slots[0] >= 0) | (slots[1] >= 0))
-            def _():
-                g = jnp.dot(mine[d][0:rows, lane].T, dgu_m[...], preferred_element_type=F32)
-                g = g.astype(BF)
-                if sib[d] is not None:
-                    g2 = jnp.dot(sib[d][0:rows, lane].T, dgu_s[...], preferred_element_type=F32)
-                    g = (g.astype(F32) + g2.astype(BF).astype(F32)).astype(BF)
-
-                @pl.when(slots[0] >= 0)
-                def _():
-                    out_ref[slots[0]] = g[:, 0:edge]
-
-                @pl.when(slots[1] >= 0)
-                def _():
-                    out_ref[slots[1]] = g[:, edge : 2 * edge]
-
-            @pl.when(slots[2] >= 0)
-            def _():
-                g = jnp.dot(hm_t, mine[d][rows : 2 * rows, lane], preferred_element_type=F32)
-                g = g.astype(BF)
-                if sib[d] is not None:
-                    g2 = jnp.dot(hs_t, sib[d][rows : 2 * rows, lane], preferred_element_type=F32)
-                    g = (g.astype(F32) + g2.astype(BF).astype(F32)).astype(BF)
-                out_ref[slots[2]] = g
-
-            return carry
-
-        lax.fori_loop(0, per, step, 0)
-
-
-def tile_grads(slot_of, shard_of, mine, sib, dgu_m, dgu_s, hid_m, hid_s, slots, blocks):
-    rows, edge = hid_m.shape
-    half = len(mine) - 1
-    arrays = [*mine, *sib, dgu_m, dgu_s, hid_m, hid_s]
+        base = d * per * 3
+        pair = 0 < d < half
+        for i in range(per):
+            lane = slice(i * edge, (i + 1) * edge)
+            g = dot(x_m[d][:, lane], dgu_m[...])
+            h = dot(hm, y_m[d][:, lane])
+            if pair:
+                g = both(g, dot(x_s[d - 1][:, lane], dgu_s[...]))
+                h = both(h, dot(hs, y_s[d - 1][:, lane]))
+            all_ref[base + 3 * i] = g[:, :edge]
+            all_ref[base + 3 * i + 1] = g[:, edge:]
+            all_ref[base + 3 * i + 2] = h
+    all_ref[(half + 1) * per * 3] = jnp.zeros((edge, edge), BF)
+
+    def step(s, carry):
+        out_ref[s] = all_ref[src_ref[s]]
+        return carry
+
+    lax.fori_loop(0, out_ref.shape[0], step, 0, unroll=4)
+
+
+def tile_grads(src, x_m, y_m, x_s, y_s, dgu_m, dgu_s, hid_m, hid_s, after):
+    edge = hid_m.shape[1]
+    half = len(x_m) - 1
+    slots = src.shape[0]
+    tiles = (half + 1) * (x_m[0].shape[1] // edge) * 3 + 1
+    arrays = [*x_m, *y_m, *x_s, *y_s, dgu_m, dgu_s, hid_m, hid_s]
     return pl.pallas_call(
-        functools.partial(
-            grads_kernel,
-            half=half,
-            blocks=blocks,
-            per=mine[0].shape[1] // edge,
-            edge=edge,
-            rows=rows,
-        ),
+        functools.partial(grads_kernel, half=half, edge=edge),
         grid_spec=pltpu.PrefetchScalarGridSpec(
-            num_scalar_prefetch=2,
+            num_scalar_prefetch=1,
             grid=(1,),
-            in_specs=[pl.BlockSpec(a.shape, lambda *_: (0, 0)) for a in arrays],
+            in_specs=[pl.BlockSpec(a.shape, lambda *_: (0, 0)) for a in arrays]
+            + [pl.BlockSpec(memory_space=pl.ANY)],
             out_specs=pl.BlockSpec((slots, edge, edge), lambda *_: (0, 0, 0)),
+            scratch_shapes=[pltpu.VMEM((tiles, edge, edge), BF)],
         ),
         out_shape=jax.ShapeDtypeStruct((slots, edge, edge), BF),
-        compiler_params=pltpu.CompilerParams(vmem_limit_bytes=24 * MIB),
+        compiler_params=pltpu.CompilerParams(vmem_limit_bytes=28 * MIB),
         cost_estimate=pl.CostEstimate(
             flops=800_000_000, bytes_accessed=8 * MIB, transcendentals=0
         ),
         name="tile_gradients",
-    )(slot_of, shard_of, *arrays)
+    )(src, *arrays, after)
 
 
 def pick(table, index):
@@ -224,72 +213,80 @@
 
     values = fwd_values[0]
     edge = values.shape[-1]
-    rows, width = tokens.shape
+    width = tokens.shape[1]
     per = width // edge
     blocks = n * per
     slots = bwd_ids.shape[1]
 
+    x_m, y_m = [tokens], [cotangent]
+    x_s, y_s = [swap(tokens)], [swap(cotangent)]
+    for k in range(1, half + 1):
+        x_m.append(hop(x_m[-1]))
+        y_m.append(hop(y_m[-1]))
+        if k < half:
+            x_s.append(hop(x_s[-1]))
+            y_s.append(hop(y_s[-1]))
+
     core = lax.axis_index("dp")
     sign = 1 - 2 * core
     here = pick(jnp.array(pos, jnp.int32), lax.axis_index("tensor")[None])[0]
-    steps = jnp.arange(n, dtype=jnp.int32)
-    shard_of = pick(jnp.array(ring, jnp.int32), (here - sign * steps) % n)
     dist_of = ((here - jnp.array(pos, jnp.int32)) * sign) % n
     where = (dist_of[:, None] * per + jnp.arange(per, dtype=jnp.int32)[None, :]).reshape(blocks)
-    slot_iota = jnp.arange(slots, dtype=jnp.int32)
-    hit = (bwd_ids[0][None, :] == jnp.arange(3 * blocks, dtype=jnp.int32)[:, None]) & (
-        slot_iota < bwd_count[0]
-    )[None, :]
-    slot_of = jnp.max(jnp.where(hit, slot_iota[None, :], -1), axis=1)
-
-    own = jnp.concatenate([tokens, cotangent], axis=0)
-    mine = [own]
-    sib = [swap(own)]
-    for k in range(1, half + 1):
-        mine.append(hop(mine[-1]))
-        if k < half:
-            sib.append(hop(sib[-1]))
-
-    w_gu, w_d = place(fwd_ids[0], fwd_count, where, values, blocks)
+    back = bwd_ids[0]
+    spot = pick(where, back % blocks)
+    held = (spot < (half + 1) * per) & (jnp.arange(slots, dtype=jnp.int32) < bwd_count[0])
+    src = jnp.where(held, spot * 3 + back // blocks, (half + 1) * per * 3)
+
+    w_gu, w_d = place(fwd_ids[0], fwd_count, where, values, y_s[0], blocks)
     gu_at = lambda d: w_gu[d * width : (d + 1) * width]
     d_at = lambda d: w_d[d * width : (d + 1) * width]
     dot = functools.partial(jnp.dot, preferred_element_type=F32)
 
-    gu_m = dot(mine[0][:rows], gu_at(0))
-    dh_m = dot(mine[0][rows:], d_at(0))
-    gu_s = dh_s = None
+    gu_m, dh_m = dot(x_m[0], gu_at(0)), dot(y_m[0], d_at(0))
+    gu_s, dh_s = dot(x_s[1], gu_at(1)), dot(y_s[1], d_at(1))
     for d in range(1, half + 1):
-        gu_m = gu_m + dot(mine[d][:rows], gu_at(d))
-        dh_m = dh_m + dot(mine[d][rows:], d_at(d))
-        if d < half:
-            part = dot(sib[d][:rows], gu_at(d))
-            gu_s = part if gu_s is None else gu_s + part
-            part = dot(sib[d][rows:], d_at(d))
-            dh_s = part if dh_s is None else dh_s + part
-    gu_tm, gu_ts = gu_m + swap(gu_s), gu_s + swap(gu_m)
-    dh_tm, dh_ts = dh_m + swap(dh_s), dh_s + swap(dh_m)
+        gu_m = gu_m + dot(x_m[d], gu_at(d))
+        dh_m = dh_m + dot(y_m[d], d_at(d))
+        if 1 < d < half:
+            gu_s = gu_s + dot(x_s[d], gu_at(d))
+            dh_s = dh_s + dot(y_s[d], d_at(d))
+    gu_tm, dh_tm = gu_m + swap(gu_s), dh_m + swap(dh_s)
+    gu_ts, dh_ts = gu_s + swap(gu_m), dh_s + swap(dh_m)
 
     hid_m, dg_m, du_m = activations(gu_tm[:, :edge], gu_tm[:, edge:], dh_tm)
     hid_s, dg_s, du_s = activations(gu_ts[:, :edge], gu_ts[:, edge:], dh_ts)
     dgu_m = jnp.concatenate([dg_m, du_m], axis=1)
     dgu_s = jnp.concatenate([dg_s, du_s], axis=1)
 
-    term = lambda dgu, d: lax.dot_general(
-        dgu, gu_at(d), (((1,), (1,)), ((), ())), preferred_element_type=F32
-    )
-    run_m = hop(term(dgu_m, half).astype(BF))
-    run_s = None
+    part = width // 2
+
+    def term(dgu, d, p):
+        rows = w_gu[d * width + p * part : d * width + (p + 1) * part]
+        return lax.dot_general(dgu, rows, (((1,), (1,)), ((), ())), preferred_element_type=F32)
+
+    run_m = [hop(term(dgu_m, half, p).astype(BF)) for p in range(2)]
+    run_s = [None, None]
+    first = None
     for d in range(half + 1, n):
-        part = term(dgu_s, d)
-        run_s = hop((part if run_s is None else part + run_s.astype(F32)).astype(BF))
-        run_m = hop((term(dgu_m, d) + run_m.astype(F32)).astype(BF))
-    dx = term(dgu_m, 0) + run_m.astype(F32) + swap(run_s).astype(F32)
+        for p in range(2):
+            out = term(dgu_s, d, p)
+            if run_s[p] is not None:
+                out = out + run_s[p].astype(F32)
+            run_s[p] = hop(out.astype(BF))
+        if first is None:
+            first = run_s[0]
+        for p in range(2):
+            run_m[p] = hop((term(dgu_m, d, p) + run_m[p].astype(F32)).astype(BF))
+    dx = [
+        (term(dgu_m, 0, p) + run_m[p].astype(F32) + swap(run_s[p]).astype(F32)).astype(BF)
+        for p in range(2)
+    ]
 
     grads = tile_grads(
-        slot_of, shard_of, mine, sib[1:], dgu_m, dgu_s, hid_m, hid_s, slots, blocks
+        src, x_m, y_m, x_s[1:half], y_s[1:half], dgu_m, dgu_s, hid_m, hid_s, first
     )
     grads = grads + swap(grads)
-    return dx.astype(BF), grads[None]
+    return jnp.concatenate(dx, axis=1), grads[None]
 
 
 def on_device(tokens, cotangent, fwd_values, *rest, n, cores):

time: 103 us -> 91.3 us (0.89)
  Pallas kernels: 13.9 us -> 6.29 us
  waiting for transfers between devices: 40 us -> 36.2 us
  local copies, waits for them, and re-layouts: 4.19 us -> 2.25 us
    pallas_call x1, Pallas kernels: 9.95 us -> 2.7 us  [tile_grads(): pl.pallas_call(functools.partial(grads_kernel, half=half, edge=edge), gri...]
    ppermute x14 -> x28, waiting for transfers between devices: 39.2 us -> 36.1 us  [ring_plan(): hop = lambda v: lax.ppermute(v, ('tensor', 'dp'), perm)]
    ppermute x14 -> x28, starting transfers between devices: 25.6 us -> 26.9 us  [ring_plan(): hop = lambda v: lax.ppermute(v, ('tensor', 'dp'), perm)]
    unnamed x7 -> x8, local copies, waits for them, and re-layouts: 3.14 us -> 2.16 us
    dot_general x24 -> x32, matrix products: 7.95 us -> 8.15 us  [the longest x16 3.56 us: term(): lax.dot_general(dgu, rows, (((1,), (1,)), ((), ())), preferred_element_ty...]
  transfers between devices with their start and end apart: 21 -> 37, of which waited for: 12 -> 16; matrix products, arithmetic and copies ran while one was open for 13% -> 15% of each run, Pallas kernels for 4% -> 7%
where the time goes in v2:
time: 91.3 us; the launch traced here: 90.6 us
  waiting for transfers between devices  36.2 us (40%)
  starting transfers between devices  28.3 us (31%)
  matrix products  8.15 us (9%)
  other arithmetic  6.97 us (8%)
  Pallas kernels  6.29 us (7%)
  between operations  2.36 us (3%)
  local copies, waits for them, and re-layouts  2.25 us (2%)
    ppermute x28, waiting for transfers between devices, ring_plan(): hop = lambda v: lax.ppermute(v, ('tensor', 'dp'), perm)  36.1 us
    ppermute x28, starting transfers between devices, ring_plan(): hop = lambda v: lax.ppermute(v, ('tensor', 'dp'), perm)  26.9 us
    pallas_call x1, Pallas kernels, place(): pl.pallas_call(functools.partial(place_kernel, blocks=blocks, edge=edge),...  3.59 us
    dot_general x16, matrix products, term(): lax.dot_general(dgu, rows, (((1,), (1,)), ((), ())), preferred_element_ty...  3.56 us
    pallas_call x1, Pallas kernels, tile_grads(): pl.pallas_call(functools.partial(grads_kernel, half=half, edge=edge), gri...  2.7 us
    unnamed x8, local copies, waits for them, and re-layouts  2.16 us
    broadcast_in_dim x1, other arithmetic, ring_plan(): return (jnp.concatenate(dx, axis=1), grads[None])  1.98 us
  transfers between devices with their start and end apart: 37, of which 16 were waited for; matrix products, arithmetic and copies ran while one was open for 15% of the time, Pallas kernels for 7%

profile of v2, /device:TPU:0, one launch (start us, length us, event | category | flops | bytes accessed | tf_op | source)
XLA Modules:
  0.0 90.6 jit_solution(14164311742079510352)
XLA Ops:
  0.6 0.5 collective-permute-start.13
  1.1 2.6 %collective-permute-start.9 = (bf16[128,1024]{1,0:T(8,128)(2,1)}, bf16[128,1024]{1,0:T(8,128)(2,1)S(1)}, u32[]{:S(2)}, u32[]{:S(2)}) collective-permute-start(bf16[128,1024]{1,0:T(8,128)(2,1)} %refs_0_.1), channel_id=1, source_target_pairs={{0,4},{1,3},{4,8},{5,1},{8,12},{9,5},{12,14},{13,9},{14,10},{15,13... | collective-permute-start | bytes 786440 | tf_op jit(solution)/shard_map/ppermute | solution.py:211
  3.9 1.5 %collective-permute-start.1 = (bf16[128,1024]{1,0:T(8,128)(2,1)}, bf16[128,1024]{1,0:T(8,128)(2,1)S(1)}, u32[]{:S(2)}, u32[]{:S(2)}) collective-permute-start(bf16[128,1024]{1,0:T(8,128)(2,1)} %refs_5_.1), channel_id=1, source_target_pairs={{0,4},{1,3},{4,8},{5,1},{8,12},{9,5},{12,14},{13,9},{14,10},{15,13... | collective-permute-start | bytes 786440 | tf_op jit(solution)/shard_map/ppermute | solution.py:211
  5.4 1.3 %fusion.52 = s32[]{:T(128)} fusion(s32[8]{0:T(128)} %constant.65.clone, s32[]{:T(128)S(6)} %axis_index.23), kind=kLoop, calls=%fused_computation.107 | loop fusion | flops 23 | bytes 40 | tf_op jit(solution)/shard_map/reduce_sum | solution.py:200
  6.7 1.3 %fusion.53 = s32[8]{0:T(128)S(1)} fusion(s32[8]{0:T(128)} %constant.71, s32[]{:T(128)S(6)} %sub.23, s32[]{:T(128)} %fusion.52), kind=kLoop, calls=%fused_computation.108 | loop fusion | flops 112 | bytes 72 | tf_op jit(solution)/shard_map/mul | solution.py:234
  8.1 0.7 and_select_fusion.2
  10.2 0.7 and_select_fusion.1.src_ref
  10.9 1.6 %collective-permute-start.14 = (bf16[128,1024]{1,0:T(8,128)(2,1)S(1)}, bf16[128,1024]{1,0:T(8,128)(2,1)S(1)}, u32[]{:S(2)}, u32[]{:S(2)}) collective-permute-start(bf16[128,1024]{1,0:T(8,128)(2,1)S(1)} %collective-permute-done.13), channel_id=1, source_target_pairs={{0,4},{1,3},{4,8},{5,1},{8,12},{9,5},{12,14},{13,9},{14,10},{15,13... | collective-permute-start | bytes 786440 | tf_op jit(solution)/shard_map/ppermute | solution.py:211
  12.5 1.5 %copy-done = bf16[1,56,128,128]{3,2,1,0:T(8,128)(2,1)S(1)} copy-done((bf16[1,56,128,128]{3,2,1,0:T(8,128)(2,1)S(1)}, bf16[1,56,128,128]{3,2,1,0:T(8,128)(2,1)}, u32[]{:S(2)}) %copy-start) | copy-done | bytes 1835032
  14.0 0.7 copy-done.3
  14.7 3.6 %place_weights.1 = (bf16[8192,256]{1,0:T(8,128)(2,1)S(1)}, bf16[8192,128]{1,0:T(8,128)(2,1)S(1)}) custom-call(s32[56]{0:T(128)S(1)} %bitcast.48, s32[1]{0:T(128)S(6)} %copy.59.cnt_ref, s32[64]{0:T(128)S(1)} %add.170.where_ref, bf16[56,128,128]{2,1,0:T(8,128)(2,1)S(1)} %bitcast.47, bf16[128,1024]{1,0:T(8,128)(2,1)S(1)} %collective-permute-done._), custom_call_target="tpu_custom_call" | custom-call | bytes 8388608 | tf_op jit(solution)/shard_map/place_weights/pallas_call | solution.py:114
  18.3 0.2 fusion.20
  18.5 1.2 %convolution_add_fusion.17 = f32[256,128]{0,1:T(8,128)S(1)} fusion(f32[256,128]{0,1:T(8,128)S(1)} %fusion.20, bf16[128,1024]{1,0:T(8,128)(2,1)} %refs_0_.1, bf16[8192,256]{1,0:T(8,128)(2,1)S(1)} %get-tuple-element.5), kind=kOutput, calls=%fused_computation.34 | convolution fusion | flops 67141632 | bytes 1048576 | tf_op jit(solution)/shard_map/dot_general | solution.py:245
  19.7 0.7 collective-permute-start.2
  20.9 0.8 collective-permute-start.10
  21.7 1.5 %collective-permute-start.5 = (bf16[128,1024]{1,0:T(8,128)(2,1)S(1)}, bf16[128,1024]{1,0:T(8,128)(2,1)S(1)}, u32[]{:S(2)}, u32[]{:S(2)}) collective-permute-start(bf16[128,1024]{1,0:T(8,128)(2,1)S(1)} %collective-permute-done._), channel_id=1, source_target_pairs={{0,4},{1,3},{4,8},{5,1},{8,12},{9,5},{12,14},{13,9},{14,10},{15,13... | collective-permute-start | bytes 786440 | tf_op jit(solution)/shard_map/ppermute | solution.py:211
  23.2 0.2 fusion.22
  23.7 2.5 %collective-permute-done.2.refs_7_ = bf16[128,1024]{1,0:T(8,128)(2,1)S(1)} collective-permute-done((bf16[128,1024]{1,0:T(8,128)(2,1)S(1)}, bf16[128,1024]{1,0:T(8,128)(2,1)S(1)}, u32[]{:S(2)}, u32[]{:S(2)}) %collective-permute-start.2) | collective-permute-done | bytes 262176 | tf_op jit(solution)/shard_map/ppermute | solution.py:211
  26.4 5.4 %collective-permute-done.5.refs_13_ = bf16[128,1024]{1,0:T(8,128)(2,1)S(1)} collective-permute-done((bf16[128,1024]{1,0:T(8,128)(2,1)S(1)}, bf16[128,1024]{1,0:T(8,128)(2,1)S(1)}, u32[]{:S(2)}, u32[]{:S(2)}) %collective-permute-start.5) | collective-permute-done | bytes 262176 | tf_op jit(solution)/shard_map/ppermute | solution.py:211
  32.0 0.7 collective-permute-start.6
  32.7 0.8 collective-permute-start.3
  33.5 1.5 %collective-permute-start.11 = (bf16[128,1024]{1,0:T(8,128)(2,1)S(1)}, bf16[128,1024]{1,0:T(8,128)(2,1)S(1)}, u32[]{:S(2)}, u32[]{:S(2)}) collective-permute-start(bf16[128,1024]{1,0:T(8,128)(2,1)S(1)} %collective-permute-done.10.refs_2_), channel_id=1, source_target_pairs={{0,4},{1,3},{4,8},{5,1},{8,12},{9,5},{12,14},{13,9},{14,10},{15,13... | collective-permute-start | bytes 786440 | tf_op jit(solution)/shard_map/ppermute | solution.py:211
  35.0 0.2 convolution_add_fusion.16
  35.4 0.2 convolution_add_fusion.13
  35.7 8.3 %collective-permute-done.11.refs_3_ = bf16[128,1024]{1,0:T(8,128)(2,1)S(1)} collective-permute-done((bf16[128,1024]{1,0:T(8,128)(2,1)S(1)}, bf16[128,1024]{1,0:T(8,128)(2,1)S(1)}, u32[]{:S(2)}, u32[]{:S(2)}) %collective-permute-start.11) | collective-permute-done | bytes 262176 | tf_op jit(solution)/shard_map/ppermute | solution.py:211
  44.0 0.7 collective-permute-start.12
  44.7 0.2 convolution_add_fusion.15
  45.0 0.8 collective-permute-start.7
  46.0 1.5 %collective-permute-start.4 = (bf16[128,1024]{1,0:T(8,128)(2,1)S(1)}, bf16[128,1024]{1,0:T(8,128)(2,1)S(1)}, u32[]{:S(2)}, u32[]{:S(2)}) collective-permute-start(bf16[128,1024]{1,0:T(8,128)(2,1)S(1)} %collective-permute-done.3.refs_8_), channel_id=1, source_target_pairs={{0,4},{1,3},{4,8},{5,1},{8,12},{9,5},{12,14},{13,9},{14,10},{15,13... | collective-permute-start | bytes 786440 | tf_op jit(solution)/shard_map/ppermute | solution.py:211
  47.8 2.6 %collective-permute-done.12.refs_4_ = bf16[128,1024]{1,0:T(8,128)(2,1)S(1)} collective-permute-done((bf16[128,1024]{1,0:T(8,128)(2,1)S(1)}, bf16[128,1024]{1,0:T(8,128)(2,1)S(1)}, u32[]{:S(2)}, u32[]{:S(2)}) %collective-permute-start.12) | collective-permute-done | bytes 262176 | tf_op jit(solution)/shard_map/ppermute | solution.py:211
  50.4 0.2 fusion.11
  50.7 5.3 %collective-permute-done.4.refs_9_ = bf16[128,1024]{1,0:T(8,128)(2,1)S(1)} collective-permute-done((bf16[128,1024]{1,0:T(8,128)(2,1)S(1)}, bf16[128,1024]{1,0:T(8,128)(2,1)S(1)}, u32[]{:S(2)}, u32[]{:S(2)}) %collective-permute-start.4) | collective-permute-done | bytes 262176 | tf_op jit(solution)/shard_map/ppermute | solution.py:211
  56.3 0.2 fusion.10
  56.6 0.6 collective-permute-start.17
  57.6 0.2 convolution_convert_fusion
  57.9 0.2 convolution_convert_fusion.2
  58.1 0.7 collective-permute-start.24
  59.2 0.8 collective-permute-start.32
  60.0 1.5 %collective-permute-start.28 = (bf16[128,512]{1,0:T(8,128)(2,1)S(1)}, bf16[128,512]{1,0:T(8,128)(2,1)S(1)}, u32[]{:S(2)}, u32[]{:S(2)}) collective-permute-start(bf16[128,512]{1,0:T(8,128)(2,1)S(1)} %convolution_convert_fusion.1), channel_id=1, source_target_pairs={{0,4},{1,3},{4,8},{5,1},{8,12},{9,5},{12,14},{13,9},{14,10},{15,13... | collective-permute-start | bytes 393224 | tf_op jit(solution)/shard_map/ppermute | solution.py:211
  61.5 1.6 %collective-permute-done.24.refs_20_ = bf16[128,512]{1,0:T(8,128)(2,1)S(1)} collective-permute-done((bf16[128,512]{1,0:T(8,128)(2,1)S(1)}, bf16[128,512]{1,0:T(8,128)(2,1)S(1)}, u32[]{:S(2)}, u32[]{:S(2)}) %collective-permute-start.24) | collective-permute-done | bytes 131104 | tf_op jit(solution)/shard_map/ppermute | solution.py:211
  63.1 2.7 %tile_gradients.1 = bf16[96,128,128]{2,1,0:T(8,128)(2,1)S(1)} custom-call(s32[96]{0:T(128)S(1)} %and_select_fusion.1.src_ref, bf16[128,1024]{1,0:T(8,128)(2,1)S(1)} %copy-done.2, bf16[128,1024]{1,0:T(8,128)(2,1)S(1)} %collective-permute-done.9.refs_1_, bf16[128,1024]{1,0:T(8,128)(2,1)S(1)} %collective-permute-done.10.refs_2_, ...), custom_call_target="tpu_custom_call" | custom-call | flops 800000000 | bytes 8388608 | tf_op jit(solution)/shard_map/tile_gradients/pallas_call | solution.py:178
  66.1 0.7 collective-permute-start.18
  67.1 0.8 collective-permute-start.33
  68.2 1.5 %collective-permute-start.29 = (bf16[128,512]{1,0:T(8,128)(2,1)S(1)}, bf16[128,512]{1,0:T(8,128)(2,1)S(1)}, u32[]{:S(2)}, u32[]{:S(2)}) collective-permute-start(bf16[128,512]{1,0:T(8,128)(2,1)S(1)} %fusion.7), channel_id=1, source_target_pairs={{0,4},{1,3},{4,8},{5,1},{8,12},{9,5},{12,14},{13,9},{14,10},{15,13... | collective-permute-start | bytes 393224 | tf_op jit(solution)/shard_map/ppermute | solution.py:211
  70.1 1.0 %collective-permute-done.18 = bf16[128,512]{1,0:T(8,128)(2,1)S(1)} collective-permute-done((bf16[128,512]{1,0:T(8,128)(2,1)S(1)}, bf16[128,512]{1,0:T(8,128)(2,1)S(1)}, u32[]{:S(2)}, u32[]{:S(2)}) %collective-permute-start.18) | collective-permute-done | bytes 131104 | tf_op jit(solution)/shard_map/ppermute | solution.py:211
  71.4 0.7 collective-permute-start.19
  72.1 0.4 collective-permute-done.33
  72.8 0.7 collective-permute-start.34
  73.5 0.4 collective-permute-done.29
  74.2 0.8 collective-permute-start.30
  74.9 0.4 collective-permute-done.25
  75.6 0.8 collective-permute-start.26
  76.4 0.4 collective-permute-done.19
  77.0 0.8 collective-permute-start.20
  77.8 1.8 %collective-permute-done.30 = bf16[128,512]{1,0:T(8,128)(2,1)S(1)} collective-permute-done((bf16[128,512]{1,0:T(8,128)(2,1)S(1)}, bf16[128,512]{1,0:T(8,128)(2,1)S(1)}, u32[]{:S(2)}, u32[]{:S(2)}) %collective-permute-start.30) | collective-permute-done | bytes 131104 | tf_op jit(solution)/shard_map/ppermute | solution.py:211
  79.8 0.8 collective-permute-start.31
  80.6 1.8 %collective-permute-done.20 = bf16[128,512]{1,0:T(8,128)(2,1)S(1)} collective-permute-done((bf16[128,512]{1,0:T(8,128)(2,1)S(1)}, bf16[128,512]{1,0:T(8,128)(2,1)S(1)}, u32[]{:S(2)}, u32[]{:S(2)}) %collective-permute-start.20) | collective-permute-done | bytes 131104 | tf_op jit(solution)/shard_map/ppermute | solution.py:211
  82.6 0.8 collective-permute-start.21
  83.4 1.4 %collective-permute-done.31 = bf16[128,512]{1,0:T(8,128)(2,1)S(1)} collective-permute-done((bf16[128,512]{1,0:T(8,128)(2,1)S(1)}, bf16[128,512]{1,0:T(8,128)(2,1)S(1)}, u32[]{:S(2)}, u32[]{:S(2)}) %collective-permute-start.31) | collective-permute-done | bytes 131104 | tf_op jit(solution)/shard_map/ppermute | solution.py:211
  84.8 0.2 add_convert_fusion
  85.1 2.6 %collective-permute-done.21 = bf16[128,512]{1,0:T(8,128)(2,1)S(1)} collective-permute-done((bf16[128,512]{1,0:T(8,128)(2,1)S(1)}, bf16[128,512]{1,0:T(8,128)(2,1)S(1)}, u32[]{:S(2)}, u32[]{:S(2)}) %collective-permute-start.21) | collective-permute-done | bytes 131104 | tf_op jit(solution)/shard_map/ppermute | solution.py:211
  87.6 0.2 add_convert_fusion.1
  87.9 0.7 pad_maximum_fusion
  88.6 2.0 %add_bitcast_fusion = bf16[1,96,128,128]{3,2,1,0:T(8,128)(2,1)} fusion(bf16[96,128,128]{2,1,0:T(8,128)(2,1)S(1)} %tile_gradients.1, bf16[96,128,128]{2,1,0:T(8,128)(2,1)S(1)} %collective-permute-done.36), kind=kLoop, calls=%fused_computation | loop fusion | flops 1572864 | bytes 9437184 | tf_op jit(solution)/shard_map/broadcast_in_dim | solution.py:289
  (67 shorter events, 6.0 us)
Async XLA Ops:
  0.6 10.2 %collective-permute-start.13 = (bf16[128,1024]{1,0:T(8,128)(2,1)}, bf16[128,1024]{1,0:T(8,128)(2,1)S(1)}, u32[]{:S(2)}, u32[]{:S(2)}) collective-permute-start(bf16[128,1024]{1,0:T(8,128)(2,1)} %refs_0_.1), channel_id=1, source_target_pairs={{0,1},{1,0},{2,3},{3,2},{4,5},{5,4},{6,7},{7,6},{8,9},{9,8},{10,11... | collective-permute-start | bytes 786440 | tf_op jit(solution)/shard_map/ppermute | solution.py:212
  1.1 17.1 %collective-permute-start.9 = (bf16[128,1024]{1,0:T(8,128)(2,1)}, bf16[128,1024]{1,0:T(8,128)(2,1)S(1)}, u32[]{:S(2)}, u32[]{:S(2)}) collective-permute-start(bf16[128,1024]{1,0:T(8,128)(2,1)} %refs_0_.1), channel_id=1, source_target_pairs={{0,4},{1,3},{4,8},{5,1},{8,12},{9,5},{12,14},{13,9},{14,10},{15,13... | collective-permute-start | bytes 786440 | tf_op jit(solution)/shard_map/ppermute | solution.py:211
  3.8 8.7 %collective-permute-start = (bf16[128,1024]{1,0:T(8,128)(2,1)}, bf16[128,1024]{1,0:T(8,128)(2,1)S(1)}, u32[]{:S(2)}, u32[]{:S(2)}) collective-permute-start(bf16[128,1024]{1,0:T(8,128)(2,1)} %refs_5_.1), channel_id=1, source_target_pairs={{0,1},{1,0},{2,3},{3,2},{4,5},{5,4},{6,7},{7,6},{8,9},{9,8},{10,11... | collective-permute-start | bytes 786440 | tf_op jit(solution)/shard_map/ppermute | solution.py:212
  3.9 15.8 %collective-permute-start.1 = (bf16[128,1024]{1,0:T(8,128)(2,1)}, bf16[128,1024]{1,0:T(8,128)(2,1)S(1)}, u32[]{:S(2)}, u32[]{:S(2)}) collective-permute-start(bf16[128,1024]{1,0:T(8,128)(2,1)} %refs_5_.1), channel_id=1, source_target_pairs={{0,4},{1,3},{4,8},{5,1},{8,12},{9,5},{12,14},{13,9},{14,10},{15,13... | collective-permute-start | bytes 786440 | tf_op jit(solution)/shard_map/ppermute | solution.py:211
  10.9 12.4 %collective-permute-start.14 = (bf16[128,1024]{1,0:T(8,128)(2,1)S(1)}, bf16[128,1024]{1,0:T(8,128)(2,1)S(1)}, u32[]{:S(2)}, u32[]{:S(2)}) collective-permute-start(bf16[128,1024]{1,0:T(8,128)(2,1)S(1)} %collective-permute-done.13), channel_id=1, source_target_pairs={{0,4},{1,3},{4,8},{5,1},{8,12},{9,5},{12,14},{13,9},{14,10},{15,13... | collective-permute-start | bytes 786440 | tf_op jit(solution)/shard_map/ppermute | solution.py:211
  12.5 1.5 %copy-start = (bf16[1,56,128,128]{3,2,1,0:T(8,128)(2,1)S(1)}, bf16[1,56,128,128]{3,2,1,0:T(8,128)(2,1)}, u32[]{:S(2)}) copy-start(bf16[1,56,128,128]{3,2,1,0:T(8,128)(2,1)} %param.11) | copy-start | bytes 5505028
  14.0 0.7 copy-start.3
  14.6 6.0 %copy-start.1 = (bf16[128,1024]{1,0:T(8,128)(2,1)S(1)}, bf16[128,1024]{1,0:T(8,128)(2,1)}, u32[]{:S(2)}) copy-start(bf16[128,1024]{1,0:T(8,128)(2,1)} %refs_5_.1) | copy-start | bytes 786436
  19.7 6.4 %collective-permute-start.2 = (bf16[128,1024]{1,0:T(8,128)(2,1)S(1)}, bf16[128,1024]{1,0:T(8,128)(2,1)S(1)}, u32[]{:S(2)}, u32[]{:S(2)}) collective-permute-start(bf16[128,1024]{1,0:T(8,128)(2,1)S(1)} %collective-permute-done.1.refs_6_), channel_id=1, source_target_pairs={{0,4},{1,3},{4,8},{5,1},{8,12},{9,5},{12,14},{13,9},{14,10},{15,13... | collective-permute-start | bytes 786440 | tf_op jit(solution)/shard_map/ppermute | solution.py:211
  20.9 12.6 %collective-permute-start.10 = (bf16[128,1024]{1,0:T(8,128)(2,1)S(1)}, bf16[128,1024]{1,0:T(8,128)(2,1)S(1)}, u32[]{:S(2)}, u32[]{:S(2)}) collective-permute-start(bf16[128,1024]{1,0:T(8,128)(2,1)S(1)} %collective-permute-done.9.refs_1_), channel_id=1, source_target_pairs={{0,4},{1,3},{4,8},{5,1},{8,12},{9,5},{12,14},{13,9},{14,10},{15,13... | collective-permute-start | bytes 786440 | tf_op jit(solution)/shard_map/ppermute | solution.py:211
  21.7 10.0 %collective-permute-start.5 = (bf16[128,1024]{1,0:T(8,128)(2,1)S(1)}, bf16[128,1024]{1,0:T(8,128)(2,1)S(1)}, u32[]{:S(2)}, u32[]{:S(2)}) collective-permute-start(bf16[128,1024]{1,0:T(8,128)(2,1)S(1)} %collective-permute-done._), channel_id=1, source_target_pairs={{0,4},{1,3},{4,8},{5,1},{8,12},{9,5},{12,14},{13,9},{14,10},{15,13... | collective-permute-start | bytes 786440 | tf_op jit(solution)/shard_map/ppermute | solution.py:211
  23.5 11.8 %collective-permute-start.15 = (bf16[128,1024]{1,0:T(8,128)(2,1)S(1)}, bf16[128,1024]{1,0:T(8,128)(2,1)S(1)}, u32[]{:S(2)}, u32[]{:S(2)}) collective-permute-start(bf16[128,1024]{1,0:T(8,128)(2,1)S(1)} %collective-permute-done.14.refs_10_), channel_id=1, source_target_pairs={{0,4},{1,3},{4,8},{5,1},{8,12},{9,5},{12,14},{13,9},{14,10},{15,13... | collective-permute-start | bytes 786440 | tf_op jit(solution)/shard_map/ppermute | solution.py:211
  32.0 13.0 %collective-permute-start.6 = (bf16[128,1024]{1,0:T(8,128)(2,1)S(1)}, bf16[128,1024]{1,0:T(8,128)(2,1)S(1)}, u32[]{:S(2)}, u32[]{:S(2)}) collective-permute-start(bf16[128,1024]{1,0:T(8,128)(2,1)S(1)} %collective-permute-done.5.refs_13_), channel_id=1, source_target_pairs={{0,4},{1,3},{4,8},{5,1},{8,12},{9,5},{12,14},{13,9},{14,10},{15,13... | collective-permute-start | bytes 786440 | tf_op jit(solution)/shard_map/ppermute | solution.py:211
  32.7 13.3 %collective-permute-start.3 = (bf16[128,1024]{1,0:T(8,128)(2,1)S(1)}, bf16[128,1024]{1,0:T(8,128)(2,1)S(1)}, u32[]{:S(2)}, u32[]{:S(2)}) collective-permute-start(bf16[128,1024]{1,0:T(8,128)(2,1)S(1)} %collective-permute-done.2.refs_7_), channel_id=1, source_target_pairs={{0,4},{1,3},{4,8},{5,1},{8,12},{9,5},{12,14},{13,9},{14,10},{15,13... | collective-permute-start | bytes 786440 | tf_op jit(solution)/shard_map/ppermute | solution.py:211
  33.5 10.5 %collective-permute-start.11 = (bf16[128,1024]{1,0:T(8,128)(2,1)S(1)}, bf16[128,1024]{1,0:T(8,128)(2,1)S(1)}, u32[]{:S(2)}, u32[]{:S(2)}) collective-permute-start(bf16[128,1024]{1,0:T(8,128)(2,1)S(1)} %collective-permute-done.10.refs_2_), channel_id=1, source_target_pairs={{0,4},{1,3},{4,8},{5,1},{8,12},{9,5},{12,14},{13,9},{14,10},{15,13... | collective-permute-start | bytes 786440 | tf_op jit(solution)/shard_map/ppermute | solution.py:211
  35.2 21.1 %collective-permute-start.16 = (bf16[128,1024]{1,0:T(8,128)(2,1)S(1)}, bf16[128,1024]{1,0:T(8,128)(2,1)S(1)}, u32[]{:S(2)}, u32[]{:S(2)}) collective-permute-start(bf16[128,1024]{1,0:T(8,128)(2,1)S(1)} %collective-permute-done.15.refs_11_), channel_id=1, source_target_pairs={{0,4},{1,3},{4,8},{5,1},{8,12},{9,5},{12,14},{13,9},{14,10},{15,13... | collective-permute-start | bytes 786440 | tf_op jit(solution)/shard_map/ppermute | solution.py:211
  44.0 6.4 %collective-permute-start.12 = (bf16[128,1024]{1,0:T(8,128)(2,1)S(1)}, bf16[128,1024]{1,0:T(8,128)(2,1)S(1)}, u32[]{:S(2)}, u32[]{:S(2)}) collective-permute-start(bf16[128,1024]{1,0:T(8,128)(2,1)S(1)} %collective-permute-done.11.refs_3_), channel_id=1, source_target_pairs={{0,4},{1,3},{4,8},{5,1},{8,12},{9,5},{12,14},{13,9},{14,10},{15,13... | collective-permute-start | bytes 786440 | tf_op jit(solution)/shard_map/ppermute | solution.py:211
  44.9 18.2 %copy-start.2 = (bf16[128,1024]{1,0:T(8,128)(2,1)S(1)}, bf16[128,1024]{1,0:T(8,128)(2,1)}, u32[]{:S(2)}) copy-start(bf16[128,1024]{1,0:T(8,128)(2,1)} %refs_0_.1) | copy-start | bytes 786436
  45.0 12.2 %collective-permute-start.7 = (bf16[128,1024]{1,0:T(8,128)(2,1)S(1)}, bf16[128,1024]{1,0:T(8,128)(2,1)S(1)}, u32[]{:S(2)}, u32[]{:S(2)}) collective-permute-start(bf16[128,1024]{1,0:T(8,128)(2,1)S(1)} %collective-permute-done.6.refs_14_), channel_id=1, source_target_pairs={{0,4},{1,3},{4,8},{5,1},{8,12},{9,5},{12,14},{13,9},{14,10},{15,13... | collective-permute-start | bytes 786440 | tf_op jit(solution)/shard_map/ppermute | solution.py:211
  46.0 10.0 %collective-permute-start.4 = (bf16[128,1024]{1,0:T(8,128)(2,1)S(1)}, bf16[128,1024]{1,0:T(8,128)(2,1)S(1)}, u32[]{:S(2)}, u32[]{:S(2)}) collective-permute-start(bf16[128,1024]{1,0:T(8,128)(2,1)S(1)} %collective-permute-done.3.refs_8_), channel_id=1, source_target_pairs={{0,4},{1,3},{4,8},{5,1},{8,12},{9,5},{12,14},{13,9},{14,10},{15,13... | collective-permute-start | bytes 786440 | tf_op jit(solution)/shard_map/ppermute | solution.py:211
  50.6 6.8 %collective-permute-start.23 = (f32[128,256]{1,0:T(8,128)S(1)}, f32[128,256]{1,0:T(8,128)S(1)}, u32[]{:S(2)}, u32[]{:S(2)}) collective-permute-start(f32[128,256]{1,0:T(8,128)S(1)} %fusion.11), channel_id=1, source_target_pairs={{0,1},{1,0},{2,3},{3,2},{4,5},{5,4},{6,7},{7,6},{8,9},{9,8},{10,11... | collective-permute-start | bytes 393224 | tf_op jit(solution)/shard_map/ppermute | solution.py:212
  56.2 1.3 %collective-permute-start.22 = (f32[128,128]{1,0:T(8,128)S(1)}, f32[128,128]{1,0:T(8,128)S(1)}, u32[]{:S(2)}, u32[]{:S(2)}) collective-permute-start(f32[128,128]{1,0:T(8,128)S(1)} %fusion.13), channel_id=1, source_target_pairs={{0,1},{1,0},{2,3},{3,2},{4,5},{5,4},{6,7},{7,6},{8,9},{9,8},{10,11... | collective-permute-start | bytes 196616 | tf_op jit(solution)/shard_map/ppermute | solution.py:212
  56.6 2.2 %collective-permute-start.17 = (f32[128,256]{1,0:T(8,128)S(1)}, f32[128,256]{1,0:T(8,128)S(1)}, u32[]{:S(2)}, u32[]{:S(2)}) collective-permute-start(f32[128,256]{1,0:T(8,128)S(1)} %fusion.10), channel_id=1, source_target_pairs={{0,1},{1,0},{2,3},{3,2},{4,5},{5,4},{6,7},{7,6},{8,9},{9,8},{10,11... | collective-permute-start | bytes 393224 | tf_op jit(solution)/shard_map/ppermute | solution.py:212
  57.4 1.5 %collective-permute-start.8 = (f32[128,128]{1,0:T(8,128)S(1)}, f32[128,128]{1,0:T(8,128)S(1)}, u32[]{:S(2)}, u32[]{:S(2)}) collective-permute-start(f32[128,128]{1,0:T(8,128)S(1)} %fusion.12), channel_id=1, source_target_pairs={{0,1},{1,0},{2,3},{3,2},{4,5},{5,4},{6,7},{7,6},{8,9},{9,8},{10,11... | collective-permute-start | bytes 196616 | tf_op jit(solution)/shard_map/ppermute | solution.py:212
  58.1 5.0 %collective-permute-start.24 = (bf16[128,512]{1,0:T(8,128)(2,1)S(1)}, bf16[128,512]{1,0:T(8,128)(2,1)S(1)}, u32[]{:S(2)}, u32[]{:S(2)}) collective-permute-start(bf16[128,512]{1,0:T(8,128)(2,1)S(1)} %convolution_convert_fusion.2), channel_id=1, source_target_pairs={{0,4},{1,3},{4,8},{5,1},{8,12},{9,5},{12,14},{13,9},{14,10},{15,13... | collective-permute-start | bytes 393224 | tf_op jit(solution)/shard_map/ppermute | solution.py:211
  59.2 7.7 %collective-permute-start.32 = (bf16[128,512]{1,0:T(8,128)(2,1)S(1)}, bf16[128,512]{1,0:T(8,128)(2,1)S(1)}, u32[]{:S(2)}, u32[]{:S(2)}) collective-permute-start(bf16[128,512]{1,0:T(8,128)(2,1)S(1)} %convolution_convert_fusion), channel_id=1, source_target_pairs={{0,4},{1,3},{4,8},{5,1},{8,12},{9,5},{12,14},{13,9},{14,10},{15,13... | collective-permute-start | bytes 393224 | tf_op jit(solution)/shard_map/ppermute | solution.py:211
  60.0 7.9 %collective-permute-start.28 = (bf16[128,512]{1,0:T(8,128)(2,1)S(1)}, bf16[128,512]{1,0:T(8,128)(2,1)S(1)}, u32[]{:S(2)}, u32[]{:S(2)}) collective-permute-start(bf16[128,512]{1,0:T(8,128)(2,1)S(1)} %convolution_convert_fusion.1), channel_id=1, source_target_pairs={{0,4},{1,3},{4,8},{5,1},{8,12},{9,5},{12,14},{13,9},{14,10},{15,13... | collective-permute-start | bytes 393224 | tf_op jit(solution)/shard_map/ppermute | solution.py:211
  65.8 22.8 %collective-permute-start.36 = (bf16[96,128,128]{2,1,0:T(8,128)(2,1)S(1)}, bf16[96,128,128]{2,1,0:T(8,128)(2,1)S(1)}, u32[]{:S(2)}, u32[]{:S(2)}) collective-permute-start(bf16[96,128,128]{2,1,0:T(8,128)(2,1)S(1)} %tile_gradients.1), channel_id=1, source_target_pairs={{0,1},{1,0},{2,3},{3,2},{4,5},{5,4},{6,7},{7,6},{8,9},{9,8},{10,11... | collective-permute-start | bytes 9437192 | tf_op jit(solution)/shard_map/ppermute | solution.py:212
  66.1 5.0 %collective-permute-start.18 = (bf16[128,512]{1,0:T(8,128)(2,1)S(1)}, bf16[128,512]{1,0:T(8,128)(2,1)S(1)}, u32[]{:S(2)}, u32[]{:S(2)}) collective-permute-start(bf16[128,512]{1,0:T(8,128)(2,1)S(1)} %convolution_convert_fusion.3), channel_id=1, source_target_pairs={{0,4},{1,3},{4,8},{5,1},{8,12},{9,5},{12,14},{13,9},{14,10},{15,13... | collective-permute-start | bytes 393224 | tf_op jit(solution)/shard_map/ppermute | solution.py:211
  67.1 5.5 %collective-permute-start.33 = (bf16[128,512]{1,0:T(8,128)(2,1)S(1)}, bf16[128,512]{1,0:T(8,128)(2,1)S(1)}, u32[]{:S(2)}, u32[]{:S(2)}) collective-permute-start(bf16[128,512]{1,0:T(8,128)(2,1)S(1)} %fusion.9), channel_id=1, source_target_pairs={{0,4},{1,3},{4,8},{5,1},{8,12},{9,5},{12,14},{13,9},{14,10},{15,13... | collective-permute-start | bytes 393224 | tf_op jit(solution)/shard_map/ppermute | solution.py:211
  68.2 5.8 %collective-permute-start.29 = (bf16[128,512]{1,0:T(8,128)(2,1)S(1)}, bf16[128,512]{1,0:T(8,128)(2,1)S(1)}, u32[]{:S(2)}, u32[]{:S(2)}) collective-permute-start(bf16[128,512]{1,0:T(8,128)(2,1)S(1)} %fusion.7), channel_id=1, source_target_pairs={{0,4},{1,3},{4,8},{5,1},{8,12},{9,5},{12,14},{13,9},{14,10},{15,13... | collective-permute-start | bytes 393224 | tf_op jit(solution)/shard_map/ppermute | solution.py:211
  69.9 5.4 %collective-permute-start.25 = (bf16[128,512]{1,0:T(8,128)(2,1)S(1)}, bf16[128,512]{1,0:T(8,128)(2,1)S(1)}, u32[]{:S(2)}, u32[]{:S(2)}) collective-permute-start(bf16[128,512]{1,0:T(8,128)(2,1)S(1)} %fusion.4), channel_id=1, source_target_pairs={{0,4},{1,3},{4,8},{5,1},{8,12},{9,5},{12,14},{13,9},{14,10},{15,13... | collective-permute-start | bytes 393224 | tf_op jit(solution)/shard_map/ppermute | solution.py:211
  71.4 5.4 %collective-permute-start.19 = (bf16[128,512]{1,0:T(8,128)(2,1)S(1)}, bf16[128,512]{1,0:T(8,128)(2,1)S(1)}, u32[]{:S(2)}, u32[]{:S(2)}) collective-permute-start(bf16[128,512]{1,0:T(8,128)(2,1)S(1)} %fusion.2), channel_id=1, source_target_pairs={{0,4},{1,3},{4,8},{5,1},{8,12},{9,5},{12,14},{13,9},{14,10},{15,13... | collective-permute-start | bytes 393224 | tf_op jit(solution)/shard_map/ppermute | solution.py:211
  72.8 7.8 %collective-permute-start.34 = (bf16[128,512]{1,0:T(8,128)(2,1)S(1)}, bf16[128,512]{1,0:T(8,128)(2,1)S(1)}, u32[]{:S(2)}, u32[]{:S(2)}) collective-permute-start(bf16[128,512]{1,0:T(8,128)(2,1)S(1)} %fusion.8), channel_id=1, source_target_pairs={{0,4},{1,3},{4,8},{5,1},{8,12},{9,5},{12,14},{13,9},{14,10},{15,13... | collective-permute-start | bytes 393224 | tf_op jit(solution)/shard_map/ppermute | solution.py:211
  74.2 5.4 %collective-permute-start.30 = (bf16[128,512]{1,0:T(8,128)(2,1)S(1)}, bf16[128,512]{1,0:T(8,128)(2,1)S(1)}, u32[]{:S(2)}, u32[]{:S(2)}) collective-permute-start(bf16[128,512]{1,0:T(8,128)(2,1)S(1)} %fusion.6), channel_id=1, source_target_pairs={{0,4},{1,3},{4,8},{5,1},{8,12},{9,5},{12,14},{13,9},{14,10},{15,13... | collective-permute-start | bytes 393224 | tf_op jit(solution)/shard_map/ppermute | solution.py:211
  75.6 7.8 %collective-permute-start.26 = (bf16[128,512]{1,0:T(8,128)(2,1)S(1)}, bf16[128,512]{1,0:T(8,128)(2,1)S(1)}, u32[]{:S(2)}, u32[]{:S(2)}) collective-permute-start(bf16[128,512]{1,0:T(8,128)(2,1)S(1)} %fusion.3), channel_id=1, source_target_pairs={{0,4},{1,3},{4,8},{5,1},{8,12},{9,5},{12,14},{13,9},{14,10},{15,13... | collective-permute-start | bytes 393224 | tf_op jit(solution)/shard_map/ppermute | solution.py:211
  77.0 5.4 %collective-permute-start.20 = (bf16[128,512]{1,0:T(8,128)(2,1)S(1)}, bf16[128,512]{1,0:T(8,128)(2,1)S(1)}, u32[]{:S(2)}, u32[]{:S(2)}) collective-permute-start(bf16[128,512]{1,0:T(8,128)(2,1)S(1)} %fusion.1), channel_id=1, source_target_pairs={{0,4},{1,3},{4,8},{5,1},{8,12},{9,5},{12,14},{13,9},{14,10},{15,13... | collective-permute-start | bytes 393224 | tf_op jit(solution)/shard_map/ppermute | solution.py:211
  79.8 5.0 %collective-permute-start.31 = (bf16[128,512]{1,0:T(8,128)(2,1)S(1)}, bf16[128,512]{1,0:T(8,128)(2,1)S(1)}, u32[]{:S(2)}, u32[]{:S(2)}) collective-permute-start(bf16[128,512]{1,0:T(8,128)(2,1)S(1)} %fusion.5), channel_id=1, source_target_pairs={{0,4},{1,3},{4,8},{5,1},{8,12},{9,5},{12,14},{13,9},{14,10},{15,13... | collective-permute-start | bytes 393224 | tf_op jit(solution)/shard_map/ppermute | solution.py:211
  80.6 2.8 %collective-permute-start.35 = (bf16[128,512]{1,0:T(8,128)(2,1)S(1)}, bf16[128,512]{1,0:T(8,128)(2,1)S(1)}, u32[]{:S(2)}, u32[]{:S(2)}) collective-permute-start(bf16[128,512]{1,0:T(8,128)(2,1)S(1)} %collective-permute-done.34), channel_id=1, source_target_pairs={{0,1},{1,0},{2,3},{3,2},{4,5},{5,4},{6,7},{7,6},{8,9},{9,8},{10,11... | collective-permute-start | bytes 393224 | tf_op jit(solution)/shard_map/ppermute | solution.py:212
  82.6 5.0 %collective-permute-start.21 = (bf16[128,512]{1,0:T(8,128)(2,1)S(1)}, bf16[128,512]{1,0:T(8,128)(2,1)S(1)}, u32[]{:S(2)}, u32[]{:S(2)}) collective-permute-start(bf16[128,512]{1,0:T(8,128)(2,1)S(1)} %fusion), channel_id=1, source_target_pairs={{0,4},{1,3},{4,8},{5,1},{8,12},{9,5},{12,14},{13,9},{14,10},{15,13... | collective-permute-start | bytes 393224 | tf_op jit(solution)/shard_map/ppermute | solution.py:211
  83.4 1.7 %collective-permute-start.27 = (bf16[128,512]{1,0:T(8,128)(2,1)S(1)}, bf16[128,512]{1,0:T(8,128)(2,1)S(1)}, u32[]{:S(2)}, u32[]{:S(2)}) collective-permute-start(bf16[128,512]{1,0:T(8,128)(2,1)S(1)} %collective-permute-done.26), channel_id=1, source_target_pairs={{0,1},{1,0},{2,3},{3,2},{4,5},{5,4},{6,7},{7,6},{8,9},{9,8},{10,11... | collective-permute-start | bytes 393224 | tf_op jit(solution)/shard_map/ppermute | solution.py:212

commit v3 on v2

--- a/solution.py
+++ b/solution.py
@@ -10,6 +10,7 @@
 BF = jnp.bfloat16
 F32 = jnp.float32
 MIB = 1024 * 1024
+LITTLE = pl.CostEstimate(flops=1, bytes_accessed=1, transcendentals=0)
 
 
 def place_tiles(tile_set, slot_ids, slot_live, block_count):
@@ -81,14 +82,28 @@
     return hidden, dgate, dup
 
 
-def place_kernel(ids_ref, cnt_ref, where_ref, val_ref, _, gu_ref, d_ref, *, blocks, edge):
+def split(value, size):
+    if size & (size - 1) == 0:
+        return value >> (size.bit_length() - 1), value & (size - 1)
+    return lax.div(value, size), lax.rem(value, size)
+
+
+def spot_of(block, here_ref, n, per):
+    shard, inner = split(block, per)
+    up, odd = split(shard, 2)
+    at = jnp.where(odd == 1, n - 1 - up, up)
+    _, dist = split((here_ref[0] - at) * here_ref[1] + n, n)
+    return dist * per + inner
+
+
+def place_kernel(here_ref, ids_ref, cnt_ref, val_ref, gu_ref, d_ref, *, n, blocks, edge):
     gu_ref[...] = jnp.zeros_like(gu_ref)
     d_ref[...] = jnp.zeros_like(d_ref)
 
     def step(s, carry):
         e = ids_ref[s]
-        kind = e // blocks
-        row = pl.multiple_of(where_ref[e % blocks] * edge, edge)
+        kind, block = split(e, blocks)
+        row = pl.multiple_of(spot_of(block, here_ref, n, blocks // n) * edge, edge)
         tile = val_ref[s]
 
         @pl.when(kind == 0)
@@ -108,18 +123,15 @@
     lax.fori_loop(0, cnt_ref[0], step, 0)
 
 
-def place(ids, count, where, values, after, blocks):
+def place(here, ids, count, values, n, blocks):
     edge = values.shape[-1]
     width = blocks * edge
     return pl.pallas_call(
-        functools.partial(place_kernel, blocks=blocks, edge=edge),
+        functools.partial(place_kernel, n=n, blocks=blocks, edge=edge),
         grid_spec=pltpu.PrefetchScalarGridSpec(
             num_scalar_prefetch=3,
             grid=(1,),
-            in_specs=[
-                pl.BlockSpec(values.shape, lambda *_: (0, 0, 0)),
-                pl.BlockSpec(memory_space=pl.ANY),
-            ],
+            in_specs=[pl.BlockSpec(values.shape, lambda *_: (0, 0, 0))],
             out_specs=[
                 pl.BlockSpec((width, 2 * edge), lambda *_: (0, 0)),
                 pl.BlockSpec((width, edge), lambda *_: (0, 0)),
@@ -130,17 +142,57 @@
             jax.ShapeDtypeStruct((width, edge), BF),
         ],
         compiler_params=pltpu.CompilerParams(vmem_limit_bytes=24 * MIB),
-        cost_estimate=pl.CostEstimate(flops=0, bytes_accessed=8 * MIB, transcendentals=0),
+        cost_estimate=LITTLE,
         name="place_weights",
-    )(ids, count, where, values, after)
-
-
-def grads_kernel(src_ref, *refs, half, edge):
+    )(here, ids, count, values)
+
+
+def forward_kernel(*refs, half, width):
+    refs = list(refs)
+    take = lambda k: [refs.pop(0) for _ in range(k)]
+    x_m, y_m, x_s, y_s = take(half), take(half), take(half - 1), take(half - 1)
+    w_gu, w_d, gu_m, dh_m, gu_s, dh_s = refs
+
+    def total(parts, w, first):
+        out = None
+        for d, part in enumerate(parts, first):
+            rows = w[d * width : (d + 1) * width, :]
+            term = jnp.dot(part[...], rows, preferred_element_type=F32)
+            out = term if out is None else out + term
+        return out
+
+    gu_m[...] = total(x_m, w_gu, 0)
+    dh_m[...] = total(y_m, w_d, 0)
+    gu_s[...] = total(x_s, w_gu, 1)
+    dh_s[...] = total(y_s, w_d, 1)
+
+
+def forward(x_m, y_m, x_s, y_s, w_gu, w_d):
+    half = len(x_m)
+    rows, width = x_m[0].shape
+    edge = w_d.shape[1]
+    whole = lambda shape: pl.BlockSpec(shape, lambda *_: (0, 0))
+    gu, dh = (rows, 2 * edge), (rows, edge)
+    arrays = [*x_m, *y_m, *x_s, *y_s, w_gu, w_d]
+    return pl.pallas_call(
+        functools.partial(forward_kernel, half=half, width=width),
+        grid=(1,),
+        in_specs=[whole(a.shape) for a in arrays],
+        out_specs=[whole(gu), whole(dh), whole(gu), whole(dh)],
+        out_shape=[jax.ShapeDtypeStruct(t, F32) for t in (gu, dh, gu, dh)],
+        compiler_params=pltpu.CompilerParams(vmem_limit_bytes=28 * MIB),
+        cost_estimate=LITTLE,
+        name="forward_terms",
+    )(*arrays)
+
+
+def grads_kernel(here_ref, ids_ref, cnt_ref, *refs, half, blocks, edge):
     refs = list(refs)
     take = lambda k: [refs.pop(0) for _ in range(k)]
     x_m, y_m = take(half + 1), take(half + 1)
     x_s, y_s = take(half - 1), take(half - 1)
-    dgu_m, dgu_s, hid_m, hid_s, _, out_ref, all_ref = take(7)
+    dgu_m, dgu_s, hid_m, hid_s = take(4)
+    out_ref, all_ref = refs[-2:]
     per = x_m[0].shape[1] // edge
     left = (((0,), (0,)), ((), ()))
     dot = lambda a, b: lax.dot_general(a, b, left, preferred_element_type=F32).astype(BF)
@@ -160,96 +212,83 @@
             all_ref[base + 3 * i] = g[:, :edge]
             all_ref[base + 3 * i + 1] = g[:, edge:]
             all_ref[base + 3 * i + 2] = h
-    all_ref[(half + 1) * per * 3] = jnp.zeros((edge, edge), BF)
+    none = (half + 1) * per * 3
+    all_ref[none] = jnp.zeros((edge, edge), BF)
+    count = cnt_ref[0]
 
     def step(s, carry):
-        out_ref[s] = all_ref[src_ref[s]]
+        e = ids_ref[s]
+        kind, block = split(e, blocks)
+        spot = spot_of(block, here_ref, 2 * half, per)
+        held = (s < count) & (spot < (half + 1) * per)
+        out_ref[s] = all_ref[jnp.where(held, spot * 3 + kind, none)]
         return carry
 
     lax.fori_loop(0, out_ref.shape[0], step, 0, unroll=4)
 
 
-def tile_grads(src, x_m, y_m, x_s, y_s, dgu_m, dgu_s, hid_m, hid_s, after):
+def tile_grads(here, ids, count, x_m, y_m, x_s, y_s, dgu_m, dgu_s, hid_m, hid_s, blocks):
     edge = hid_m.shape[1]
     half = len(x_m) - 1
-    slots = src.shape[0]
+    slots = ids.shape[0]
     tiles = (half + 1) * (x_m[0].shape[1] // edge) * 3 + 1
     arrays = [*x_m, *y_m, *x_s, *y_s, dgu_m, dgu_s, hid_m, hid_s]
     return pl.pallas_call(
-        functools.partial(grads_kernel, half=half, edge=edge),
+        functools.partial(grads_kernel, half=half, blocks=blocks, edge=edge),
         grid_spec=pltpu.PrefetchScalarGridSpec(
-            num_scalar_prefetch=1,
+            num_scalar_prefetch=3,
             grid=(1,),
-            in_specs=[pl.BlockSpec(a.shape, lambda *_: (0, 0)) for a in arrays]
-            + [pl.BlockSpec(memory_space=pl.ANY)],
+            in_specs=[pl.BlockSpec(a.shape, lambda *_: (0, 0)) for a in arrays],
             out_specs=pl.BlockSpec((slots, edge, edge), lambda *_: (0, 0, 0)),
             scratch_shapes=[pltpu.VMEM((tiles, edge, edge), BF)],
         ),
         out_shape=jax.ShapeDtypeStruct((slots, edge, edge), BF),
         compiler_params=pltpu.CompilerParams(vmem_limit_bytes=28 * MIB),
-        cost_estimate=pl.CostEstimate(
-            flops=800_000_000, bytes_accessed=8 * MIB, transcendentals=0
-        ),
+        cost_estimate=LITTLE,
         name="tile_gradients",
-    )(src, *arrays, after)
-
-
-def pick(table, index):
-    n = table.shape[0]
-    hit = index[:, None] == jnp.arange(n, dtype=jnp.int32)[None, :]
-    return jnp.sum(jnp.where(hit, table[None, :], 0), axis=1, dtype=jnp.int32)
+    )(here, ids, count, *arrays)
 
 
 def ring_plan(tokens, cotangent, fwd_values, fwd_ids, fwd_count, bwd_ids, bwd_count, *, n):
     half = n // 2
     ring = [2 * i for i in range(half)] + [2 * i + 1 for i in reversed(range(half))]
-    pos = [ring.index(t) for t in range(n)]
-    perm = []
+    perm, cross = [], []
     for i in range(n):
-        perm.append((ring[i] * 2, ring[(i + 1) % n] * 2))
-        perm.append((ring[i] * 2 + 1, ring[(i - 1) % n] * 2 + 1))
-    hop = lambda v: lax.ppermute(v, ("tensor", "dp"), perm)
+        ahead, behind = ring[(i + 1) % n], ring[(i - 1) % n]
+        perm += [(ring[i] * 2, ahead * 2), (ring[i] * 2 + 1, behind * 2 + 1)]
+        cross += [(ring[i] * 2 + 1, ahead * 2), (ring[i] * 2, behind * 2 + 1)]
+    axes = ("tensor", "dp")
+    hop = lambda v: lax.ppermute(v, axes, perm)
     swap = lambda v: lax.ppermute(v, "dp", [(0, 1), (1, 0)])
 
     values = fwd_values[0]
     edge = values.shape[-1]
     width = tokens.shape[1]
-    per = width // edge
-    blocks = n * per
-    slots = bwd_ids.shape[1]
-
-    x_m, y_m = [tokens], [cotangent]
-    x_s, y_s = [swap(tokens)], [swap(cotangent)]
-    for k in range(1, half + 1):
+    blocks = n * (width // edge)
+
+    shard = lax.axis_index("tensor")
+    here = jnp.stack(
+        [
+            jnp.where(shard % 2 == 1, n - 1 - shard // 2, shard // 2),
+            1 - 2 * lax.axis_index("dp"),
+        ]
+    ).astype(jnp.int32)
+    w_gu, w_d = place(here, fwd_ids[0], fwd_count, values, n, blocks)
+
+    x_m, y_m = [tokens, hop(tokens)], [cotangent, hop(cotangent)]
+    x_s, y_s = [lax.ppermute(tokens, axes, cross)], [lax.ppermute(cotangent, axes, cross)]
+    x_m[1], w_gu, w_d = lax.optimization_barrier((x_m[1], w_gu, w_d))
+    for k in range(2, half + 1):
         x_m.append(hop(x_m[-1]))
         y_m.append(hop(y_m[-1]))
         if k < half:
             x_s.append(hop(x_s[-1]))
             y_s.append(hop(y_s[-1]))
 
-    core = lax.axis_index("dp")
-    sign = 1 - 2 * core
-    here = pick(jnp.array(pos, jnp.int32), lax.axis_index("tensor")[None])[0]
-    dist_of = ((here - jnp.array(pos, jnp.int32)) * sign) % n
-    where = (dist_of[:, None] * per + jnp.arange(per, dtype=jnp.int32)[None, :]).reshape(blocks)
-    back = bwd_ids[0]
-    spot = pick(where, back % blocks)
-    held = (spot < (half + 1) * per) & (jnp.arange(slots, dtype=jnp.int32) < bwd_count[0])
-    src = jnp.where(held, spot * 3 + back // blocks, (half + 1) * per * 3)
-
-    w_gu, w_d = place(fwd_ids[0], fwd_count, where, values, y_s[0], blocks)
-    gu_at = lambda d: w_gu[d * width : (d + 1) * width]
-    d_at = lambda d: w_d[d * width : (d + 1) * width]
-    dot = functools.partial(jnp.dot, preferred_element_type=F32)
-
-    gu_m, dh_m = dot(x_m[0], gu_at(0)), dot(y_m[0], d_at(0))
-    gu_s, dh_s = dot(x_s[1], gu_at(1)), dot(y_s[1], d_at(1))
-    for d in range(1, half + 1):
-        gu_m = gu_m + dot(x_m[d], gu_at(d))
-        dh_m = dh_m + dot(y_m[d], d_at(d))
-        if 1 < d < half:
-            gu_s = gu_s + dot(x_s[d], gu_at(d))
-            dh_s = dh_s + dot(y_s[d], d_at(d))
+    gu_m, dh_m, gu_s, dh_s = forward(x_m[:half], y_m[:half], x_s, y_s, w_gu, w_d)
+    last = slice(half * width, (half + 1) * width)
+    gu_m = gu_m + jnp.dot(x_m[half], w_gu[last], preferred_element_type=F32)
+    dh_m = dh_m + jnp.dot(y_m[half], w_d[last], preferred_element_type=F32)
     gu_tm, dh_tm = gu_m + swap(gu_s), dh_m + swap(dh_s)
     gu_ts, dh_ts = gu_s + swap(gu_m), dh_s + swap(dh_m)
 
@@ -266,26 +305,25 @@
 
     run_m = [hop(term(dgu_m, half, p).astype(BF)) for p in range(2)]
     run_s = [None, None]
-    first = None
     for d in range(half + 1, n):
         for p in range(2):
             out = term(dgu_s, d, p)
             if run_s[p] is not None:
                 out = out + run_s[p].astype(F32)
             run_s[p] = hop(out.astype(BF))
-        if first is None:
-            first = run_s[0]
         for p in range(2):
             run_m[p] = hop((term(dgu_m, d, p) + run_m[p].astype(F32)).astype(BF))
+    back = [swap(v) for v in run_s]
+
+    grads = tile_grads(
+        here, bwd_ids[0], bwd_count, x_m, y_m, x_s, y_s, dgu_m, dgu_s, hid_m, hid_s, blocks
+    )
+    grads = grads + swap(grads)
+    run_m[0], run_m[1], grads = lax.optimization_barrier((run_m[0], run_m[1], grads))
     dx = [
-        (term(dgu_m, 0, p) + run_m[p].astype(F32) + swap(run_s[p]).astype(F32)).astype(BF)
+        (term(dgu_m, 0, p) + run_m[p].astype(F32) + back[p].astype(F32)).astype(BF)
         for p in range(2)
     ]
-
-    grads = tile_grads(
-        src, x_m, y_m, x_s[1:half], y_s[1:half], dgu_m, dgu_s, hid_m, hid_s, first
-    )
-    grads = grads + swap(grads)
     return jnp.concatenate(dx, axis=1), grads[None]
 
 

time: 91.3 us -> 81.1 us (0.89)
  waiting for transfers between devices: 36.2 us -> 10.8 us
  starting transfers between devices: 28.3 us -> 47.4 us
  matrix products: 8.15 us -> 4.01 us
  other arithmetic: 6.97 us -> 4.01 us
  local copies, waits for them, and re-layouts: 2.25 us -> 4.07 us
  Pallas kernels: 6.29 us -> 7.6 us
    ppermute x28, waiting for transfers between devices: 36.1 us -> 10.8 us  [the longest x26 10.8 us: ring_plan(): hop = lambda v: lax.ppermute(v, axes, perm)]
    ppermute x28, starting transfers between devices: 26.9 us -> 46.6 us  [the longest x26 44.8 us: ring_plan(): hop = lambda v: lax.ppermute(v, axes, perm)]
    dot_general x16 -> x2, matrix products: 4.59 us -> 0.45 us  [the longest x1 0.23 us: ring_plan(): gu_m = gu_m + jnp.dot(x_m[half], w_gu[last], preferred_element_type=F32)]
    add x1, other arithmetic: 0.07 us -> 3.03 us  [ring_plan(): grads = grads + swap(grads)]
    broadcast_in_dim x1 -> x0, other arithmetic: 1.98 us -> none  [ring_plan(): return (jnp.concatenate(dx, axis=1), grads[None])]
    unnamed x8 -> x14, local copies, waits for them, and re-layouts: 2.16 us -> 4.07 us
    reduce_sum x2 -> x0, other arithmetic: 1.39 us -> none  [pick(): return jnp.sum(jnp.where(hit, table[None, :], 0), axis=1, dtype=jnp.int32)]
    select_n x2 -> x0, other arithmetic: 1.33 us -> none  [the longest x1 0.67 us: ring_plan(): src = jnp.where(held, spot * 3 + back // blocks, (half + 1) * per * 3)]
  transfers between devices with their start and end apart: 37 -> 35, of which waited for: 16 -> 11; matrix products, arithmetic and copies ran while one was open for 15% -> 9% of each run, Pallas kernels for 7% -> 9%
where the time goes in v3:
time: 81.1 us; the launch traced here: 80.2 us
  starting transfers between devices  47.4 us (58%)
  waiting for transfers between devices  10.8 us (13%)
  Pallas kernels  7.6 us (9%)
  local copies, waits for them, and re-layouts  4.07 us (5%)
  other arithmetic  4.01 us (5%)
  matrix products  4.01 us (5%)
  between operations  2.31 us (3%)
    ppermute x26, starting transfers between devices, ring_plan(): hop = lambda v: lax.ppermute(v, axes, perm)  44.8 us
    ppermute x26, waiting for transfers between devices, ring_plan(): hop = lambda v: lax.ppermute(v, axes, perm)  10.8 us
    unnamed x14, local copies, waits for them, and re-layouts  4.07 us
    dot_general x16, matrix products, term(): lax.dot_general(dgu, rows, (((1,), (1,)), ((), ())), preferred_element_ty...  3.56 us
    pallas_call x1, Pallas kernels, tile_grads(): pl.pallas_call(functools.partial(grads_kernel, half=half, blocks=blocks,...  3.23 us
    pallas_call x1, Pallas kernels, place(): pl.pallas_call(functools.partial(place_kernel, n=n, blocks=blocks, edge=e...  3.23 us
    add x1, other arithmetic, ring_plan(): grads = grads + swap(grads)  3.03 us
  transfers between devices with their start and end apart: 35, of which 11 were waited for; matrix products, arithmetic and copies ran while one was open for 9% of the time, Pallas kernels for 9%

profile of v3, /device:TPU:0, one launch (start us, length us, event | category | flops | bytes accessed | tf_op | source)
XLA Modules:
  0.0 80.2 jit_solution(7382787140380342739)
XLA Ops:
  0.6 3.1 %collective-permute-start.3 = (bf16[128,1024]{1,0:T(8,128)(2,1)}, bf16[128,1024]{1,0:T(8,128)(2,1)S(1)}, u32[]{:S(2)}, u32[]{:S(2)}) collective-permute-start(bf16[128,1024]{1,0:T(8,128)(2,1)} %refs_5_.1), channel_id=1, source_target_pairs={{0,4},{1,3},{4,8},{5,1},{8,12},{9,5},{12,14},{13,9},{14,10},{15,13... | collective-permute-start | bytes 786440 | tf_op jit(solution)/shard_map/ppermute | solution.py:261
  3.7 1.6 %collective-permute-start = (bf16[128,1024]{1,0:T(8,128)(2,1)}, bf16[128,1024]{1,0:T(8,128)(2,1)S(1)}, u32[]{:S(2)}, u32[]{:S(2)}) collective-permute-start(bf16[128,1024]{1,0:T(8,128)(2,1)} %refs_0_.3), channel_id=1, source_target_pairs={{0,4},{1,3},{4,8},{5,1},{8,12},{9,5},{12,14},{13,9},{14,10},{15,13... | collective-permute-start | bytes 786440 | tf_op jit(solution)/shard_map/ppermute | solution.py:261
  5.3 0.4 collective-permute-start.9
  5.7 1.4 %collective-permute-start.6 = (bf16[128,1024]{1,0:T(8,128)(2,1)}, bf16[128,1024]{1,0:T(8,128)(2,1)S(1)}, u32[]{:S(2)}, u32[]{:S(2)}) collective-permute-start(bf16[128,1024]{1,0:T(8,128)(2,1)} %refs_0_.3), channel_id=1, source_target_pairs={{1,4},{0,3},{5,8},{4,1},{9,12},{8,5},{13,14},{12,9},{15,10},{14,13... | collective-permute-start | bytes 786440 | tf_op jit(solution)/shard_map/ppermute | solution.py:279
  7.0 1.2 %collective-permute-done.3.refs_5_.refs_6_ = bf16[128,1024]{1,0:T(8,128)(2,1)S(1)} collective-permute-done((bf16[128,1024]{1,0:T(8,128)(2,1)}, bf16[128,1024]{1,0:T(8,128)(2,1)S(1)}, u32[]{:S(2)}, u32[]{:S(2)}) %collective-permute-start.3) | collective-permute-done | bytes 262176 | tf_op jit(solution)/shard_map/ppermute | solution.py:261
  8.2 2.3 %collective-permute-start.4 = (bf16[128,1024]{1,0:T(8,128)(2,1)S(1)}, bf16[128,1024]{1,0:T(8,128)(2,1)S(1)}, u32[]{:S(2)}, u32[]{:S(2)}) collective-permute-start(bf16[128,1024]{1,0:T(8,128)(2,1)S(1)} %collective-permute-done.3.refs_5_.refs_6_), channel_id=1, source_target_pairs={{0,4},{1,3},{4,8},{5,1},{8,12},{9,5},{12,14},{13,9},{14,10},{15,13... | collective-permute-start | bytes 786440 | tf_op jit(solution)/shard_map/ppermute | solution.py:261
  11.2 1.5 %copy-done = bf16[1,56,128,128]{3,2,1,0:T(8,128)(2,1)S(1)} copy-done((bf16[1,56,128,128]{3,2,1,0:T(8,128)(2,1)S(1)}, bf16[1,56,128,128]{3,2,1,0:T(8,128)(2,1)}, u32[]{:S(2)}) %copy-start) | copy-done | bytes 1835032
  12.7 0.7 copy-done.6
  13.3 3.2 %place_weights.1 = (bf16[8192,256]{1,0:T(8,128)(2,1)S(1)}, bf16[8192,128]{1,0:T(8,128)(2,1)S(1)}) custom-call(s32[2]{0:T(128)S(1)} %pad_add_fusion.here_ref, s32[56]{0:T(128)S(1)} %bitcast.14, s32[1]{0:T(128)S(6)} %copy.11.cnt_ref, bf16[56,128,128]{2,1,0:T(8,128)(2,1)S(1)} %bitcast.12), custom_call_target="tpu_custom_call" | custom-call | flops 1 | bytes 1 | tf_op jit(solution)/shard_map/place_weights/pallas_call | solution.py:129
  16.6 2.7 %collective-permute-start.1 = (bf16[128,1024]{1,0:T(8,128)(2,1)S(1)}, bf16[128,1024]{1,0:T(8,128)(2,1)S(1)}, u32[]{:S(2)}, u32[]{:S(2)}) collective-permute-start(bf16[128,1024]{1,0:T(8,128)(2,1)S(1)} %collective-permute-done.refs_1_), channel_id=1, source_target_pairs={{0,4},{1,3},{4,8},{5,1},{8,12},{9,5},{12,14},{13,9},{14,10},{15,13... | collective-permute-start | bytes 786440 | tf_op jit(solution)/shard_map/ppermute | solution.py:261
  19.3 2.0 %collective-permute-start.10 = (bf16[128,1024]{1,0:T(8,128)(2,1)S(1)}, bf16[128,1024]{1,0:T(8,128)(2,1)S(1)}, u32[]{:S(2)}, u32[]{:S(2)}) collective-permute-start(bf16[128,1024]{1,0:T(8,128)(2,1)S(1)} %collective-permute-done.9.refs_11_.refs_13_), channel_id=1, source_target_pairs={{0,4},{1,3},{4,8},{5,1},{8,12},{9,5},{12,14},{13,9},{14,10},{15,13... | collective-permute-start | bytes 786440 | tf_op jit(solution)/shard_map/ppermute | solution.py:261
  21.3 0.9 %collective-permute-start.7 = (bf16[128,1024]{1,0:T(8,128)(2,1)S(1)}, bf16[128,1024]{1,0:T(8,128)(2,1)S(1)}, u32[]{:S(2)}, u32[]{:S(2)}) collective-permute-start(bf16[128,1024]{1,0:T(8,128)(2,1)S(1)} %collective-permute-done.6.refs_8_.refs_10_), channel_id=1, source_target_pairs={{0,4},{1,3},{4,8},{5,1},{8,12},{9,5},{12,14},{13,9},{14,10},{15,13... | collective-permute-start | bytes 786440 | tf_op jit(solution)/shard_map/ppermute | solution.py:261
  22.2 0.9 %collective-permute-start.5 = (bf16[128,1024]{1,0:T(8,128)(2,1)S(1)}, bf16[128,1024]{1,0:T(8,128)(2,1)S(1)}, u32[]{:S(2)}, u32[]{:S(2)}) collective-permute-start(bf16[128,1024]{1,0:T(8,128)(2,1)S(1)} %collective-permute-done.4.refs_6_.refs_7_), channel_id=1, source_target_pairs={{0,4},{1,3},{4,8},{5,1},{8,12},{9,5},{12,14},{13,9},{14,10},{15,13... | collective-permute-start | bytes 786440 | tf_op jit(solution)/shard_map/ppermute | solution.py:261
  23.2 2.5 %collective-permute-start.2 = (bf16[128,1024]{1,0:T(8,128)(2,1)S(1)}, bf16[128,1024]{1,0:T(8,128)(2,1)S(1)}, u32[]{:S(2)}, u32[]{:S(2)}) collective-permute-start(bf16[128,1024]{1,0:T(8,128)(2,1)S(1)} %collective-permute-done.1.refs_2_), channel_id=1, source_target_pairs={{0,4},{1,3},{4,8},{5,1},{8,12},{9,5},{12,14},{13,9},{14,10},{15,13... | collective-permute-start | bytes 786440 | tf_op jit(solution)/shard_map/ppermute | solution.py:261
  25.7 0.3 collective-permute-done.10.refs_12_.refs_14_
  26.0 2.5 %collective-permute-start.11 = (bf16[128,1024]{1,0:T(8,128)(2,1)S(1)}, bf16[128,1024]{1,0:T(8,128)(2,1)S(1)}, u32[]{:S(2)}, u32[]{:S(2)}) collective-permute-start(bf16[128,1024]{1,0:T(8,128)(2,1)S(1)} %collective-permute-done.10.refs_12_.refs_14_), channel_id=1, source_target_pairs={{0,4},{1,3},{4,8},{5,1},{8,12},{9,5},{12,14},{13,9},{14,10},{15,13... | collective-permute-start | bytes 786440 | tf_op jit(solution)/shard_map/ppermute | solution.py:261
  28.5 0.3 collective-permute-done.7.refs_9_.refs_11_
  28.8 2.5 %collective-permute-start.8 = (bf16[128,1024]{1,0:T(8,128)(2,1)S(1)}, bf16[128,1024]{1,0:T(8,128)(2,1)S(1)}, u32[]{:S(2)}, u32[]{:S(2)}) collective-permute-start(bf16[128,1024]{1,0:T(8,128)(2,1)S(1)} %collective-permute-done.7.refs_9_.refs_11_), channel_id=1, source_target_pairs={{0,4},{1,3},{4,8},{5,1},{8,12},{9,5},{12,14},{13,9},{14,10},{15,13... | collective-permute-start | bytes 786440 | tf_op jit(solution)/shard_map/ppermute | solution.py:261
  31.3 0.3 collective-permute-done.5.refs_7_.refs_8_
  31.6 2.5 %collective-permute-start.12 = (bf16[128,1024]{1,0:T(8,128)(2,1)S(1)}, bf16[128,1024]{1,0:T(8,128)(2,1)S(1)}, u32[]{:S(2)}, u32[]{:S(2)}) collective-permute-start(bf16[128,1024]{1,0:T(8,128)(2,1)S(1)} %collective-permute-done.5.refs_7_.refs_8_), channel_id=1, source_target_pairs={{0,4},{1,3},{4,8},{5,1},{8,12},{9,5},{12,14},{13,9},{14,10},{15,13... | collective-permute-start | bytes 786440 | tf_op jit(solution)/shard_map/ppermute | solution.py:261
  34.1 0.3 collective-permute-done.2.refs_3_
  34.4 2.5 %collective-permute-start.14 = (bf16[128,1024]{1,0:T(8,128)(2,1)S(1)}, bf16[128,1024]{1,0:T(8,128)(2,1)S(1)}, u32[]{:S(2)}, u32[]{:S(2)}) collective-permute-start(bf16[128,1024]{1,0:T(8,128)(2,1)S(1)} %collective-permute-done.2.refs_3_), channel_id=1, source_target_pairs={{0,4},{1,3},{4,8},{5,1},{8,12},{9,5},{12,14},{13,9},{14,10},{15,13... | collective-permute-start | bytes 786440 | tf_op jit(solution)/shard_map/ppermute | solution.py:261
  37.6 2.5 %collective-permute-done.8.refs_10_.refs_12_ = bf16[128,1024]{1,0:T(8,128)(2,1)S(1)} collective-permute-done((bf16[128,1024]{1,0:T(8,128)(2,1)S(1)}, bf16[128,1024]{1,0:T(8,128)(2,1)S(1)}, u32[]{:S(2)}, u32[]{:S(2)}) %collective-permute-start.8) | collective-permute-done | bytes 262176 | tf_op jit(solution)/shard_map/ppermute | solution.py:261
  40.1 0.9 %copy-done.1 = bf16[128,1024]{1,0:T(8,128)(2,1)S(1)} copy-done((bf16[128,1024]{1,0:T(8,128)(2,1)S(1)}, bf16[128,1024]{1,0:T(8,128)(2,1)}, u32[]{:S(2)}) %copy-start.1) | copy-done | bytes 262168
  41.0 0.9 %copy-done.3 = bf16[128,1024]{1,0:T(8,128)(2,1)S(1)} copy-done((bf16[128,1024]{1,0:T(8,128)(2,1)S(1)}, bf16[128,1024]{1,0:T(8,128)(2,1)}, u32[]{:S(2)}) %copy-start.3) | copy-done | bytes 262168
  42.0 1.1 %forward_terms.1 = (f32[128,256]{1,0:T(8,128)S(1)}, f32[128,128]{1,0:T(8,128)S(1)}, f32[128,256]{1,0:T(8,128)S(1)}, f32[128,128]{1,0:T(8,128)S(1)}) custom-call(bf16[128,1024]{1,0:T(8,128)(2,1)S(1)} %copy-done.1, bf16[128,1024]{1,0:T(8,128)(2,1)S(1)} %collective-permute-done.refs_1_, bf16[128,1024]{1,0:T(8,128)(2,1)S(1)} %collective-permute-done.1.refs_2_, ...), custom_call_target="tpu_custom_call" | custom-call | flops 1 | bytes 1 | tf_op jit(solution)/shard_map/forward_terms/pallas_call | solution.py:177
  43.2 0.5 collective-permute-start.13
  43.7 0.2 fusion.10
  44.1 1.6 %collective-permute-done.14.refs_4_ = bf16[128,1024]{1,0:T(8,128)(2,1)S(1)} collective-permute-done((bf16[128,1024]{1,0:T(8,128)(2,1)S(1)}, bf16[128,1024]{1,0:T(8,128)(2,1)S(1)}, u32[]{:S(2)}, u32[]{:S(2)}) %collective-permute-start.14) | collective-permute-done | bytes 262176 | tf_op jit(solution)/shard_map/ppermute | solution.py:261
  45.7 0.2 fusion.11
  46.1 0.2 convolution_convert_fusion.2
  46.3 2.5 %collective-permute-start.20 = (bf16[128,512]{1,0:T(8,128)(2,1)S(1)}, bf16[128,512]{1,0:T(8,128)(2,1)S(1)}, u32[]{:S(2)}, u32[]{:S(2)}) collective-permute-start(bf16[128,512]{1,0:T(8,128)(2,1)S(1)} %convolution_convert_fusion.2), channel_id=1, source_target_pairs={{0,4},{1,3},{4,8},{5,1},{8,12},{9,5},{12,14},{13,9},{14,10},{15,13... | collective-permute-start | bytes 393224 | tf_op jit(solution)/shard_map/ppermute | solution.py:261
  49.0 3.2 %tile_gradients.1 = bf16[96,128,128]{2,1,0:T(8,128)(2,1)S(1)} custom-call(s32[2]{0:T(128)S(1)} %pad_add_fusion.here_ref, s32[96]{0:T(128)S(1)} %bitcast.13, s32[1]{0:T(128)S(6)} %copy.12.cnt_ref, bf16[128,1024]{1,0:T(8,128)(2,1)S(1)} %copy-done.2, bf16[128,1024]{1,0:T(8,128)(2,1)S(1)} %collective-permute-done.refs_1_, ...), custom_call_target="tpu_custom_call" | custom-call | flops 1 | bytes 1 | tf_op jit(solution)/shard_map/tile_gradients/pallas_call | solution.py:236
  52.4 0.2 convolution_convert_fusion.3
  52.6 2.0 %collective-permute-start.16 = (bf16[128,512]{1,0:T(8,128)(2,1)S(1)}, bf16[128,512]{1,0:T(8,128)(2,1)S(1)}, u32[]{:S(2)}, u32[]{:S(2)}) collective-permute-start(bf16[128,512]{1,0:T(8,128)(2,1)S(1)} %convolution_convert_fusion.3), channel_id=1, source_target_pairs={{0,4},{1,3},{4,8},{5,1},{8,12},{9,5},{12,14},{13,9},{14,10},{15,13... | collective-permute-start | bytes 393224 | tf_op jit(solution)/shard_map/ppermute | solution.py:261
  54.6 0.2 convolution_convert_fusion.1
  54.8 1.1 %collective-permute-start.27 = (bf16[128,512]{1,0:T(8,128)(2,1)S(1)}, bf16[128,512]{1,0:T(8,128)(2,1)S(1)}, u32[]{:S(2)}, u32[]{:S(2)}) collective-permute-start(bf16[128,512]{1,0:T(8,128)(2,1)S(1)} %convolution_convert_fusion.1), channel_id=1, source_target_pairs={{0,4},{1,3},{4,8},{5,1},{8,12},{9,5},{12,14},{13,9},{14,10},{15,13... | collective-permute-start | bytes 393224 | tf_op jit(solution)/shard_map/ppermute | solution.py:261
  56.0 0.2 fusion.5
  56.2 1.2 %collective-permute-start.21 = (bf16[128,512]{1,0:T(8,128)(2,1)S(1)}, bf16[128,512]{1,0:T(8,128)(2,1)S(1)}, u32[]{:S(2)}, u32[]{:S(2)}) collective-permute-start(bf16[128,512]{1,0:T(8,128)(2,1)S(1)} %fusion.5), channel_id=1, source_target_pairs={{0,4},{1,3},{4,8},{5,1},{8,12},{9,5},{12,14},{13,9},{14,10},{15,13... | collective-permute-start | bytes 393224 | tf_op jit(solution)/shard_map/ppermute | solution.py:261
  57.6 0.2 fusion.2
  57.8 2.0 %collective-permute-start.17 = (bf16[128,512]{1,0:T(8,128)(2,1)S(1)}, bf16[128,512]{1,0:T(8,128)(2,1)S(1)}, u32[]{:S(2)}, u32[]{:S(2)}) collective-permute-start(bf16[128,512]{1,0:T(8,128)(2,1)S(1)} %fusion.2), channel_id=1, source_target_pairs={{0,4},{1,3},{4,8},{5,1},{8,12},{9,5},{12,14},{13,9},{14,10},{15,13... | collective-permute-start | bytes 393224 | tf_op jit(solution)/shard_map/ppermute | solution.py:261
  59.9 0.2 convolution_convert_fusion
  60.1 1.1 %collective-permute-start.31 = (bf16[128,512]{1,0:T(8,128)(2,1)S(1)}, bf16[128,512]{1,0:T(8,128)(2,1)S(1)}, u32[]{:S(2)}, u32[]{:S(2)}) collective-permute-start(bf16[128,512]{1,0:T(8,128)(2,1)S(1)} %convolution_convert_fusion), channel_id=1, source_target_pairs={{0,4},{1,3},{4,8},{5,1},{8,12},{9,5},{12,14},{13,9},{14,10},{15,13... | collective-permute-start | bytes 393224 | tf_op jit(solution)/shard_map/ppermute | solution.py:261
  61.2 0.2 fusion.7
  61.5 1.2 %collective-permute-start.28 = (bf16[128,512]{1,0:T(8,128)(2,1)S(1)}, bf16[128,512]{1,0:T(8,128)(2,1)S(1)}, u32[]{:S(2)}, u32[]{:S(2)}) collective-permute-start(bf16[128,512]{1,0:T(8,128)(2,1)S(1)} %fusion.7), channel_id=1, source_target_pairs={{0,4},{1,3},{4,8},{5,1},{8,12},{9,5},{12,14},{13,9},{14,10},{15,13... | collective-permute-start | bytes 393224 | tf_op jit(solution)/shard_map/ppermute | solution.py:261
  62.7 0.2 fusion.4
  62.9 0.9 %collective-permute-start.22 = (bf16[128,512]{1,0:T(8,128)(2,1)S(1)}, bf16[128,512]{1,0:T(8,128)(2,1)S(1)}, u32[]{:S(2)}, u32[]{:S(2)}) collective-permute-start(bf16[128,512]{1,0:T(8,128)(2,1)S(1)} %fusion.4), channel_id=1, source_target_pairs={{0,4},{1,3},{4,8},{5,1},{8,12},{9,5},{12,14},{13,9},{14,10},{15,13... | collective-permute-start | bytes 393224 | tf_op jit(solution)/shard_map/ppermute | solution.py:261
  63.8 0.2 fusion.1
  64.0 1.1 %collective-permute-start.18 = (bf16[128,512]{1,0:T(8,128)(2,1)S(1)}, bf16[128,512]{1,0:T(8,128)(2,1)S(1)}, u32[]{:S(2)}, u32[]{:S(2)}) collective-permute-start(bf16[128,512]{1,0:T(8,128)(2,1)S(1)} %fusion.1), channel_id=1, source_target_pairs={{0,4},{1,3},{4,8},{5,1},{8,12},{9,5},{12,14},{13,9},{14,10},{15,13... | collective-permute-start | bytes 393224 | tf_op jit(solution)/shard_map/ppermute | solution.py:261
  65.1 0.2 fusion.9
  65.4 1.2 %collective-permute-start.32 = (bf16[128,512]{1,0:T(8,128)(2,1)S(1)}, bf16[128,512]{1,0:T(8,128)(2,1)S(1)}, u32[]{:S(2)}, u32[]{:S(2)}) collective-permute-start(bf16[128,512]{1,0:T(8,128)(2,1)S(1)} %fusion.9), channel_id=1, source_target_pairs={{0,4},{1,3},{4,8},{5,1},{8,12},{9,5},{12,14},{13,9},{14,10},{15,13... | collective-permute-start | bytes 393224 | tf_op jit(solution)/shard_map/ppermute | solution.py:261
  66.5 0.2 fusion.6
  66.8 1.2 %collective-permute-start.29 = (bf16[128,512]{1,0:T(8,128)(2,1)S(1)}, bf16[128,512]{1,0:T(8,128)(2,1)S(1)}, u32[]{:S(2)}, u32[]{:S(2)}) collective-permute-start(bf16[128,512]{1,0:T(8,128)(2,1)S(1)} %fusion.6), channel_id=1, source_target_pairs={{0,4},{1,3},{4,8},{5,1},{8,12},{9,5},{12,14},{13,9},{14,10},{15,13... | collective-permute-start | bytes 393224 | tf_op jit(solution)/shard_map/ppermute | solution.py:261
  68.2 1.2 %collective-permute-start.23 = (bf16[128,512]{1,0:T(8,128)(2,1)S(1)}, bf16[128,512]{1,0:T(8,128)(2,1)S(1)}, u32[]{:S(2)}, u32[]{:S(2)}) collective-permute-start(bf16[128,512]{1,0:T(8,128)(2,1)S(1)} %fusion.3), channel_id=1, source_target_pairs={{0,4},{1,3},{4,8},{5,1},{8,12},{9,5},{12,14},{13,9},{14,10},{15,13... | collective-permute-start | bytes 393224 | tf_op jit(solution)/shard_map/ppermute | solution.py:261
  69.3 1.4 %collective-permute-done.32 = bf16[128,512]{1,0:T(8,128)(2,1)S(1)} collective-permute-done((bf16[128,512]{1,0:T(8,128)(2,1)S(1)}, bf16[128,512]{1,0:T(8,128)(2,1)S(1)}, u32[]{:S(2)}, u32[]{:S(2)}) %collective-permute-start.32) | collective-permute-done | bytes 131104 | tf_op jit(solution)/shard_map/ppermute | solution.py:261
  70.7 0.2 fusion.8
  71.0 1.2 %collective-permute-start.33 = (bf16[128,512]{1,0:T(8,128)(2,1)S(1)}, bf16[128,512]{1,0:T(8,128)(2,1)S(1)}, u32[]{:S(2)}, u32[]{:S(2)}) collective-permute-start(bf16[128,512]{1,0:T(8,128)(2,1)S(1)} %fusion.8), channel_id=1, source_target_pairs={{0,4},{1,3},{4,8},{5,1},{8,12},{9,5},{12,14},{13,9},{14,10},{15,13... | collective-permute-start | bytes 393224 | tf_op jit(solution)/shard_map/ppermute | solution.py:261
  72.1 0.2 fusion
  72.4 1.2 %collective-permute-start.19 = (bf16[128,512]{1,0:T(8,128)(2,1)S(1)}, bf16[128,512]{1,0:T(8,128)(2,1)S(1)}, u32[]{:S(2)}, u32[]{:S(2)}) collective-permute-start(bf16[128,512]{1,0:T(8,128)(2,1)S(1)} %fusion), channel_id=1, source_target_pairs={{0,4},{1,3},{4,8},{5,1},{8,12},{9,5},{12,14},{13,9},{14,10},{15,13... | collective-permute-start | bytes 393224 | tf_op jit(solution)/shard_map/ppermute | solution.py:261
  73.5 2.5 %collective-permute-done.33 = bf16[128,512]{1,0:T(8,128)(2,1)S(1)} collective-permute-done((bf16[128,512]{1,0:T(8,128)(2,1)S(1)}, bf16[128,512]{1,0:T(8,128)(2,1)S(1)}, u32[]{:S(2)}, u32[]{:S(2)}) %collective-permute-start.33) | collective-permute-done | bytes 131104 | tf_op jit(solution)/shard_map/ppermute | solution.py:261
  76.0 3.0 %add.97 = bf16[96,128,128]{2,1,0:T(8,128)(2,1)} add(bf16[96,128,128]{2,1,0:T(8,128)(2,1)S(1)} %tile_gradients.1, bf16[96,128,128]{2,1,0:T(8,128)(2,1)S(1)} %collective-permute-done.26) | non-fusion elementwise | flops 1572864 | bytes 9437184 | tf_op jit(solution)/shard_map/add | solution.py:321
  79.0 0.2 add_convert_fusion.1
  79.3 0.2 add_convert_fusion
  79.5 0.7 pad_maximum_fusion
  (50 shorter events, 1.3 us)
Async XLA Ops:
  0.6 7.6 %collective-permute-start.3 = (bf16[128,1024]{1,0:T(8,128)(2,1)}, bf16[128,1024]{1,0:T(8,128)(2,1)S(1)}, u32[]{:S(2)}, u32[]{:S(2)}) collective-permute-start(bf16[128,1024]{1,0:T(8,128)(2,1)} %refs_5_.1), channel_id=1, source_target_pairs={{0,4},{1,3},{4,8},{5,1},{8,12},{9,5},{12,14},{13,9},{14,10},{15,13... | collective-permute-start | bytes 786440 | tf_op jit(solution)/shard_map/ppermute | solution.py:261
  3.7 12.9 %collective-permute-start = (bf16[128,1024]{1,0:T(8,128)(2,1)}, bf16[128,1024]{1,0:T(8,128)(2,1)S(1)}, u32[]{:S(2)}, u32[]{:S(2)}) collective-permute-start(bf16[128,1024]{1,0:T(8,128)(2,1)} %refs_0_.3), channel_id=1, source_target_pairs={{0,4},{1,3},{4,8},{5,1},{8,12},{9,5},{12,14},{13,9},{14,10},{15,13... | collective-permute-start | bytes 786440 | tf_op jit(solution)/shard_map/ppermute | solution.py:261
  5.3 14.0 %collective-permute-start.9 = (bf16[128,1024]{1,0:T(8,128)(2,1)}, bf16[128,1024]{1,0:T(8,128)(2,1)S(1)}, u32[]{:S(2)}, u32[]{:S(2)}) collective-permute-start(bf16[128,1024]{1,0:T(8,128)(2,1)} %refs_5_.1), channel_id=1, source_target_pairs={{1,4},{0,3},{5,8},{4,1},{9,12},{8,5},{13,14},{12,9},{15,10},{14,13... | collective-permute-start | bytes 786440 | tf_op jit(solution)/shard_map/ppermute | solution.py:279
  5.7 15.6 %collective-permute-start.6 = (bf16[128,1024]{1,0:T(8,128)(2,1)}, bf16[128,1024]{1,0:T(8,128)(2,1)S(1)}, u32[]{:S(2)}, u32[]{:S(2)}) collective-permute-start(bf16[128,1024]{1,0:T(8,128)(2,1)} %refs_0_.3), channel_id=1, source_target_pairs={{1,4},{0,3},{5,8},{4,1},{9,12},{8,5},{13,14},{12,9},{15,10},{14,13... | collective-permute-start | bytes 786440 | tf_op jit(solution)/shard_map/ppermute | solution.py:279
  8.2 14.0 %collective-permute-start.4 = (bf16[128,1024]{1,0:T(8,128)(2,1)S(1)}, bf16[128,1024]{1,0:T(8,128)(2,1)S(1)}, u32[]{:S(2)}, u32[]{:S(2)}) collective-permute-start(bf16[128,1024]{1,0:T(8,128)(2,1)S(1)} %collective-permute-done.3.refs_5_.refs_6_), channel_id=1, source_target_pairs={{0,4},{1,3},{4,8},{5,1},{8,12},{9,5},{12,14},{13,9},{14,10},{15,13... | collective-permute-start | bytes 786440 | tf_op jit(solution)/shard_map/ppermute | solution.py:261
  11.2 1.5 %copy-start = (bf16[1,56,128,128]{3,2,1,0:T(8,128)(2,1)S(1)}, bf16[1,56,128,128]{3,2,1,0:T(8,128)(2,1)}, u32[]{:S(2)}) copy-start(bf16[1,56,128,128]{3,2,1,0:T(8,128)(2,1)} %param.9) | copy-start | bytes 5505028
  12.7 0.7 copy-start.6
  16.6 6.6 %collective-permute-start.1 = (bf16[128,1024]{1,0:T(8,128)(2,1)S(1)}, bf16[128,1024]{1,0:T(8,128)(2,1)S(1)}, u32[]{:S(2)}, u32[]{:S(2)}) collective-permute-start(bf16[128,1024]{1,0:T(8,128)(2,1)S(1)} %collective-permute-done.refs_1_), channel_id=1, source_target_pairs={{0,4},{1,3},{4,8},{5,1},{8,12},{9,5},{12,14},{13,9},{14,10},{15,13... | collective-permute-start | bytes 786440 | tf_op jit(solution)/shard_map/ppermute | solution.py:261
  19.3 6.7 %collective-permute-start.10 = (bf16[128,1024]{1,0:T(8,128)(2,1)S(1)}, bf16[128,1024]{1,0:T(8,128)(2,1)S(1)}, u32[]{:S(2)}, u32[]{:S(2)}) collective-permute-start(bf16[128,1024]{1,0:T(8,128)(2,1)S(1)} %collective-permute-done.9.refs_11_.refs_13_), channel_id=1, source_target_pairs={{0,4},{1,3},{4,8},{5,1},{8,12},{9,5},{12,14},{13,9},{14,10},{15,13... | collective-permute-start | bytes 786440 | tf_op jit(solution)/shard_map/ppermute | solution.py:261
  21.3 7.5 %collective-permute-start.7 = (bf16[128,1024]{1,0:T(8,128)(2,1)S(1)}, bf16[128,1024]{1,0:T(8,128)(2,1)S(1)}, u32[]{:S(2)}, u32[]{:S(2)}) collective-permute-start(bf16[128,1024]{1,0:T(8,128)(2,1)S(1)} %collective-permute-done.6.refs_8_.refs_10_), channel_id=1, source_target_pairs={{0,4},{1,3},{4,8},{5,1},{8,12},{9,5},{12,14},{13,9},{14,10},{15,13... | collective-permute-start | bytes 786440 | tf_op jit(solution)/shard_map/ppermute | solution.py:261
  22.2 9.5 %collective-permute-start.5 = (bf16[128,1024]{1,0:T(8,128)(2,1)S(1)}, bf16[128,1024]{1,0:T(8,128)(2,1)S(1)}, u32[]{:S(2)}, u32[]{:S(2)}) collective-permute-start(bf16[128,1024]{1,0:T(8,128)(2,1)S(1)} %collective-permute-done.4.refs_6_.refs_7_), channel_id=1, source_target_pairs={{0,4},{1,3},{4,8},{5,1},{8,12},{9,5},{12,14},{13,9},{14,10},{15,13... | collective-permute-start | bytes 786440 | tf_op jit(solution)/shard_map/ppermute | solution.py:261
  23.2 11.2 %collective-permute-start.2 = (bf16[128,1024]{1,0:T(8,128)(2,1)S(1)}, bf16[128,1024]{1,0:T(8,128)(2,1)S(1)}, u32[]{:S(2)}, u32[]{:S(2)}) collective-permute-start(bf16[128,1024]{1,0:T(8,128)(2,1)S(1)} %collective-permute-done.1.refs_2_), channel_id=1, source_target_pairs={{0,4},{1,3},{4,8},{5,1},{8,12},{9,5},{12,14},{13,9},{14,10},{15,13... | collective-permute-start | bytes 786440 | tf_op jit(solution)/shard_map/ppermute | solution.py:261
  26.0 11.6 %collective-permute-start.11 = (bf16[128,1024]{1,0:T(8,128)(2,1)S(1)}, bf16[128,1024]{1,0:T(8,128)(2,1)S(1)}, u32[]{:S(2)}, u32[]{:S(2)}) collective-permute-start(bf16[128,1024]{1,0:T(8,128)(2,1)S(1)} %collective-permute-done.10.refs_12_.refs_14_), channel_id=1, source_target_pairs={{0,4},{1,3},{4,8},{5,1},{8,12},{9,5},{12,14},{13,9},{14,10},{15,13... | collective-permute-start | bytes 786440 | tf_op jit(solution)/shard_map/ppermute | solution.py:261
  28.8 11.2 %collective-permute-start.8 = (bf16[128,1024]{1,0:T(8,128)(2,1)S(1)}, bf16[128,1024]{1,0:T(8,128)(2,1)S(1)}, u32[]{:S(2)}, u32[]{:S(2)}) collective-permute-start(bf16[128,1024]{1,0:T(8,128)(2,1)S(1)} %collective-permute-done.7.refs_9_.refs_11_), channel_id=1, source_target_pairs={{0,4},{1,3},{4,8},{5,1},{8,12},{9,5},{12,14},{13,9},{14,10},{15,13... | collective-permute-start | bytes 786440 | tf_op jit(solution)/shard_map/ppermute | solution.py:261
  31.6 12.1 %collective-permute-start.12 = (bf16[128,1024]{1,0:T(8,128)(2,1)S(1)}, bf16[128,1024]{1,0:T(8,128)(2,1)S(1)}, u32[]{:S(2)}, u32[]{:S(2)}) collective-permute-start(bf16[128,1024]{1,0:T(8,128)(2,1)S(1)} %collective-permute-done.5.refs_7_.refs_8_), channel_id=1, source_target_pairs={{0,4},{1,3},{4,8},{5,1},{8,12},{9,5},{12,14},{13,9},{14,10},{15,13... | collective-permute-start | bytes 786440 | tf_op jit(solution)/shard_map/ppermute | solution.py:261
  34.4 11.2 %collective-permute-start.14 = (bf16[128,1024]{1,0:T(8,128)(2,1)S(1)}, bf16[128,1024]{1,0:T(8,128)(2,1)S(1)}, u32[]{:S(2)}, u32[]{:S(2)}) collective-permute-start(bf16[128,1024]{1,0:T(8,128)(2,1)S(1)} %collective-permute-done.2.refs_3_), channel_id=1, source_target_pairs={{0,4},{1,3},{4,8},{5,1},{8,12},{9,5},{12,14},{13,9},{14,10},{15,13... | collective-permute-start | bytes 786440 | tf_op jit(solution)/shard_map/ppermute | solution.py:261
  36.9 12.1 %copy-start.5 = (s32[1,96]{1,0:T(1,128)S(1)}, s32[1,96]{1,0:T(1,128)}, u32[]{:S(2)}) copy-start(s32[1,96]{1,0:T(1,128)} %param.12) | copy-start | bytes 1156
  40.1 0.9 %copy-start.1 = (bf16[128,1024]{1,0:T(8,128)(2,1)S(1)}, bf16[128,1024]{1,0:T(8,128)(2,1)}, u32[]{:S(2)}) copy-start(bf16[128,1024]{1,0:T(8,128)(2,1)} %refs_0_.3) | copy-start | bytes 786436
  41.0 0.9 %copy-start.3 = (bf16[128,1024]{1,0:T(8,128)(2,1)S(1)}, bf16[128,1024]{1,0:T(8,128)(2,1)}, u32[]{:S(2)}) copy-start(bf16[128,1024]{1,0:T(8,128)(2,1)} %refs_5_.1) | copy-start | bytes 786436
  43.1 5.9 %copy-start.2 = (bf16[128,1024]{1,0:T(8,128)(2,1)S(1)}, bf16[128,1024]{1,0:T(8,128)(2,1)}, u32[]{:S(2)}) copy-start(bf16[128,1024]{1,0:T(8,128)(2,1)} %refs_0_.3) | copy-start | bytes 786436
  43.1 5.9 %copy-start.4 = (bf16[128,1024]{1,0:T(8,128)(2,1)S(1)}, bf16[128,1024]{1,0:T(8,128)(2,1)}, u32[]{:S(2)}) copy-start(bf16[128,1024]{1,0:T(8,128)(2,1)} %refs_5_.1) | copy-start | bytes 786436
  43.1 2.8 %collective-permute-start.15 = (f32[128,256]{1,0:T(8,128)S(1)}, f32[128,256]{1,0:T(8,128)S(1)}, u32[]{:S(2)}, u32[]{:S(2)}) collective-permute-start(f32[128,256]{1,0:T(8,128)S(1)} %get-tuple-element.22), channel_id=1, source_target_pairs={{0,1},{1,0},{2,3},{3,2},{4,5},{5,4},{6,7},{7,6},{8,9},{9,8},{10,11... | collective-permute-start | bytes 393224 | tf_op jit(solution)/shard_map/ppermute | solution.py:262
  43.2 2.8 %collective-permute-start.13 = (f32[128,128]{1,0:T(8,128)S(1)}, f32[128,128]{1,0:T(8,128)S(1)}, u32[]{:S(2)}, u32[]{:S(2)}) collective-permute-start(f32[128,128]{1,0:T(8,128)S(1)} %get-tuple-element.20), channel_id=1, source_target_pairs={{0,1},{1,0},{2,3},{3,2},{4,5},{5,4},{6,7},{7,6},{8,9},{9,8},{10,11... | collective-permute-start | bytes 196616 | tf_op jit(solution)/shard_map/ppermute | solution.py:262
  43.9 5.0 %collective-permute-start.24 = (f32[128,128]{1,0:T(8,128)S(1)}, f32[128,128]{1,0:T(8,128)S(1)}, u32[]{:S(2)}, u32[]{:S(2)}) collective-permute-start(f32[128,128]{1,0:T(8,128)S(1)} %fusion.10), channel_id=1, source_target_pairs={{0,1},{1,0},{2,3},{3,2},{4,5},{5,4},{6,7},{7,6},{8,9},{9,8},{10,11... | collective-permute-start | bytes 196616 | tf_op jit(solution)/shard_map/ppermute | solution.py:262
  46.0 2.9 %collective-permute-start.25 = (f32[128,256]{1,0:T(8,128)S(1)}, f32[128,256]{1,0:T(8,128)S(1)}, u32[]{:S(2)}, u32[]{:S(2)}) collective-permute-start(f32[128,256]{1,0:T(8,128)S(1)} %get-tuple-element.27), channel_id=1, source_target_pairs={{0,1},{1,0},{2,3},{3,2},{4,5},{5,4},{6,7},{7,6},{8,9},{9,8},{10,11... | collective-permute-start | bytes 393224 | tf_op jit(solution)/shard_map/ppermute | solution.py:262
  46.3 9.6 %collective-permute-start.20 = (bf16[128,512]{1,0:T(8,128)(2,1)S(1)}, bf16[128,512]{1,0:T(8,128)(2,1)S(1)}, u32[]{:S(2)}, u32[]{:S(2)}) collective-permute-start(bf16[128,512]{1,0:T(8,128)(2,1)S(1)} %convolution_convert_fusion.2), channel_id=1, source_target_pairs={{0,4},{1,3},{4,8},{5,1},{8,12},{9,5},{12,14},{13,9},{14,10},{15,13... | collective-permute-start | bytes 393224 | tf_op jit(solution)/shard_map/ppermute | solution.py:261
  52.3 23.7 %collective-permute-start.26 = (bf16[96,128,128]{2,1,0:T(8,128)(2,1)S(1)}, bf16[96,128,128]{2,1,0:T(8,128)(2,1)S(1)}, u32[]{:S(2)}, u32[]{:S(2)}) collective-permute-start(bf16[96,128,128]{2,1,0:T(8,128)(2,1)S(1)} %tile_gradients.1), channel_id=1, source_target_pairs={{0,1},{1,0},{2,3},{3,2},{4,5},{5,4},{6,7},{7,6},{8,9},{9,8},{10,11... | collective-permute-start | bytes 9437192 | tf_op jit(solution)/shard_map/ppermute | solution.py:262
  52.6 5.0 %collective-permute-start.16 = (bf16[128,512]{1,0:T(8,128)(2,1)S(1)}, bf16[128,512]{1,0:T(8,128)(2,1)S(1)}, u32[]{:S(2)}, u32[]{:S(2)}) collective-permute-start(bf16[128,512]{1,0:T(8,128)(2,1)S(1)} %convolution_convert_fusion.3), channel_id=1, source_target_pairs={{0,4},{1,3},{4,8},{5,1},{8,12},{9,5},{12,14},{13,9},{14,10},{15,13... | collective-permute-start | bytes 393224 | tf_op jit(solution)/shard_map/ppermute | solution.py:261
  54.8 6.4 %collective-permute-start.27 = (bf16[128,512]{1,0:T(8,128)(2,1)S(1)}, bf16[128,512]{1,0:T(8,128)(2,1)S(1)}, u32[]{:S(2)}, u32[]{:S(2)}) collective-permute-start(bf16[128,512]{1,0:T(8,128)(2,1)S(1)} %convolution_convert_fusion.1), channel_id=1, source_target_pairs={{0,4},{1,3},{4,8},{5,1},{8,12},{9,5},{12,14},{13,9},{14,10},{15,13... | collective-permute-start | bytes 393224 | tf_op jit(solution)/shard_map/ppermute | solution.py:261
  56.2 6.4 %collective-permute-start.21 = (bf16[128,512]{1,0:T(8,128)(2,1)S(1)}, bf16[128,512]{1,0:T(8,128)(2,1)S(1)}, u32[]{:S(2)}, u32[]{:S(2)}) collective-permute-start(bf16[128,512]{1,0:T(8,128)(2,1)S(1)} %fusion.5), channel_id=1, source_target_pairs={{0,4},{1,3},{4,8},{5,1},{8,12},{9,5},{12,14},{13,9},{14,10},{15,13... | collective-permute-start | bytes 393224 | tf_op jit(solution)/shard_map/ppermute | solution.py:261
  57.8 6.0 %collective-permute-start.17 = (bf16[128,512]{1,0:T(8,128)(2,1)S(1)}, bf16[128,512]{1,0:T(8,128)(2,1)S(1)}, u32[]{:S(2)}, u32[]{:S(2)}) collective-permute-start(bf16[128,512]{1,0:T(8,128)(2,1)S(1)} %fusion.2), channel_id=1, source_target_pairs={{0,4},{1,3},{4,8},{5,1},{8,12},{9,5},{12,14},{13,9},{14,10},{15,13... | collective-permute-start | bytes 393224 | tf_op jit(solution)/shard_map/ppermute | solution.py:261
  60.1 5.0 %collective-permute-start.31 = (bf16[128,512]{1,0:T(8,128)(2,1)S(1)}, bf16[128,512]{1,0:T(8,128)(2,1)S(1)}, u32[]{:S(2)}, u32[]{:S(2)}) collective-permute-start(bf16[128,512]{1,0:T(8,128)(2,1)S(1)} %convolution_convert_fusion), channel_id=1, source_target_pairs={{0,4},{1,3},{4,8},{5,1},{8,12},{9,5},{12,14},{13,9},{14,10},{15,13... | collective-permute-start | bytes 393224 | tf_op jit(solution)/shard_map/ppermute | solution.py:261
  61.5 5.1 %collective-permute-start.28 = (bf16[128,512]{1,0:T(8,128)(2,1)S(1)}, bf16[128,512]{1,0:T(8,128)(2,1)S(1)}, u32[]{:S(2)}, u32[]{:S(2)}) collective-permute-start(bf16[128,512]{1,0:T(8,128)(2,1)S(1)} %fusion.7), channel_id=1, source_target_pairs={{0,4},{1,3},{4,8},{5,1},{8,12},{9,5},{12,14},{13,9},{14,10},{15,13... | collective-permute-start | bytes 393224 | tf_op jit(solution)/shard_map/ppermute | solution.py:261
  62.9 5.0 %collective-permute-start.22 = (bf16[128,512]{1,0:T(8,128)(2,1)S(1)}, bf16[128,512]{1,0:T(8,128)(2,1)S(1)}, u32[]{:S(2)}, u32[]{:S(2)}) collective-permute-start(bf16[128,512]{1,0:T(8,128)(2,1)S(1)} %fusion.4), channel_id=1, source_target_pairs={{0,4},{1,3},{4,8},{5,1},{8,12},{9,5},{12,14},{13,9},{14,10},{15,13... | collective-permute-start | bytes 393224 | tf_op jit(solution)/shard_map/ppermute | solution.py:261
  64.0 8.1 %collective-permute-start.18 = (bf16[128,512]{1,0:T(8,128)(2,1)S(1)}, bf16[128,512]{1,0:T(8,128)(2,1)S(1)}, u32[]{:S(2)}, u32[]{:S(2)}) collective-permute-start(bf16[128,512]{1,0:T(8,128)(2,1)S(1)} %fusion.1), channel_id=1, source_target_pairs={{0,4},{1,3},{4,8},{5,1},{8,12},{9,5},{12,14},{13,9},{14,10},{15,13... | collective-permute-start | bytes 393224 | tf_op jit(solution)/shard_map/ppermute | solution.py:261
  65.4 5.4 %collective-permute-start.32 = (bf16[128,512]{1,0:T(8,128)(2,1)S(1)}, bf16[128,512]{1,0:T(8,128)(2,1)S(1)}, u32[]{:S(2)}, u32[]{:S(2)}) collective-permute-start(bf16[128,512]{1,0:T(8,128)(2,1)S(1)} %fusion.9), channel_id=1, source_target_pairs={{0,4},{1,3},{4,8},{5,1},{8,12},{9,5},{12,14},{13,9},{14,10},{15,13... | collective-permute-start | bytes 393224 | tf_op jit(solution)/shard_map/ppermute | solution.py:261
  66.8 6.8 %collective-permute-start.29 = (bf16[128,512]{1,0:T(8,128)(2,1)S(1)}, bf16[128,512]{1,0:T(8,128)(2,1)S(1)}, u32[]{:S(2)}, u32[]{:S(2)}) collective-permute-start(bf16[128,512]{1,0:T(8,128)(2,1)S(1)} %fusion.6), channel_id=1, source_target_pairs={{0,4},{1,3},{4,8},{5,1},{8,12},{9,5},{12,14},{13,9},{14,10},{15,13... | collective-permute-start | bytes 393224 | tf_op jit(solution)/shard_map/ppermute | solution.py:261
  68.2 10.9 %collective-permute-start.23 = (bf16[128,512]{1,0:T(8,128)(2,1)S(1)}, bf16[128,512]{1,0:T(8,128)(2,1)S(1)}, u32[]{:S(2)}, u32[]{:S(2)}) collective-permute-start(bf16[128,512]{1,0:T(8,128)(2,1)S(1)} %fusion.3), channel_id=1, source_target_pairs={{0,4},{1,3},{4,8},{5,1},{8,12},{9,5},{12,14},{13,9},{14,10},{15,13... | collective-permute-start | bytes 393224 | tf_op jit(solution)/shard_map/ppermute | solution.py:261
  71.0 5.0 %collective-permute-start.33 = (bf16[128,512]{1,0:T(8,128)(2,1)S(1)}, bf16[128,512]{1,0:T(8,128)(2,1)S(1)}, u32[]{:S(2)}, u32[]{:S(2)}) collective-permute-start(bf16[128,512]{1,0:T(8,128)(2,1)S(1)} %fusion.8), channel_id=1, source_target_pairs={{0,4},{1,3},{4,8},{5,1},{8,12},{9,5},{12,14},{13,9},{14,10},{15,13... | collective-permute-start | bytes 393224 | tf_op jit(solution)/shard_map/ppermute | solution.py:261
  72.4 6.6 %collective-permute-start.19 = (bf16[128,512]{1,0:T(8,128)(2,1)S(1)}, bf16[128,512]{1,0:T(8,128)(2,1)S(1)}, u32[]{:S(2)}, u32[]{:S(2)}) collective-permute-start(bf16[128,512]{1,0:T(8,128)(2,1)S(1)} %fusion), channel_id=1, source_target_pairs={{0,4},{1,3},{4,8},{5,1},{8,12},{9,5},{12,14},{13,9},{14,10},{15,13... | collective-permute-start | bytes 393224 | tf_op jit(solution)/shard_map/ppermute | solution.py:261
  73.5 5.5 %collective-permute-start.30 = (bf16[128,512]{1,0:T(8,128)(2,1)S(1)}, bf16[128,512]{1,0:T(8,128)(2,1)S(1)}, u32[]{:S(2)}, u32[]{:S(2)}) collective-permute-start(bf16[128,512]{1,0:T(8,128)(2,1)S(1)} %collective-permute-done.29), channel_id=1, source_target_pairs={{0,1},{1,0},{2,3},{3,2},{4,5},{5,4},{6,7},{7,6},{8,9},{9,8},{10,11... | collective-permute-start | bytes 393224 | tf_op jit(solution)/shard_map/ppermute | solution.py:262
  76.0 3.3 %collective-permute-start.34 = (bf16[128,512]{1,0:T(8,128)(2,1)S(1)}, bf16[128,512]{1,0:T(8,128)(2,1)S(1)}, u32[]{:S(2)}, u32[]{:S(2)}) collective-permute-start(bf16[128,512]{1,0:T(8,128)(2,1)S(1)} %collective-permute-done.33), channel_id=1, source_target_pairs={{0,1},{1,0},{2,3},{3,2},{4,5},{5,4},{6,7},{7,6},{8,9},{9,8},{10,11... | collective-permute-start | bytes 393224 | tf_op jit(solution)/shard_map/ppermute | solution.py:262

commit v4 on v3

--- a/solution.py
+++ b/solution.py
@@ -10,6 +10,8 @@
 BF = jnp.bfloat16
 F32 = jnp.float32
 MIB = 1024 * 1024
+VMEM = pl.BlockSpec(memory_space=pltpu.VMEM)
+SMEM = pl.BlockSpec(memory_space=pltpu.SMEM)
 LITTLE = pl.CostEstimate(flops=1, bytes_accessed=1, transcendentals=0)
 
 
@@ -128,15 +130,8 @@
     width = blocks * edge
     return pl.pallas_call(
         functools.partial(place_kernel, n=n, blocks=blocks, edge=edge),
-        grid_spec=pltpu.PrefetchScalarGridSpec(
-            num_scalar_prefetch=3,
-            grid=(1,),
-            in_specs=[pl.BlockSpec(values.shape, lambda *_: (0, 0, 0))],
-            out_specs=[
-                pl.BlockSpec((width, 2 * edge), lambda *_: (0, 0)),
-                pl.BlockSpec((width, edge), lambda *_: (0, 0)),
-            ],
-        ),
+        in_specs=[SMEM, SMEM, SMEM, VMEM],
+        out_specs=[VMEM, VMEM],
         out_shape=[
             jax.ShapeDtypeStruct((width, 2 * edge), BF),
             jax.ShapeDtypeStruct((width, edge), BF),
@@ -171,14 +166,12 @@
     half = len(x_m)
     rows, width = x_m[0].shape
     edge = w_d.shape[1]
-    whole = lambda shape: pl.BlockSpec(shape, lambda *_: (0, 0))
     gu, dh = (rows, 2 * edge), (rows, edge)
     arrays = [*x_m, *y_m, *x_s, *y_s, w_gu, w_d]
     return pl.pallas_call(
         functools.partial(forward_kernel, half=half, width=width),
-        grid=(1,),
-        in_specs=[whole(a.shape) for a in arrays],
-        out_specs=[whole(gu), whole(dh), whole(gu), whole(dh)],
+        in_specs=[VMEM] * len(arrays),
+        out_specs=[VMEM] * 4,
         out_shape=[jax.ShapeDtypeStruct(t, F32) for t in (gu, dh, gu, dh)],
         compiler_params=pltpu.CompilerParams(vmem_limit_bytes=28 * MIB),
         cost_estimate=LITTLE,
@@ -235,18 +228,35 @@
     arrays = [*x_m, *y_m, *x_s, *y_s, dgu_m, dgu_s, hid_m, hid_s]
     return pl.pallas_call(
         functools.partial(grads_kernel, half=half, blocks=blocks, edge=edge),
-        grid_spec=pltpu.PrefetchScalarGridSpec(
-            num_scalar_prefetch=3,
-            grid=(1,),
-            in_specs=[pl.BlockSpec(a.shape, lambda *_: (0, 0)) for a in arrays],
-            out_specs=pl.BlockSpec((slots, edge, edge), lambda *_: (0, 0, 0)),
-            scratch_shapes=[pltpu.VMEM((tiles, edge, edge), BF)],
-        ),
+        in_specs=[SMEM, SMEM, SMEM] + [VMEM] * len(arrays),
+        out_specs=VMEM,
+        scratch_shapes=[pltpu.VMEM((tiles, edge, edge), BF)],
         out_shape=jax.ShapeDtypeStruct((slots, edge, edge), BF),
         compiler_params=pltpu.CompilerParams(vmem_limit_bytes=28 * MIB),
         cost_estimate=LITTLE,
         name="tile_gradients",
     )(here, ids, count, *arrays)
+
+
+def sum_kernel(a_ref, b_ref, out_ref):
+    size = out_ref.shape[0]
+    rows = pl.ds(pl.program_id(0) * size, size)
+    out_ref[...] = (a_ref[rows].astype(F32) + b_ref[rows].astype(F32)).astype(BF)
+
+
+def sum_grads(a, b):
+    slots, edge, _ = a.shape
+    size = slots // 2 if slots % 2 == 0 else slots
+    return pl.pallas_call(
+        sum_kernel,
+        grid=(slots // size,),
+        in_specs=[pl.BlockSpec(memory_space=pltpu.VMEM)] * 2,
+        out_specs=pl.BlockSpec((size, edge, edge), lambda i: (i, 0, 0)),
+        out_shape=jax.ShapeDtypeStruct(a.shape, BF),
+        compiler_params=pltpu.CompilerParams(vmem_limit_bytes=16 * MIB),
+        cost_estimate=LITTLE,
+        name="sum_tile_gradients",
+    )(a, b)
 
 
 def ring_plan(tokens, cotangent, fwd_values, fwd_ids, fwd_count, bwd_ids, bwd_count, *, n):
@@ -297,34 +307,27 @@
     dgu_m = jnp.concatenate([dg_m, du_m], axis=1)
     dgu_s = jnp.concatenate([dg_s, du_s], axis=1)
 
-    part = width // 2
-
-    def term(dgu, d, p):
-        rows = w_gu[d * width + p * part : d * width + (p + 1) * part]
+    def term(dgu, d):
+        rows = w_gu[d * width : (d + 1) * width]
         return lax.dot_general(dgu, rows, (((1,), (1,)), ((), ())), preferred_element_type=F32)
 
-    run_m = [hop(term(dgu_m, half, p).astype(BF)) for p in range(2)]
-    run_s = [None, None]
-    for d in range(half + 1, n):
-        for p in range(2):
-            out = term(dgu_s, d, p)
-            if run_s[p] is not None:
-                out = out + run_s[p].astype(F32)
-            run_s[p] = hop(out.astype(BF))
-        for p in range(2):
-            run_m[p] = hop((term(dgu_m, d, p) + run_m[p].astype(F32)).astype(BF))
-    back = [swap(v) for v in run_s]
-
+    run_m = hop(term(dgu_m, half).astype(BF))
+    run_s = hop(term(dgu_s, half + 1).astype(BF))
     grads = tile_grads(
         here, bwd_ids[0], bwd_count, x_m, y_m, x_s, y_s, dgu_m, dgu_s, hid_m, hid_s, blocks
     )
-    grads = grads + swap(grads)
-    run_m[0], run_m[1], grads = lax.optimization_barrier((run_m[0], run_m[1], grads))
-    dx = [
-        (term(dgu_m, 0, p) + run_m[p].astype(F32) + back[p].astype(F32)).astype(BF)
-        for p in range(2)
-    ]
-    return jnp.concatenate(dx, axis=1), grads[None]
+    run_m, grads = lax.optimization_barrier((run_m, grads))
+    other = swap(grads)
+    for d in range(half + 1, n):
+        if d > half + 1:
+            run_s = hop((term(dgu_s, d) + run_s.astype(F32)).astype(BF))
+        run_m = hop((term(dgu_m, d) + run_m.astype(F32)).astype(BF))
+    back = swap(run_s)
+
+    grads = sum_grads(grads, other)
+    run_m, grads = lax.optimization_barrier((run_m, grads))
+    dx = term(dgu_m, 0) + run_m.astype(F32) + back.astype(F32)
+    return dx.astype(BF), grads[None]
 
 
 def on_device(tokens, cotangent, fwd_values, *rest, n, cores):

time: 81.1 us -> 77.5 us (0.956)
  other arithmetic: 4.01 us -> 0.25 us
  waiting for transfers between devices: 10.8 us -> 12.6 us
  starting transfers between devices: 47.4 us -> 46 us
    add x1 -> x0, other arithmetic: 3.03 us -> none  [ring_plan(): grads = grads + swap(grads)]
    pallas_call x0 -> x1, Pallas kernels: none -> 2.04 us  [sum_grads(): pl.pallas_call(sum_kernel, grid=(slots // size,), in_specs=[pl.BlockSpec(...]
    ppermute x26 -> x19, waiting for transfers between devices: 10.8 us -> 12.6 us  [ring_plan(): hop = lambda v: lax.ppermute(v, axes, perm)]
    pallas_call x1, Pallas kernels: 3.23 us -> 1.85 us  [place(): pl.pallas_call(functools.partial(place_kernel, n=n, blocks=blocks, edge=e...]
    ppermute x26 -> x19, starting transfers between devices: 44.8 us -> 43.5 us  [ring_plan(): hop = lambda v: lax.ppermute(v, axes, perm)]
    dot_general x16 -> x8, matrix products: 3.56 us -> 3.16 us  [term(): lax.dot_general(dgu, rows, (((1,), (1,)), ((), ())), preferred_element_ty...]
  transfers between devices with their start and end apart: 35 -> 27, of which waited for: 11 -> 10; matrix products, arithmetic and copies ran while one was open for 9% -> 4% of each run, Pallas kernels for 9% -> 11%
where the time goes in v4:
time: 77.5 us; the launch traced here: 77.1 us
  starting transfers between devices  46 us (59%)
  waiting for transfers between devices  12.6 us (16%)
  Pallas kernels  8.28 us (11%)
  local copies, waits for them, and re-layouts  4.07 us (5%)
  matrix products  3.61 us (5%)
  between operations  2.2 us (3%)
    ppermute x19, starting transfers between devices, ring_plan(): hop = lambda v: lax.ppermute(v, axes, perm)  43.5 us
    ppermute x19, waiting for transfers between devices, ring_plan(): hop = lambda v: lax.ppermute(v, axes, perm)  12.6 us
    unnamed x14, local copies, waits for them, and re-layouts  4.07 us
    pallas_call x1, Pallas kernels, tile_grads(): pl.pallas_call(functools.partial(grads_kernel, half=half, blocks=blocks,...  3.25 us
    dot_general x8, matrix products, term(): lax.dot_general(dgu, rows, (((1,), (1,)), ((), ())), preferred_element_ty...  3.16 us
    pallas_call x1, Pallas kernels, sum_grads(): pl.pallas_call(sum_kernel, grid=(slots // size,), in_specs=[pl.BlockSpec(...  2.04 us
    pallas_call x1, Pallas kernels, place(): pl.pallas_call(functools.partial(place_kernel, n=n, blocks=blocks, edge=e...  1.85 us
  transfers between devices with their start and end apart: 27, of which 10 were waited for; matrix products, arithmetic and copies ran while one was open for 4% of the time, Pallas kernels for 11%

profile of v4, /device:TPU:0, one launch (start us, length us, event | category | flops | bytes accessed | tf_op | source)
XLA Modules:
  0.0 77.1 jit_solution(10276523542374995659)
XLA Ops:
  0.6 3.1 %collective-permute-start.3 = (bf16[128,1024]{1,0:T(8,128)(2,1)}, bf16[128,1024]{1,0:T(8,128)(2,1)S(1)}, u32[]{:S(2)}, u32[]{:S(2)}) collective-permute-start(bf16[128,1024]{1,0:T(8,128)(2,1)} %refs_5_.1), channel_id=1, source_target_pairs={{0,4},{1,3},{4,8},{5,1},{8,12},{9,5},{12,14},{13,9},{14,10},{15,13... | collective-permute-start | bytes 786440 | tf_op jit(solution)/shard_map/ppermute | solution.py:271
  3.7 1.6 %collective-permute-start = (bf16[128,1024]{1,0:T(8,128)(2,1)}, bf16[128,1024]{1,0:T(8,128)(2,1)S(1)}, u32[]{:S(2)}, u32[]{:S(2)}) collective-permute-start(bf16[128,1024]{1,0:T(8,128)(2,1)} %refs_0_.3), channel_id=1, source_target_pairs={{0,4},{1,3},{4,8},{5,1},{8,12},{9,5},{12,14},{13,9},{14,10},{15,13... | collective-permute-start | bytes 786440 | tf_op jit(solution)/shard_map/ppermute | solution.py:271
  5.3 0.4 collective-permute-start.9
  5.7 1.4 %collective-permute-start.6 = (bf16[128,1024]{1,0:T(8,128)(2,1)}, bf16[128,1024]{1,0:T(8,128)(2,1)S(1)}, u32[]{:S(2)}, u32[]{:S(2)}) collective-permute-start(bf16[128,1024]{1,0:T(8,128)(2,1)} %refs_0_.3), channel_id=1, source_target_pairs={{1,4},{0,3},{5,8},{4,1},{9,12},{8,5},{13,14},{12,9},{15,10},{14,13... | collective-permute-start | bytes 786440 | tf_op jit(solution)/shard_map/ppermute | solution.py:289
  7.0 1.2 %collective-permute-done.3.refs_5_.refs_6_ = bf16[128,1024]{1,0:T(8,128)(2,1)S(1)} collective-permute-done((bf16[128,1024]{1,0:T(8,128)(2,1)}, bf16[128,1024]{1,0:T(8,128)(2,1)S(1)}, u32[]{:S(2)}, u32[]{:S(2)}) %collective-permute-start.3) | collective-permute-done | bytes 262176 | tf_op jit(solution)/shard_map/ppermute | solution.py:271
  8.2 2.3 %collective-permute-start.4 = (bf16[128,1024]{1,0:T(8,128)(2,1)S(1)}, bf16[128,1024]{1,0:T(8,128)(2,1)S(1)}, u32[]{:S(2)}, u32[]{:S(2)}) collective-permute-start(bf16[128,1024]{1,0:T(8,128)(2,1)S(1)} %collective-permute-done.3.refs_5_.refs_6_), channel_id=1, source_target_pairs={{0,4},{1,3},{4,8},{5,1},{8,12},{9,5},{12,14},{13,9},{14,10},{15,13... | collective-permute-start | bytes 786440 | tf_op jit(solution)/shard_map/ppermute | solution.py:271
  11.1 0.1 pad_add_fusion.here_ref
  11.2 1.5 %copy-done = bf16[1,56,128,128]{3,2,1,0:T(8,128)(2,1)S(1)} copy-done((bf16[1,56,128,128]{3,2,1,0:T(8,128)(2,1)S(1)}, bf16[1,56,128,128]{3,2,1,0:T(8,128)(2,1)}, u32[]{:S(2)}) %copy-start) | copy-done | bytes 1835032
  12.7 0.7 copy-done.6
  13.3 1.9 %place_weights.1 = (bf16[8192,256]{1,0:T(8,128)(2,1)S(1)}, bf16[8192,128]{1,0:T(8,128)(2,1)S(1)}) custom-call(s32[2]{0:T(128)S(1)} %pad_add_fusion.here_ref, s32[56]{0:T(128)S(1)} %bitcast.14, s32[1]{0:T(128)S(6)} %copy.11.cnt_ref, bf16[56,128,128]{2,1,0:T(8,128)(2,1)S(1)} %bitcast.12), custom_call_target="tpu_custom_call" | custom-call | flops 1 | bytes 1 | tf_op jit(solution)/shard_map/place_weights/pallas_call | solution.py:131
  15.2 0.0 collective-permute-done.refs_1_
  15.2 2.1 %collective-permute-start.1 = (bf16[128,1024]{1,0:T(8,128)(2,1)S(1)}, bf16[128,1024]{1,0:T(8,128)(2,1)S(1)}, u32[]{:S(2)}, u32[]{:S(2)}) collective-permute-start(bf16[128,1024]{1,0:T(8,128)(2,1)S(1)} %collective-permute-done.refs_1_), channel_id=1, source_target_pairs={{0,4},{1,3},{4,8},{5,1},{8,12},{9,5},{12,14},{13,9},{14,10},{15,13... | collective-permute-start | bytes 786440 | tf_op jit(solution)/shard_map/ppermute | solution.py:271
  17.3 4.0 %collective-permute-start.10 = (bf16[128,1024]{1,0:T(8,128)(2,1)S(1)}, bf16[128,1024]{1,0:T(8,128)(2,1)S(1)}, u32[]{:S(2)}, u32[]{:S(2)}) collective-permute-start(bf16[128,1024]{1,0:T(8,128)(2,1)S(1)} %collective-permute-done.9.refs_11_.refs_13_), channel_id=1, source_target_pairs={{0,4},{1,3},{4,8},{5,1},{8,12},{9,5},{12,14},{13,9},{14,10},{15,13... | collective-permute-start | bytes 786440 | tf_op jit(solution)/shard_map/ppermute | solution.py:271
  21.4 1.5 %collective-permute-start.7 = (bf16[128,1024]{1,0:T(8,128)(2,1)S(1)}, bf16[128,1024]{1,0:T(8,128)(2,1)S(1)}, u32[]{:S(2)}, u32[]{:S(2)}) collective-permute-start(bf16[128,1024]{1,0:T(8,128)(2,1)S(1)} %collective-permute-done.6.refs_8_.refs_10_), channel_id=1, source_target_pairs={{0,4},{1,3},{4,8},{5,1},{8,12},{9,5},{12,14},{13,9},{14,10},{15,13... | collective-permute-start | bytes 786440 | tf_op jit(solution)/shard_map/ppermute | solution.py:271
  22.9 1.5 %collective-permute-start.5 = (bf16[128,1024]{1,0:T(8,128)(2,1)S(1)}, bf16[128,1024]{1,0:T(8,128)(2,1)S(1)}, u32[]{:S(2)}, u32[]{:S(2)}) collective-permute-start(bf16[128,1024]{1,0:T(8,128)(2,1)S(1)} %collective-permute-done.4.refs_6_.refs_7_), channel_id=1, source_target_pairs={{0,4},{1,3},{4,8},{5,1},{8,12},{9,5},{12,14},{13,9},{14,10},{15,13... | collective-permute-start | bytes 786440 | tf_op jit(solution)/shard_map/ppermute | solution.py:271
  24.4 0.8 %collective-permute-start.2 = (bf16[128,1024]{1,0:T(8,128)(2,1)S(1)}, bf16[128,1024]{1,0:T(8,128)(2,1)S(1)}, u32[]{:S(2)}, u32[]{:S(2)}) collective-permute-start(bf16[128,1024]{1,0:T(8,128)(2,1)S(1)} %collective-permute-done.1.refs_2_), channel_id=1, source_target_pairs={{0,4},{1,3},{4,8},{5,1},{8,12},{9,5},{12,14},{13,9},{14,10},{15,13... | collective-permute-start | bytes 786440 | tf_op jit(solution)/shard_map/ppermute | solution.py:271
  25.3 0.0 collective-permute-done.10.refs_12_.refs_14_
  25.3 2.8 %collective-permute-start.11 = (bf16[128,1024]{1,0:T(8,128)(2,1)S(1)}, bf16[128,1024]{1,0:T(8,128)(2,1)S(1)}, u32[]{:S(2)}, u32[]{:S(2)}) collective-permute-start(bf16[128,1024]{1,0:T(8,128)(2,1)S(1)} %collective-permute-done.10.refs_12_.refs_14_), channel_id=1, source_target_pairs={{0,4},{1,3},{4,8},{5,1},{8,12},{9,5},{12,14},{13,9},{14,10},{15,13... | collective-permute-start | bytes 786440 | tf_op jit(solution)/shard_map/ppermute | solution.py:271
  28.1 0.0 collective-permute-done.7.refs_9_.refs_11_
  28.1 2.8 %collective-permute-start.8 = (bf16[128,1024]{1,0:T(8,128)(2,1)S(1)}, bf16[128,1024]{1,0:T(8,128)(2,1)S(1)}, u32[]{:S(2)}, u32[]{:S(2)}) collective-permute-start(bf16[128,1024]{1,0:T(8,128)(2,1)S(1)} %collective-permute-done.7.refs_9_.refs_11_), channel_id=1, source_target_pairs={{0,4},{1,3},{4,8},{5,1},{8,12},{9,5},{12,14},{13,9},{14,10},{15,13... | collective-permute-start | bytes 786440 | tf_op jit(solution)/shard_map/ppermute | solution.py:271
  30.9 0.0 collective-permute-done.5.refs_7_.refs_8_
  30.9 2.8 %collective-permute-start.12 = (bf16[128,1024]{1,0:T(8,128)(2,1)S(1)}, bf16[128,1024]{1,0:T(8,128)(2,1)S(1)}, u32[]{:S(2)}, u32[]{:S(2)}) collective-permute-start(bf16[128,1024]{1,0:T(8,128)(2,1)S(1)} %collective-permute-done.5.refs_7_.refs_8_), channel_id=1, source_target_pairs={{0,4},{1,3},{4,8},{5,1},{8,12},{9,5},{12,14},{13,9},{14,10},{15,13... | collective-permute-start | bytes 786440 | tf_op jit(solution)/shard_map/ppermute | solution.py:271
  33.7 0.0 collective-permute-done.2.refs_3_
  33.7 2.8 %collective-permute-start.14 = (bf16[128,1024]{1,0:T(8,128)(2,1)S(1)}, bf16[128,1024]{1,0:T(8,128)(2,1)S(1)}, u32[]{:S(2)}, u32[]{:S(2)}) collective-permute-start(bf16[128,1024]{1,0:T(8,128)(2,1)S(1)} %collective-permute-done.2.refs_3_), channel_id=1, source_target_pairs={{0,4},{1,3},{4,8},{5,1},{8,12},{9,5},{12,14},{13,9},{14,10},{15,13... | collective-permute-start | bytes 786440 | tf_op jit(solution)/shard_map/ppermute | solution.py:271
  37.1 2.1 %collective-permute-done.8.refs_10_.refs_12_ = bf16[128,1024]{1,0:T(8,128)(2,1)S(1)} collective-permute-done((bf16[128,1024]{1,0:T(8,128)(2,1)S(1)}, bf16[128,1024]{1,0:T(8,128)(2,1)S(1)}, u32[]{:S(2)}, u32[]{:S(2)}) %collective-permute-start.8) | collective-permute-done | bytes 262176 | tf_op jit(solution)/shard_map/ppermute | solution.py:271
  39.3 0.9 %copy-done.1 = bf16[128,1024]{1,0:T(8,128)(2,1)S(1)} copy-done((bf16[128,1024]{1,0:T(8,128)(2,1)S(1)}, bf16[128,1024]{1,0:T(8,128)(2,1)}, u32[]{:S(2)}) %copy-start.1) | copy-done | bytes 262168
  40.3 0.9 %copy-done.3 = bf16[128,1024]{1,0:T(8,128)(2,1)S(1)} copy-done((bf16[128,1024]{1,0:T(8,128)(2,1)S(1)}, bf16[128,1024]{1,0:T(8,128)(2,1)}, u32[]{:S(2)}) %copy-start.3) | copy-done | bytes 262168
  41.2 1.1 %forward_terms.1 = (f32[128,256]{1,0:T(8,128)S(1)}, f32[128,128]{1,0:T(8,128)S(1)}, f32[128,256]{1,0:T(8,128)S(1)}, f32[128,128]{1,0:T(8,128)S(1)}) custom-call(bf16[128,1024]{1,0:T(8,128)(2,1)S(1)} %copy-done.1, bf16[128,1024]{1,0:T(8,128)(2,1)S(1)} %collective-permute-done.refs_1_, bf16[128,1024]{1,0:T(8,128)(2,1)S(1)} %collective-permute-done.1.refs_2_, ...), custom_call_target="tpu_custom_call" | custom-call | flops 1 | bytes 1 | tf_op jit(solution)/shard_map/forward_terms/pallas_call | solution.py:171
  42.3 0.0 copy-start.2
  42.4 0.0 copy-start.4
  42.4 0.0 copy-start.5
  42.4 0.1 collective-permute-start.15
  42.5 0.5 collective-permute-start.13
  43.0 0.2 fusion.5
  43.2 0.1 collective-permute-start.17
  43.3 1.6 %collective-permute-done.14.refs_4_ = bf16[128,1024]{1,0:T(8,128)(2,1)S(1)} collective-permute-done((bf16[128,1024]{1,0:T(8,128)(2,1)S(1)}, bf16[128,1024]{1,0:T(8,128)(2,1)S(1)}, u32[]{:S(2)}, u32[]{:S(2)}) %collective-permute-start.14) | collective-permute-done | bytes 262176 | tf_op jit(solution)/shard_map/ppermute | solution.py:271
  44.9 0.2 fusion.14
  45.2 0.1 collective-permute-start.18
  45.3 0.1 multiply_convert_fusion.5
  45.4 0.3 convolution_convert_fusion.1
  45.7 2.9 %collective-permute-start.16 = (bf16[128,1024]{1,0:T(8,128)(2,1)S(1)}, bf16[128,1024]{1,0:T(8,128)(2,1)S(1)}, u32[]{:S(2)}, u32[]{:S(2)}) collective-permute-start(bf16[128,1024]{1,0:T(8,128)(2,1)S(1)} %convolution_convert_fusion.1), channel_id=1, source_target_pairs={{0,4},{1,3},{4,8},{5,1},{8,12},{9,5},{12,14},{13,9},{14,10},{15,13... | collective-permute-start | bytes 786440 | tf_op jit(solution)/shard_map/ppermute | solution.py:271
  48.6 0.1 multiply_convert_fusion.3
  48.7 3.3 %tile_gradients.1.a_ref = bf16[96,128,128]{2,1,0:T(8,128)(2,1)S(1)} custom-call(s32[2]{0:T(128)S(1)} %pad_add_fusion.here_ref, s32[96]{0:T(128)S(1)} %bitcast.13, s32[1]{0:T(128)S(6)} %copy.12.cnt_ref, bf16[128,1024]{1,0:T(8,128)(2,1)S(1)} %copy-done.2, bf16[128,1024]{1,0:T(8,128)(2,1)S(1)} %collective-permute-done.refs_1_, ...), custom_call_target="tpu_custom_call" | custom-call | flops 1 | bytes 1 | tf_op jit(solution)/shard_map/tile_gradients/pallas_call | solution.py:229
  52.0 1.1 %collective-permute-done.16 = bf16[128,1024]{1,0:T(8,128)(2,1)S(1)} collective-permute-done((bf16[128,1024]{1,0:T(8,128)(2,1)S(1)}, bf16[128,1024]{1,0:T(8,128)(2,1)S(1)}, u32[]{:S(2)}, u32[]{:S(2)}) %collective-permute-start.16) | collective-permute-done | bytes 262176 | tf_op jit(solution)/shard_map/ppermute | solution.py:271
  53.0 0.3 convolution_convert_fusion
  53.4 2.0 %collective-permute-start.23 = (bf16[128,1024]{1,0:T(8,128)(2,1)S(1)}, bf16[128,1024]{1,0:T(8,128)(2,1)S(1)}, u32[]{:S(2)}, u32[]{:S(2)}) collective-permute-start(bf16[128,1024]{1,0:T(8,128)(2,1)S(1)} %convolution_convert_fusion), channel_id=1, source_target_pairs={{0,4},{1,3},{4,8},{5,1},{8,12},{9,5},{12,14},{13,9},{14,10},{15,13... | collective-permute-start | bytes 786440 | tf_op jit(solution)/shard_map/ppermute | solution.py:271
  55.4 0.3 fusion.2
  55.7 2.4 %collective-permute-start.19 = (bf16[128,1024]{1,0:T(8,128)(2,1)S(1)}, bf16[128,1024]{1,0:T(8,128)(2,1)S(1)}, u32[]{:S(2)}, u32[]{:S(2)}) collective-permute-start(bf16[128,1024]{1,0:T(8,128)(2,1)S(1)} %fusion.2), channel_id=1, source_target_pairs={{0,4},{1,3},{4,8},{5,1},{8,12},{9,5},{12,14},{13,9},{14,10},{15,13... | collective-permute-start | bytes 786440 | tf_op jit(solution)/shard_map/ppermute | solution.py:271
  58.1 1.7 %collective-permute-done.23 = bf16[128,1024]{1,0:T(8,128)(2,1)S(1)} collective-permute-done((bf16[128,1024]{1,0:T(8,128)(2,1)S(1)}, bf16[128,1024]{1,0:T(8,128)(2,1)S(1)}, u32[]{:S(2)}, u32[]{:S(2)}) %collective-permute-start.23) | collective-permute-done | bytes 262176 | tf_op jit(solution)/shard_map/ppermute | solution.py:271
  59.8 0.3 fusion.4
  60.1 2.0 %collective-permute-start.24 = (bf16[128,1024]{1,0:T(8,128)(2,1)S(1)}, bf16[128,1024]{1,0:T(8,128)(2,1)S(1)}, u32[]{:S(2)}, u32[]{:S(2)}) collective-permute-start(bf16[128,1024]{1,0:T(8,128)(2,1)S(1)} %fusion.4), channel_id=1, source_target_pairs={{0,4},{1,3},{4,8},{5,1},{8,12},{9,5},{12,14},{13,9},{14,10},{15,13... | collective-permute-start | bytes 786440 | tf_op jit(solution)/shard_map/ppermute | solution.py:271
  62.1 0.5 collective-permute-done.19
  62.6 0.3 fusion.1
  62.9 2.0 %collective-permute-start.20 = (bf16[128,1024]{1,0:T(8,128)(2,1)S(1)}, bf16[128,1024]{1,0:T(8,128)(2,1)S(1)}, u32[]{:S(2)}, u32[]{:S(2)}) collective-permute-start(bf16[128,1024]{1,0:T(8,128)(2,1)S(1)} %fusion.1), channel_id=1, source_target_pairs={{0,4},{1,3},{4,8},{5,1},{8,12},{9,5},{12,14},{13,9},{14,10},{15,13... | collective-permute-start | bytes 786440 | tf_op jit(solution)/shard_map/ppermute | solution.py:271
  64.9 1.6 %collective-permute-done.24 = bf16[128,1024]{1,0:T(8,128)(2,1)S(1)} collective-permute-done((bf16[128,1024]{1,0:T(8,128)(2,1)S(1)}, bf16[128,1024]{1,0:T(8,128)(2,1)S(1)}, u32[]{:S(2)}, u32[]{:S(2)}) %collective-permute-start.24) | collective-permute-done | bytes 262176 | tf_op jit(solution)/shard_map/ppermute | solution.py:271
  66.5 0.3 fusion.3
  66.8 2.0 %collective-permute-start.25 = (bf16[128,1024]{1,0:T(8,128)(2,1)S(1)}, bf16[128,1024]{1,0:T(8,128)(2,1)S(1)}, u32[]{:S(2)}, u32[]{:S(2)}) collective-permute-start(bf16[128,1024]{1,0:T(8,128)(2,1)S(1)} %fusion.3), channel_id=1, source_target_pairs={{0,4},{1,3},{4,8},{5,1},{8,12},{9,5},{12,14},{13,9},{14,10},{15,13... | collective-permute-start | bytes 786440 | tf_op jit(solution)/shard_map/ppermute | solution.py:271
  68.8 0.5 collective-permute-done.20
  69.3 0.3 fusion
  69.7 2.0 %collective-permute-start.21 = (bf16[128,1024]{1,0:T(8,128)(2,1)S(1)}, bf16[128,1024]{1,0:T(8,128)(2,1)S(1)}, u32[]{:S(2)}, u32[]{:S(2)}) collective-permute-start(bf16[128,1024]{1,0:T(8,128)(2,1)S(1)} %fusion), channel_id=1, source_target_pairs={{0,4},{1,3},{4,8},{5,1},{8,12},{9,5},{12,14},{13,9},{14,10},{15,13... | collective-permute-start | bytes 786440 | tf_op jit(solution)/shard_map/ppermute | solution.py:271
  71.7 1.6 %collective-permute-done.25 = bf16[128,1024]{1,0:T(8,128)(2,1)S(1)} collective-permute-done((bf16[128,1024]{1,0:T(8,128)(2,1)S(1)}, bf16[128,1024]{1,0:T(8,128)(2,1)S(1)}, u32[]{:S(2)}, u32[]{:S(2)}) %collective-permute-start.25) | collective-permute-done | bytes 262176 | tf_op jit(solution)/shard_map/ppermute | solution.py:271
  73.3 2.0 %sum_tile_gradients.1 = bf16[96,128,128]{2,1,0:T(8,128)(2,1)} custom-call(bf16[96,128,128]{2,1,0:T(8,128)(2,1)S(1)} %tile_gradients.1.a_ref, bf16[96,128,128]{2,1,0:T(8,128)(2,1)S(1)} %collective-permute-done.22.b_ref), custom_call_target="tpu_custom_call" | custom-call | flops 1 | bytes 1 | tf_op jit(solution)/shard_map/sum_tile_gradients/pallas_call | solution.py:250
  75.3 0.8 collective-permute-done.21
  76.1 1.0 %add_convert_fusion = bf16[128,1024]{1,0:T(8,128)(2,1)} fusion(bf16[128,1024]{1,0:T(8,128)(2,1)S(1)} %collective-permute-done.26, bf16[128,1024]{1,0:T(8,128)(2,1)S(1)} %collective-permute-done.21, bf16[8192,256]{1,0:T(8,128)(2,1)S(1)} %get-tuple-element.18.refs_14_, bf16[128,128]{1,0:T(8,128)(2,1)S(1)} %get-tuple-element.31, ...), kind=kOutput, calls=%fused_computation.15 | convolution fusion | flops 67895296 | bytes 1376256 | tf_op jit(solution)/shard_map/dot_general | solution.py:312
  (25 shorter events, 0.1 us)
Async XLA Ops:
  0.6 7.6 %collective-permute-start.3 = (bf16[128,1024]{1,0:T(8,128)(2,1)}, bf16[128,1024]{1,0:T(8,128)(2,1)S(1)}, u32[]{:S(2)}, u32[]{:S(2)}) collective-permute-start(bf16[128,1024]{1,0:T(8,128)(2,1)} %refs_5_.1), channel_id=1, source_target_pairs={{0,4},{1,3},{4,8},{5,1},{8,12},{9,5},{12,14},{13,9},{14,10},{15,13... | collective-permute-start | bytes 786440 | tf_op jit(solution)/shard_map/ppermute | solution.py:271
  3.7 11.5 %collective-permute-start = (bf16[128,1024]{1,0:T(8,128)(2,1)}, bf16[128,1024]{1,0:T(8,128)(2,1)S(1)}, u32[]{:S(2)}, u32[]{:S(2)}) collective-permute-start(bf16[128,1024]{1,0:T(8,128)(2,1)} %refs_0_.3), channel_id=1, source_target_pairs={{0,4},{1,3},{4,8},{5,1},{8,12},{9,5},{12,14},{13,9},{14,10},{15,13... | collective-permute-start | bytes 786440 | tf_op jit(solution)/shard_map/ppermute | solution.py:271
  5.3 12.0 %collective-permute-start.9 = (bf16[128,1024]{1,0:T(8,128)(2,1)}, bf16[128,1024]{1,0:T(8,128)(2,1)S(1)}, u32[]{:S(2)}, u32[]{:S(2)}) collective-permute-start(bf16[128,1024]{1,0:T(8,128)(2,1)} %refs_5_.1), channel_id=1, source_target_pairs={{1,4},{0,3},{5,8},{4,1},{9,12},{8,5},{13,14},{12,9},{15,10},{14,13... | collective-permute-start | bytes 786440 | tf_op jit(solution)/shard_map/ppermute | solution.py:289
  5.7 15.7 %collective-permute-start.6 = (bf16[128,1024]{1,0:T(8,128)(2,1)}, bf16[128,1024]{1,0:T(8,128)(2,1)S(1)}, u32[]{:S(2)}, u32[]{:S(2)}) collective-permute-start(bf16[128,1024]{1,0:T(8,128)(2,1)} %refs_0_.3), channel_id=1, source_target_pairs={{1,4},{0,3},{5,8},{4,1},{9,12},{8,5},{13,14},{12,9},{15,10},{14,13... | collective-permute-start | bytes 786440 | tf_op jit(solution)/shard_map/ppermute | solution.py:289
  8.2 14.7 %collective-permute-start.4 = (bf16[128,1024]{1,0:T(8,128)(2,1)S(1)}, bf16[128,1024]{1,0:T(8,128)(2,1)S(1)}, u32[]{:S(2)}, u32[]{:S(2)}) collective-permute-start(bf16[128,1024]{1,0:T(8,128)(2,1)S(1)} %collective-permute-done.3.refs_5_.refs_6_), channel_id=1, source_target_pairs={{0,4},{1,3},{4,8},{5,1},{8,12},{9,5},{12,14},{13,9},{14,10},{15,13... | collective-permute-start | bytes 786440 | tf_op jit(solution)/shard_map/ppermute | solution.py:271
  11.2 1.5 %copy-start = (bf16[1,56,128,128]{3,2,1,0:T(8,128)(2,1)S(1)}, bf16[1,56,128,128]{3,2,1,0:T(8,128)(2,1)}, u32[]{:S(2)}) copy-start(bf16[1,56,128,128]{3,2,1,0:T(8,128)(2,1)} %param.9) | copy-start | bytes 5505028
  12.7 0.7 copy-start.6
  15.2 9.2 %collective-permute-start.1 = (bf16[128,1024]{1,0:T(8,128)(2,1)S(1)}, bf16[128,1024]{1,0:T(8,128)(2,1)S(1)}, u32[]{:S(2)}, u32[]{:S(2)}) collective-permute-start(bf16[128,1024]{1,0:T(8,128)(2,1)S(1)} %collective-permute-done.refs_1_), channel_id=1, source_target_pairs={{0,4},{1,3},{4,8},{5,1},{8,12},{9,5},{12,14},{13,9},{14,10},{15,13... | collective-permute-start | bytes 786440 | tf_op jit(solution)/shard_map/ppermute | solution.py:271
  17.3 7.9 %collective-permute-start.10 = (bf16[128,1024]{1,0:T(8,128)(2,1)S(1)}, bf16[128,1024]{1,0:T(8,128)(2,1)S(1)}, u32[]{:S(2)}, u32[]{:S(2)}) collective-permute-start(bf16[128,1024]{1,0:T(8,128)(2,1)S(1)} %collective-permute-done.9.refs_11_.refs_13_), channel_id=1, source_target_pairs={{0,4},{1,3},{4,8},{5,1},{8,12},{9,5},{12,14},{13,9},{14,10},{15,13... | collective-permute-start | bytes 786440 | tf_op jit(solution)/shard_map/ppermute | solution.py:271
  21.4 6.7 %collective-permute-start.7 = (bf16[128,1024]{1,0:T(8,128)(2,1)S(1)}, bf16[128,1024]{1,0:T(8,128)(2,1)S(1)}, u32[]{:S(2)}, u32[]{:S(2)}) collective-permute-start(bf16[128,1024]{1,0:T(8,128)(2,1)S(1)} %collective-permute-done.6.refs_8_.refs_10_), channel_id=1, source_target_pairs={{0,4},{1,3},{4,8},{5,1},{8,12},{9,5},{12,14},{13,9},{14,10},{15,13... | collective-permute-start | bytes 786440 | tf_op jit(solution)/shard_map/ppermute | solution.py:271
  22.9 8.0 %collective-permute-start.5 = (bf16[128,1024]{1,0:T(8,128)(2,1)S(1)}, bf16[128,1024]{1,0:T(8,128)(2,1)S(1)}, u32[]{:S(2)}, u32[]{:S(2)}) collective-permute-start(bf16[128,1024]{1,0:T(8,128)(2,1)S(1)} %collective-permute-done.4.refs_6_.refs_7_), channel_id=1, source_target_pairs={{0,4},{1,3},{4,8},{5,1},{8,12},{9,5},{12,14},{13,9},{14,10},{15,13... | collective-permute-start | bytes 786440 | tf_op jit(solution)/shard_map/ppermute | solution.py:271
  24.4 9.3 %collective-permute-start.2 = (bf16[128,1024]{1,0:T(8,128)(2,1)S(1)}, bf16[128,1024]{1,0:T(8,128)(2,1)S(1)}, u32[]{:S(2)}, u32[]{:S(2)}) collective-permute-start(bf16[128,1024]{1,0:T(8,128)(2,1)S(1)} %collective-permute-done.1.refs_2_), channel_id=1, source_target_pairs={{0,4},{1,3},{4,8},{5,1},{8,12},{9,5},{12,14},{13,9},{14,10},{15,13... | collective-permute-start | bytes 786440 | tf_op jit(solution)/shard_map/ppermute | solution.py:271
  25.3 11.9 %collective-permute-start.11 = (bf16[128,1024]{1,0:T(8,128)(2,1)S(1)}, bf16[128,1024]{1,0:T(8,128)(2,1)S(1)}, u32[]{:S(2)}, u32[]{:S(2)}) collective-permute-start(bf16[128,1024]{1,0:T(8,128)(2,1)S(1)} %collective-permute-done.10.refs_12_.refs_14_), channel_id=1, source_target_pairs={{0,4},{1,3},{4,8},{5,1},{8,12},{9,5},{12,14},{13,9},{14,10},{15,13... | collective-permute-start | bytes 786440 | tf_op jit(solution)/shard_map/ppermute | solution.py:271
  28.1 11.2 %collective-permute-start.8 = (bf16[128,1024]{1,0:T(8,128)(2,1)S(1)}, bf16[128,1024]{1,0:T(8,128)(2,1)S(1)}, u32[]{:S(2)}, u32[]{:S(2)}) collective-permute-start(bf16[128,1024]{1,0:T(8,128)(2,1)S(1)} %collective-permute-done.7.refs_9_.refs_11_), channel_id=1, source_target_pairs={{0,4},{1,3},{4,8},{5,1},{8,12},{9,5},{12,14},{13,9},{14,10},{15,13... | collective-permute-start | bytes 786440 | tf_op jit(solution)/shard_map/ppermute | solution.py:271
  30.9 12.1 %collective-permute-start.12 = (bf16[128,1024]{1,0:T(8,128)(2,1)S(1)}, bf16[128,1024]{1,0:T(8,128)(2,1)S(1)}, u32[]{:S(2)}, u32[]{:S(2)}) collective-permute-start(bf16[128,1024]{1,0:T(8,128)(2,1)S(1)} %collective-permute-done.5.refs_7_.refs_8_), channel_id=1, source_target_pairs={{0,4},{1,3},{4,8},{5,1},{8,12},{9,5},{12,14},{13,9},{14,10},{15,13... | collective-permute-start | bytes 786440 | tf_op jit(solution)/shard_map/ppermute | solution.py:271
  33.7 11.2 %collective-permute-start.14 = (bf16[128,1024]{1,0:T(8,128)(2,1)S(1)}, bf16[128,1024]{1,0:T(8,128)(2,1)S(1)}, u32[]{:S(2)}, u32[]{:S(2)}) collective-permute-start(bf16[128,1024]{1,0:T(8,128)(2,1)S(1)} %collective-permute-done.2.refs_3_), channel_id=1, source_target_pairs={{0,4},{1,3},{4,8},{5,1},{8,12},{9,5},{12,14},{13,9},{14,10},{15,13... | collective-permute-start | bytes 786440 | tf_op jit(solution)/shard_map/ppermute | solution.py:271
  39.3 0.9 %copy-start.1 = (bf16[128,1024]{1,0:T(8,128)(2,1)S(1)}, bf16[128,1024]{1,0:T(8,128)(2,1)}, u32[]{:S(2)}) copy-start(bf16[128,1024]{1,0:T(8,128)(2,1)} %refs_0_.3) | copy-start | bytes 786436
  40.3 0.9 %copy-start.3 = (bf16[128,1024]{1,0:T(8,128)(2,1)S(1)}, bf16[128,1024]{1,0:T(8,128)(2,1)}, u32[]{:S(2)}) copy-start(bf16[128,1024]{1,0:T(8,128)(2,1)} %refs_5_.1) | copy-start | bytes 786436
  42.3 6.3 %copy-start.2 = (bf16[128,1024]{1,0:T(8,128)(2,1)S(1)}, bf16[128,1024]{1,0:T(8,128)(2,1)}, u32[]{:S(2)}) copy-start(bf16[128,1024]{1,0:T(8,128)(2,1)} %refs_0_.3) | copy-start | bytes 786436
  42.4 6.3 %copy-start.4 = (bf16[128,1024]{1,0:T(8,128)(2,1)S(1)}, bf16[128,1024]{1,0:T(8,128)(2,1)}, u32[]{:S(2)}) copy-start(bf16[128,1024]{1,0:T(8,128)(2,1)} %refs_5_.1) | copy-start | bytes 786436
  42.4 6.3 %copy-start.5 = (s32[1,96]{1,0:T(1,128)S(1)}, s32[1,96]{1,0:T(1,128)}, u32[]{:S(2)}) copy-start(s32[1,96]{1,0:T(1,128)} %param.12) | copy-start | bytes 1156
  42.4 2.8 %collective-permute-start.15 = (f32[128,256]{1,0:T(8,128)S(1)}, f32[128,256]{1,0:T(8,128)S(1)}, u32[]{:S(2)}, u32[]{:S(2)}) collective-permute-start(f32[128,256]{1,0:T(8,128)S(1)} %get-tuple-element.23), channel_id=1, source_target_pairs={{0,1},{1,0},{2,3},{3,2},{4,5},{5,4},{6,7},{7,6},{8,9},{9,8},{10,11... | collective-permute-start | bytes 393224 | tf_op jit(solution)/shard_map/ppermute | solution.py:272
  42.5 2.8 %collective-permute-start.13 = (f32[128,128]{1,0:T(8,128)S(1)}, f32[128,128]{1,0:T(8,128)S(1)}, u32[]{:S(2)}, u32[]{:S(2)}) collective-permute-start(f32[128,128]{1,0:T(8,128)S(1)} %get-tuple-element.21), channel_id=1, source_target_pairs={{0,1},{1,0},{2,3},{3,2},{4,5},{5,4},{6,7},{7,6},{8,9},{9,8},{10,11... | collective-permute-start | bytes 196616 | tf_op jit(solution)/shard_map/ppermute | solution.py:272
  43.2 5.4 %collective-permute-start.17 = (f32[128,128]{1,0:T(8,128)S(1)}, f32[128,128]{1,0:T(8,128)S(1)}, u32[]{:S(2)}, u32[]{:S(2)}) collective-permute-start(f32[128,128]{1,0:T(8,128)S(1)} %fusion.5), channel_id=1, source_target_pairs={{0,1},{1,0},{2,3},{3,2},{4,5},{5,4},{6,7},{7,6},{8,9},{9,8},{10,11... | collective-permute-start | bytes 196616 | tf_op jit(solution)/shard_map/ppermute | solution.py:272
  45.2 3.3 %collective-permute-start.18 = (f32[128,256]{1,0:T(8,128)S(1)}, f32[128,256]{1,0:T(8,128)S(1)}, u32[]{:S(2)}, u32[]{:S(2)}) collective-permute-start(f32[128,256]{1,0:T(8,128)S(1)} %get-tuple-element.29), channel_id=1, source_target_pairs={{0,1},{1,0},{2,3},{3,2},{4,5},{5,4},{6,7},{7,6},{8,9},{9,8},{10,11... | collective-permute-start | bytes 393224 | tf_op jit(solution)/shard_map/ppermute | solution.py:272
  45.7 7.4 %collective-permute-start.16 = (bf16[128,1024]{1,0:T(8,128)(2,1)S(1)}, bf16[128,1024]{1,0:T(8,128)(2,1)S(1)}, u32[]{:S(2)}, u32[]{:S(2)}) collective-permute-start(bf16[128,1024]{1,0:T(8,128)(2,1)S(1)} %convolution_convert_fusion.1), channel_id=1, source_target_pairs={{0,4},{1,3},{4,8},{5,1},{8,12},{9,5},{12,14},{13,9},{14,10},{15,13... | collective-permute-start | bytes 786440 | tf_op jit(solution)/shard_map/ppermute | solution.py:271
  53.0 20.2 %collective-permute-start.22 = (bf16[96,128,128]{2,1,0:T(8,128)(2,1)S(1)}, bf16[96,128,128]{2,1,0:T(8,128)(2,1)S(1)}, u32[]{:S(2)}, u32[]{:S(2)}) collective-permute-start(bf16[96,128,128]{2,1,0:T(8,128)(2,1)S(1)} %tile_gradients.1.a_ref), channel_id=1, source_target_pairs={{0,1},{1,0},{2,3},{3,2},{4,5},{5,4},{6,7},{7,6},{8,9},{9,8},{10,11... | collective-permute-start | bytes 9437192 | tf_op jit(solution)/shard_map/ppermute | solution.py:272
  53.4 6.4 %collective-permute-start.23 = (bf16[128,1024]{1,0:T(8,128)(2,1)S(1)}, bf16[128,1024]{1,0:T(8,128)(2,1)S(1)}, u32[]{:S(2)}, u32[]{:S(2)}) collective-permute-start(bf16[128,1024]{1,0:T(8,128)(2,1)S(1)} %convolution_convert_fusion), channel_id=1, source_target_pairs={{0,4},{1,3},{4,8},{5,1},{8,12},{9,5},{12,14},{13,9},{14,10},{15,13... | collective-permute-start | bytes 786440 | tf_op jit(solution)/shard_map/ppermute | solution.py:271
  55.7 6.9 %collective-permute-start.19 = (bf16[128,1024]{1,0:T(8,128)(2,1)S(1)}, bf16[128,1024]{1,0:T(8,128)(2,1)S(1)}, u32[]{:S(2)}, u32[]{:S(2)}) collective-permute-start(bf16[128,1024]{1,0:T(8,128)(2,1)S(1)} %fusion.2), channel_id=1, source_target_pairs={{0,4},{1,3},{4,8},{5,1},{8,12},{9,5},{12,14},{13,9},{14,10},{15,13... | collective-permute-start | bytes 786440 | tf_op jit(solution)/shard_map/ppermute | solution.py:271
  60.1 6.4 %collective-permute-start.24 = (bf16[128,1024]{1,0:T(8,128)(2,1)S(1)}, bf16[128,1024]{1,0:T(8,128)(2,1)S(1)}, u32[]{:S(2)}, u32[]{:S(2)}) collective-permute-start(bf16[128,1024]{1,0:T(8,128)(2,1)S(1)} %fusion.4), channel_id=1, source_target_pairs={{0,4},{1,3},{4,8},{5,1},{8,12},{9,5},{12,14},{13,9},{14,10},{15,13... | collective-permute-start | bytes 786440 | tf_op jit(solution)/shard_map/ppermute | solution.py:271
  62.9 6.4 %collective-permute-start.20 = (bf16[128,1024]{1,0:T(8,128)(2,1)S(1)}, bf16[128,1024]{1,0:T(8,128)(2,1)S(1)}, u32[]{:S(2)}, u32[]{:S(2)}) collective-permute-start(bf16[128,1024]{1,0:T(8,128)(2,1)S(1)} %fusion.1), channel_id=1, source_target_pairs={{0,4},{1,3},{4,8},{5,1},{8,12},{9,5},{12,14},{13,9},{14,10},{15,13... | collective-permute-start | bytes 786440 | tf_op jit(solution)/shard_map/ppermute | solution.py:271
  66.8 6.4 %collective-permute-start.25 = (bf16[128,1024]{1,0:T(8,128)(2,1)S(1)}, bf16[128,1024]{1,0:T(8,128)(2,1)S(1)}, u32[]{:S(2)}, u32[]{:S(2)}) collective-permute-start(bf16[128,1024]{1,0:T(8,128)(2,1)S(1)} %fusion.3), channel_id=1, source_target_pairs={{0,4},{1,3},{4,8},{5,1},{8,12},{9,5},{12,14},{13,9},{14,10},{15,13... | collective-permute-start | bytes 786440 | tf_op jit(solution)/shard_map/ppermute | solution.py:271
  69.7 6.4 %collective-permute-start.21 = (bf16[128,1024]{1,0:T(8,128)(2,1)S(1)}, bf16[128,1024]{1,0:T(8,128)(2,1)S(1)}, u32[]{:S(2)}, u32[]{:S(2)}) collective-permute-start(bf16[128,1024]{1,0:T(8,128)(2,1)S(1)} %fusion), channel_id=1, source_target_pairs={{0,4},{1,3},{4,8},{5,1},{8,12},{9,5},{12,14},{13,9},{14,10},{15,13... | collective-permute-start | bytes 786440 | tf_op jit(solution)/shard_map/ppermute | solution.py:271
  73.3 2.8 %collective-permute-start.26 = (bf16[128,1024]{1,0:T(8,128)(2,1)S(1)}, bf16[128,1024]{1,0:T(8,128)(2,1)S(1)}, u32[]{:S(2)}, u32[]{:S(2)}) collective-permute-start(bf16[128,1024]{1,0:T(8,128)(2,1)S(1)} %collective-permute-done.25), channel_id=1, source_target_pairs={{0,1},{1,0},{2,3},{3,2},{4,5},{5,4},{6,7},{7,6},{8,9},{9,8},{10,11... | collective-permute-start | bytes 786440 | tf_op jit(solution)/shard_map/ppermute | solution.py:272

commit v5 on v4

--- a/solution.py
+++ b/solution.py
@@ -321,18 +321,21 @@
     for d in range(half + 1, n):
         if d > half + 1:
             run_s = hop((term(dgu_s, d) + run_s.astype(F32)).astype(BF))
+        if d == half + 2:
+            own = term(dgu_m, 0)
+            run_m, own = lax.optimization_barrier((run_m, own))
         run_m = hop((term(dgu_m, d) + run_m.astype(F32)).astype(BF))
     back = swap(run_s)
 
     grads = sum_grads(grads, other)
     run_m, grads = lax.optimization_barrier((run_m, grads))
-    dx = term(dgu_m, 0) + run_m.astype(F32) + back.astype(F32)
+    dx = own + run_m.astype(F32) + back.astype(F32)
     return dx.astype(BF), grads[None]
 
 
 def on_device(tokens, cotangent, fwd_values, *rest, n, cores):
     width, edge = tokens.shape[1], fwd_values.shape[-1]
-    if cores == 2 and n % 2 == 0 and 4 <= n <= 16 and width % edge == 0:
+    if cores == 2 and n % 2 == 0 and 6 <= n <= 16 and width % edge == 0:
         return ring_plan(tokens, cotangent, fwd_values, *rest, n=n)
     return gather_plan(tokens, cotangent, fwd_values, *rest)
 

time: 77.5 us -> 77.5 us (level)
  starting transfers between devices: 46 us -> 44.3 us
  Pallas kernels: 8.28 us -> 9.68 us
  other arithmetic: 0.25 us -> 1.07 us
    ppermute x19, starting transfers between devices: 43.5 us -> 41.7 us  [ring_plan(): hop = lambda v: lax.ppermute(v, axes, perm)]
    pallas_call x1, Pallas kernels: 1.85 us -> 3.24 us  [place(): pl.pallas_call(functools.partial(place_kernel, n=n, blocks=blocks, edge=e...]
    ppermute x1, starting transfers between devices: 0.37 us -> 1.38 us  [ring_plan(): lax.ppermute(cotangent, axes, cross)]
    ppermute x1, starting transfers between devices: 1.38 us -> 0.37 us  [ring_plan(): lax.ppermute(tokens, axes, cross)]
    convert_element_type x0 -> x1, other arithmetic: none -> 0.81 us  [ring_plan(): return (dx.astype(BF), grads[None])]
  transfers between devices with their start and end apart: 27 -> 27, of which waited for: 10 -> 13; matrix products, arithmetic and copies ran while one was open for 4% -> 4% of each run, Pallas kernels for 11% -> 13%
where the time goes in v5:
time: 77.5 us; the launch traced here: 76.8 us
  starting transfers between devices  44.3 us (57%)
  waiting for transfers between devices  12.6 us (16%)
  Pallas kernels  9.68 us (12%)
  local copies, waits for them, and re-layouts  4.07 us (5%)
  matrix products  2.89 us (4%)
  between operations  2.21 us (3%)
  other arithmetic  1.07 us (1%)
    ppermute x19, starting transfers between devices, ring_plan(): hop = lambda v: lax.ppermute(v, axes, perm)  41.7 us
    ppermute x19, waiting for transfers between devices, ring_plan(): hop = lambda v: lax.ppermute(v, axes, perm)  12.6 us
    unnamed x14, local copies, waits for them, and re-layouts  4.07 us
    pallas_call x1, Pallas kernels, tile_grads(): pl.pallas_call(functools.partial(grads_kernel, half=half, blocks=blocks,...  3.26 us
    pallas_call x1, Pallas kernels, place(): pl.pallas_call(functools.partial(place_kernel, n=n, blocks=blocks, edge=e...  3.24 us
    dot_general x8, matrix products, term(): lax.dot_general(dgu, rows, (((1,), (1,)), ((), ())), preferred_element_ty...  2.44 us
    pallas_call x1, Pallas kernels, sum_grads(): pl.pallas_call(sum_kernel, grid=(slots // size,), in_specs=[pl.BlockSpec(...  2.04 us
  transfers between devices with their start and end apart: 27, of which 13 were waited for; matrix products, arithmetic and copies ran while one was open for 4% of the time, Pallas kernels for 13%

profile of v5, /device:TPU:0, one launch (start us, length us, event | category | flops | bytes accessed | tf_op | source)
XLA Modules:
  0.0 76.8 jit_solution(2718958370517122133)
XLA Ops:
  0.6 3.1 %collective-permute-start.3 = (bf16[128,1024]{1,0:T(8,128)(2,1)}, bf16[128,1024]{1,0:T(8,128)(2,1)S(1)}, u32[]{:S(2)}, u32[]{:S(2)}) collective-permute-start(bf16[128,1024]{1,0:T(8,128)(2,1)} %refs_5_.1), channel_id=1, source_target_pairs={{0,4},{1,3},{4,8},{5,1},{8,12},{9,5},{12,14},{13,9},{14,10},{15,13... | collective-permute-start | bytes 786440 | tf_op jit(solution)/shard_map/ppermute | solution.py:271
  3.7 1.6 %collective-permute-start = (bf16[128,1024]{1,0:T(8,128)(2,1)}, bf16[128,1024]{1,0:T(8,128)(2,1)S(1)}, u32[]{:S(2)}, u32[]{:S(2)}) collective-permute-start(bf16[128,1024]{1,0:T(8,128)(2,1)} %refs_0_.3), channel_id=1, source_target_pairs={{0,4},{1,3},{4,8},{5,1},{8,12},{9,5},{12,14},{13,9},{14,10},{15,13... | collective-permute-start | bytes 786440 | tf_op jit(solution)/shard_map/ppermute | solution.py:271
  5.3 0.4 collective-permute-start.6
  5.7 1.4 %collective-permute-start.9 = (bf16[128,1024]{1,0:T(8,128)(2,1)}, bf16[128,1024]{1,0:T(8,128)(2,1)S(1)}, u32[]{:S(2)}, u32[]{:S(2)}) collective-permute-start(bf16[128,1024]{1,0:T(8,128)(2,1)} %refs_5_.1), channel_id=1, source_target_pairs={{1,4},{0,3},{5,8},{4,1},{9,12},{8,5},{13,14},{12,9},{15,10},{14,13... | collective-permute-start | bytes 786440 | tf_op jit(solution)/shard_map/ppermute | solution.py:289
  7.0 1.2 %collective-permute-done.3.refs_5_.refs_6_ = bf16[128,1024]{1,0:T(8,128)(2,1)S(1)} collective-permute-done((bf16[128,1024]{1,0:T(8,128)(2,1)}, bf16[128,1024]{1,0:T(8,128)(2,1)S(1)}, u32[]{:S(2)}, u32[]{:S(2)}) %collective-permute-start.3) | collective-permute-done | bytes 262176 | tf_op jit(solution)/shard_map/ppermute | solution.py:271
  8.2 2.3 %collective-permute-start.4 = (bf16[128,1024]{1,0:T(8,128)(2,1)S(1)}, bf16[128,1024]{1,0:T(8,128)(2,1)S(1)}, u32[]{:S(2)}, u32[]{:S(2)}) collective-permute-start(bf16[128,1024]{1,0:T(8,128)(2,1)S(1)} %collective-permute-done.3.refs_5_.refs_6_), channel_id=1, source_target_pairs={{0,4},{1,3},{4,8},{5,1},{8,12},{9,5},{12,14},{13,9},{14,10},{15,13... | collective-permute-start | bytes 786440 | tf_op jit(solution)/shard_map/ppermute | solution.py:271
  11.1 0.1 pad_add_fusion.here_ref
  11.2 1.5 %copy-done = bf16[1,56,128,128]{3,2,1,0:T(8,128)(2,1)S(1)} copy-done((bf16[1,56,128,128]{3,2,1,0:T(8,128)(2,1)S(1)}, bf16[1,56,128,128]{3,2,1,0:T(8,128)(2,1)}, u32[]{:S(2)}) %copy-start) | copy-done | bytes 1835032
  12.7 0.7 copy-done.6
  13.3 3.2 %place_weights.1 = (bf16[8192,256]{1,0:T(8,128)(2,1)S(1)}, bf16[8192,128]{1,0:T(8,128)(2,1)S(1)}) custom-call(s32[2]{0:T(128)S(1)} %pad_add_fusion.here_ref, s32[56]{0:T(128)S(1)} %bitcast.14, s32[1]{0:T(128)S(6)} %copy.11.cnt_ref, bf16[56,128,128]{2,1,0:T(8,128)(2,1)S(1)} %bitcast.12), custom_call_target="tpu_custom_call" | custom-call | flops 1 | bytes 1 | tf_op jit(solution)/shard_map/place_weights/pallas_call | solution.py:131
  16.6 0.6 collective-permute-start.1
  17.2 4.2 %collective-permute-start.7 = (bf16[128,1024]{1,0:T(8,128)(2,1)S(1)}, bf16[128,1024]{1,0:T(8,128)(2,1)S(1)}, u32[]{:S(2)}, u32[]{:S(2)}) collective-permute-start(bf16[128,1024]{1,0:T(8,128)(2,1)S(1)} %collective-permute-done.6.refs_8_.refs_10_), channel_id=1, source_target_pairs={{0,4},{1,3},{4,8},{5,1},{8,12},{9,5},{12,14},{13,9},{14,10},{15,13... | collective-permute-start | bytes 786440 | tf_op jit(solution)/shard_map/ppermute | solution.py:271
  21.5 0.8 collective-permute-start.10
  22.2 2.6 %collective-permute-start.5 = (bf16[128,1024]{1,0:T(8,128)(2,1)S(1)}, bf16[128,1024]{1,0:T(8,128)(2,1)S(1)}, u32[]{:S(2)}, u32[]{:S(2)}) collective-permute-start(bf16[128,1024]{1,0:T(8,128)(2,1)S(1)} %collective-permute-done.4.refs_6_.refs_7_), channel_id=1, source_target_pairs={{0,4},{1,3},{4,8},{5,1},{8,12},{9,5},{12,14},{13,9},{14,10},{15,13... | collective-permute-start | bytes 786440 | tf_op jit(solution)/shard_map/ppermute | solution.py:271
  24.9 0.5 collective-permute-start.2
  25.3 0.5 collective-permute-done.7.refs_9_.refs_11_
  25.8 2.3 %collective-permute-start.8 = (bf16[128,1024]{1,0:T(8,128)(2,1)S(1)}, bf16[128,1024]{1,0:T(8,128)(2,1)S(1)}, u32[]{:S(2)}, u32[]{:S(2)}) collective-permute-start(bf16[128,1024]{1,0:T(8,128)(2,1)S(1)} %collective-permute-done.7.refs_9_.refs_11_), channel_id=1, source_target_pairs={{0,4},{1,3},{4,8},{5,1},{8,12},{9,5},{12,14},{13,9},{14,10},{15,13... | collective-permute-start | bytes 786440 | tf_op jit(solution)/shard_map/ppermute | solution.py:271
  28.2 0.5 collective-permute-done.10.refs_12_.refs_14_
  28.6 2.3 %collective-permute-start.11 = (bf16[128,1024]{1,0:T(8,128)(2,1)S(1)}, bf16[128,1024]{1,0:T(8,128)(2,1)S(1)}, u32[]{:S(2)}, u32[]{:S(2)}) collective-permute-start(bf16[128,1024]{1,0:T(8,128)(2,1)S(1)} %collective-permute-done.10.refs_12_.refs_14_), channel_id=1, source_target_pairs={{0,4},{1,3},{4,8},{5,1},{8,12},{9,5},{12,14},{13,9},{14,10},{15,13... | collective-permute-start | bytes 786440 | tf_op jit(solution)/shard_map/ppermute | solution.py:271
  31.0 0.5 collective-permute-done.5.refs_7_.refs_8_
  31.4 2.3 %collective-permute-start.12 = (bf16[128,1024]{1,0:T(8,128)(2,1)S(1)}, bf16[128,1024]{1,0:T(8,128)(2,1)S(1)}, u32[]{:S(2)}, u32[]{:S(2)}) collective-permute-start(bf16[128,1024]{1,0:T(8,128)(2,1)S(1)} %collective-permute-done.5.refs_7_.refs_8_), channel_id=1, source_target_pairs={{0,4},{1,3},{4,8},{5,1},{8,12},{9,5},{12,14},{13,9},{14,10},{15,13... | collective-permute-start | bytes 786440 | tf_op jit(solution)/shard_map/ppermute | solution.py:271
  33.8 0.5 collective-permute-done.2.refs_3_
  34.3 2.3 %collective-permute-start.14 = (bf16[128,1024]{1,0:T(8,128)(2,1)S(1)}, bf16[128,1024]{1,0:T(8,128)(2,1)S(1)}, u32[]{:S(2)}, u32[]{:S(2)}) collective-permute-start(bf16[128,1024]{1,0:T(8,128)(2,1)S(1)} %collective-permute-done.2.refs_3_), channel_id=1, source_target_pairs={{0,4},{1,3},{4,8},{5,1},{8,12},{9,5},{12,14},{13,9},{14,10},{15,13... | collective-permute-start | bytes 786440 | tf_op jit(solution)/shard_map/ppermute | solution.py:271
  37.2 2.6 %collective-permute-done.11.refs_13_.refs_15_ = bf16[128,1024]{1,0:T(8,128)(2,1)S(1)} collective-permute-done((bf16[128,1024]{1,0:T(8,128)(2,1)S(1)}, bf16[128,1024]{1,0:T(8,128)(2,1)S(1)}, u32[]{:S(2)}, u32[]{:S(2)}) %collective-permute-start.11) | collective-permute-done | bytes 262176 | tf_op jit(solution)/shard_map/ppermute | solution.py:271
  39.9 0.9 %copy-done.1 = bf16[128,1024]{1,0:T(8,128)(2,1)S(1)} copy-done((bf16[128,1024]{1,0:T(8,128)(2,1)S(1)}, bf16[128,1024]{1,0:T(8,128)(2,1)}, u32[]{:S(2)}) %copy-start.1) | copy-done | bytes 262168
  40.8 0.9 %copy-done.3 = bf16[128,1024]{1,0:T(8,128)(2,1)S(1)} copy-done((bf16[128,1024]{1,0:T(8,128)(2,1)S(1)}, bf16[128,1024]{1,0:T(8,128)(2,1)}, u32[]{:S(2)}) %copy-start.3) | copy-done | bytes 262168
  41.8 1.1 %forward_terms.1 = (f32[128,256]{1,0:T(8,128)S(1)}, f32[128,128]{1,0:T(8,128)S(1)}, f32[128,256]{1,0:T(8,128)S(1)}, f32[128,128]{1,0:T(8,128)S(1)}) custom-call(bf16[128,1024]{1,0:T(8,128)(2,1)S(1)} %copy-done.1, bf16[128,1024]{1,0:T(8,128)(2,1)S(1)} %collective-permute-done.refs_1_, bf16[128,1024]{1,0:T(8,128)(2,1)S(1)} %collective-permute-done.1.refs_2_, ...), custom_call_target="tpu_custom_call" | custom-call | flops 1 | bytes 1 | tf_op jit(solution)/shard_map/forward_terms/pallas_call | solution.py:171
  42.9 0.0 copy-start.2
  42.9 0.0 copy-start.4
  42.9 0.0 copy-start.5
  43.0 0.1 collective-permute-start.13
  43.0 0.5 collective-permute-start.15
  43.5 0.2 fusion.5
  43.8 0.1 collective-permute-start.17
  43.9 1.6 %collective-permute-done.14.refs_4_ = bf16[128,1024]{1,0:T(8,128)(2,1)S(1)} collective-permute-done((bf16[128,1024]{1,0:T(8,128)(2,1)S(1)}, bf16[128,1024]{1,0:T(8,128)(2,1)S(1)}, u32[]{:S(2)}, u32[]{:S(2)}) %collective-permute-start.14) | collective-permute-done | bytes 262176 | tf_op jit(solution)/shard_map/ppermute | solution.py:271
  45.5 0.2 fusion.15
  45.8 0.1 collective-permute-start.18
  45.9 0.1 multiply_convert_fusion.5
  45.9 0.3 convolution_convert_fusion.1
  46.2 2.4 %collective-permute-start.16 = (bf16[128,1024]{1,0:T(8,128)(2,1)S(1)}, bf16[128,1024]{1,0:T(8,128)(2,1)S(1)}, u32[]{:S(2)}, u32[]{:S(2)}) collective-permute-start(bf16[128,1024]{1,0:T(8,128)(2,1)S(1)} %convolution_convert_fusion.1), channel_id=1, source_target_pairs={{0,4},{1,3},{4,8},{5,1},{8,12},{9,5},{12,14},{13,9},{14,10},{15,13... | collective-permute-start | bytes 786440 | tf_op jit(solution)/shard_map/ppermute | solution.py:271
  48.7 0.1 multiply_convert_fusion.3
  48.8 3.3 %tile_gradients.1.a_ref = bf16[96,128,128]{2,1,0:T(8,128)(2,1)S(1)} custom-call(s32[2]{0:T(128)S(1)} %pad_add_fusion.here_ref, s32[96]{0:T(128)S(1)} %bitcast.13, s32[1]{0:T(128)S(6)} %copy.12.cnt_ref, bf16[128,1024]{1,0:T(8,128)(2,1)S(1)} %copy-done.2, bf16[128,1024]{1,0:T(8,128)(2,1)S(1)} %collective-permute-done.refs_1_, ...), custom_call_target="tpu_custom_call" | custom-call | flops 1 | bytes 1 | tf_op jit(solution)/shard_map/tile_gradients/pallas_call | solution.py:229
  52.0 0.6 collective-permute-done.16
  52.7 0.1 collective-permute-start.22
  52.8 0.3 convolution_convert_fusion
  53.1 2.4 %collective-permute-start.23 = (bf16[128,1024]{1,0:T(8,128)(2,1)S(1)}, bf16[128,1024]{1,0:T(8,128)(2,1)S(1)}, u32[]{:S(2)}, u32[]{:S(2)}) collective-permute-start(bf16[128,1024]{1,0:T(8,128)(2,1)S(1)} %convolution_convert_fusion), channel_id=1, source_target_pairs={{0,4},{1,3},{4,8},{5,1},{8,12},{9,5},{12,14},{13,9},{14,10},{15,13... | collective-permute-start | bytes 786440 | tf_op jit(solution)/shard_map/ppermute | solution.py:271
  55.5 0.3 fusion
  55.8 2.4 %collective-permute-start.19 = (bf16[128,1024]{1,0:T(8,128)(2,1)S(1)}, bf16[128,1024]{1,0:T(8,128)(2,1)S(1)}, u32[]{:S(2)}, u32[]{:S(2)}) collective-permute-start(bf16[128,1024]{1,0:T(8,128)(2,1)S(1)} %fusion), channel_id=1, source_target_pairs={{0,4},{1,3},{4,8},{5,1},{8,12},{9,5},{12,14},{13,9},{14,10},{15,13... | collective-permute-start | bytes 786440 | tf_op jit(solution)/shard_map/ppermute | solution.py:271
  58.2 1.3 %collective-permute-done.23 = bf16[128,1024]{1,0:T(8,128)(2,1)S(1)} collective-permute-done((bf16[128,1024]{1,0:T(8,128)(2,1)S(1)}, bf16[128,1024]{1,0:T(8,128)(2,1)S(1)}, u32[]{:S(2)}, u32[]{:S(2)}) %collective-permute-start.23) | collective-permute-done | bytes 262176 | tf_op jit(solution)/shard_map/ppermute | solution.py:271
  59.5 0.3 fusion.4
  59.8 2.4 %collective-permute-start.24 = (bf16[128,1024]{1,0:T(8,128)(2,1)S(1)}, bf16[128,1024]{1,0:T(8,128)(2,1)S(1)}, u32[]{:S(2)}, u32[]{:S(2)}) collective-permute-start(bf16[128,1024]{1,0:T(8,128)(2,1)S(1)} %fusion.4), channel_id=1, source_target_pairs={{0,4},{1,3},{4,8},{5,1},{8,12},{9,5},{12,14},{13,9},{14,10},{15,13... | collective-permute-start | bytes 786440 | tf_op jit(solution)/shard_map/ppermute | solution.py:271
  62.2 0.3 fusion.6
  62.5 0.3 fusion.2
  62.8 2.4 %collective-permute-start.20 = (bf16[128,1024]{1,0:T(8,128)(2,1)S(1)}, bf16[128,1024]{1,0:T(8,128)(2,1)S(1)}, u32[]{:S(2)}, u32[]{:S(2)}) collective-permute-start(bf16[128,1024]{1,0:T(8,128)(2,1)S(1)} %fusion.2), channel_id=1, source_target_pairs={{0,4},{1,3},{4,8},{5,1},{8,12},{9,5},{12,14},{13,9},{14,10},{15,13... | collective-permute-start | bytes 786440 | tf_op jit(solution)/shard_map/ppermute | solution.py:271
  65.3 1.0 %collective-permute-done.24 = bf16[128,1024]{1,0:T(8,128)(2,1)S(1)} collective-permute-done((bf16[128,1024]{1,0:T(8,128)(2,1)S(1)}, bf16[128,1024]{1,0:T(8,128)(2,1)S(1)}, u32[]{:S(2)}, u32[]{:S(2)}) %collective-permute-start.24) | collective-permute-done | bytes 262176 | tf_op jit(solution)/shard_map/ppermute | solution.py:271
  66.3 0.3 fusion.3
  66.6 2.4 %collective-permute-start.25 = (bf16[128,1024]{1,0:T(8,128)(2,1)S(1)}, bf16[128,1024]{1,0:T(8,128)(2,1)S(1)}, u32[]{:S(2)}, u32[]{:S(2)}) collective-permute-start(bf16[128,1024]{1,0:T(8,128)(2,1)S(1)} %fusion.3), channel_id=1, source_target_pairs={{0,4},{1,3},{4,8},{5,1},{8,12},{9,5},{12,14},{13,9},{14,10},{15,13... | collective-permute-start | bytes 786440 | tf_op jit(solution)/shard_map/ppermute | solution.py:271
  68.9 0.3 collective-permute-done.20
  69.3 0.3 fusion.1
  69.6 2.4 %collective-permute-start.21 = (bf16[128,1024]{1,0:T(8,128)(2,1)S(1)}, bf16[128,1024]{1,0:T(8,128)(2,1)S(1)}, u32[]{:S(2)}, u32[]{:S(2)}) collective-permute-start(bf16[128,1024]{1,0:T(8,128)(2,1)S(1)} %fusion.1), channel_id=1, source_target_pairs={{0,4},{1,3},{4,8},{5,1},{8,12},{9,5},{12,14},{13,9},{14,10},{15,13... | collective-permute-start | bytes 786440 | tf_op jit(solution)/shard_map/ppermute | solution.py:271
  72.0 1.0 %collective-permute-done.25 = bf16[128,1024]{1,0:T(8,128)(2,1)S(1)} collective-permute-done((bf16[128,1024]{1,0:T(8,128)(2,1)S(1)}, bf16[128,1024]{1,0:T(8,128)(2,1)S(1)}, u32[]{:S(2)}, u32[]{:S(2)}) %collective-permute-start.25) | collective-permute-done | bytes 262176 | tf_op jit(solution)/shard_map/ppermute | solution.py:271
  73.0 2.0 %sum_tile_gradients.1 = bf16[96,128,128]{2,1,0:T(8,128)(2,1)} custom-call(bf16[96,128,128]{2,1,0:T(8,128)(2,1)S(1)} %tile_gradients.1.a_ref, bf16[96,128,128]{2,1,0:T(8,128)(2,1)S(1)} %collective-permute-done.22.b_ref), custom_call_target="tpu_custom_call" | custom-call | flops 1 | bytes 1 | tf_op jit(solution)/shard_map/sum_tile_gradients/pallas_call | solution.py:250
  75.0 1.0 %collective-permute-done.21 = bf16[128,1024]{1,0:T(8,128)(2,1)S(1)} collective-permute-done((bf16[128,1024]{1,0:T(8,128)(2,1)S(1)}, bf16[128,1024]{1,0:T(8,128)(2,1)S(1)}, u32[]{:S(2)}, u32[]{:S(2)}) %collective-permute-start.21) | collective-permute-done | bytes 262176 | tf_op jit(solution)/shard_map/ppermute | solution.py:271
  76.0 0.8 %add_convert_fusion = bf16[128,1024]{1,0:T(8,128)(2,1)} fusion(bf16[128,1024]{1,0:T(8,128)(2,1)S(1)} %collective-permute-done.26, f32[128,1024]{1,0:T(8,128)S(1)} %fusion.6, bf16[128,1024]{1,0:T(8,128)(2,1)S(1)} %collective-permute-done.21), kind=kLoop, calls=%fused_computation.14 | loop fusion | flops 655360 | bytes 1310720 | tf_op jit(solution)/shard_map/convert_element_type | solution.py:333
  (26 shorter events, 0.1 us)
Async XLA Ops:
  0.6 7.6 %collective-permute-start.3 = (bf16[128,1024]{1,0:T(8,128)(2,1)}, bf16[128,1024]{1,0:T(8,128)(2,1)S(1)}, u32[]{:S(2)}, u32[]{:S(2)}) collective-permute-start(bf16[128,1024]{1,0:T(8,128)(2,1)} %refs_5_.1), channel_id=1, source_target_pairs={{0,4},{1,3},{4,8},{5,1},{8,12},{9,5},{12,14},{13,9},{14,10},{15,13... | collective-permute-start | bytes 786440 | tf_op jit(solution)/shard_map/ppermute | solution.py:271
  3.7 12.9 %collective-permute-start = (bf16[128,1024]{1,0:T(8,128)(2,1)}, bf16[128,1024]{1,0:T(8,128)(2,1)S(1)}, u32[]{:S(2)}, u32[]{:S(2)}) collective-permute-start(bf16[128,1024]{1,0:T(8,128)(2,1)} %refs_0_.3), channel_id=1, source_target_pairs={{0,4},{1,3},{4,8},{5,1},{8,12},{9,5},{12,14},{13,9},{14,10},{15,13... | collective-permute-start | bytes 786440 | tf_op jit(solution)/shard_map/ppermute | solution.py:271
  5.3 11.9 %collective-permute-start.6 = (bf16[128,1024]{1,0:T(8,128)(2,1)}, bf16[128,1024]{1,0:T(8,128)(2,1)S(1)}, u32[]{:S(2)}, u32[]{:S(2)}) collective-permute-start(bf16[128,1024]{1,0:T(8,128)(2,1)} %refs_0_.3), channel_id=1, source_target_pairs={{1,4},{0,3},{5,8},{4,1},{9,12},{8,5},{13,14},{12,9},{15,10},{14,13... | collective-permute-start | bytes 786440 | tf_op jit(solution)/shard_map/ppermute | solution.py:289
  5.7 15.8 %collective-permute-start.9 = (bf16[128,1024]{1,0:T(8,128)(2,1)}, bf16[128,1024]{1,0:T(8,128)(2,1)S(1)}, u32[]{:S(2)}, u32[]{:S(2)}) collective-permute-start(bf16[128,1024]{1,0:T(8,128)(2,1)} %refs_5_.1), channel_id=1, source_target_pairs={{1,4},{0,3},{5,8},{4,1},{9,12},{8,5},{13,14},{12,9},{15,10},{14,13... | collective-permute-start | bytes 786440 | tf_op jit(solution)/shard_map/ppermute | solution.py:289
  8.2 14.0 %collective-permute-start.4 = (bf16[128,1024]{1,0:T(8,128)(2,1)S(1)}, bf16[128,1024]{1,0:T(8,128)(2,1)S(1)}, u32[]{:S(2)}, u32[]{:S(2)}) collective-permute-start(bf16[128,1024]{1,0:T(8,128)(2,1)S(1)} %collective-permute-done.3.refs_5_.refs_6_), channel_id=1, source_target_pairs={{0,4},{1,3},{4,8},{5,1},{8,12},{9,5},{12,14},{13,9},{14,10},{15,13... | collective-permute-start | bytes 786440 | tf_op jit(solution)/shard_map/ppermute | solution.py:271
  11.2 1.5 %copy-start = (bf16[1,56,128,128]{3,2,1,0:T(8,128)(2,1)S(1)}, bf16[1,56,128,128]{3,2,1,0:T(8,128)(2,1)}, u32[]{:S(2)}) copy-start(bf16[1,56,128,128]{3,2,1,0:T(8,128)(2,1)} %param.9) | copy-start | bytes 5505028
  12.7 0.7 copy-start.6
  16.6 8.3 %collective-permute-start.1 = (bf16[128,1024]{1,0:T(8,128)(2,1)S(1)}, bf16[128,1024]{1,0:T(8,128)(2,1)S(1)}, u32[]{:S(2)}, u32[]{:S(2)}) collective-permute-start(bf16[128,1024]{1,0:T(8,128)(2,1)S(1)} %collective-permute-done.refs_1_), channel_id=1, source_target_pairs={{0,4},{1,3},{4,8},{5,1},{8,12},{9,5},{12,14},{13,9},{14,10},{15,13... | collective-permute-start | bytes 786440 | tf_op jit(solution)/shard_map/ppermute | solution.py:271
  17.2 8.6 %collective-permute-start.7 = (bf16[128,1024]{1,0:T(8,128)(2,1)S(1)}, bf16[128,1024]{1,0:T(8,128)(2,1)S(1)}, u32[]{:S(2)}, u32[]{:S(2)}) collective-permute-start(bf16[128,1024]{1,0:T(8,128)(2,1)S(1)} %collective-permute-done.6.refs_8_.refs_10_), channel_id=1, source_target_pairs={{0,4},{1,3},{4,8},{5,1},{8,12},{9,5},{12,14},{13,9},{14,10},{15,13... | collective-permute-start | bytes 786440 | tf_op jit(solution)/shard_map/ppermute | solution.py:271
  21.5 7.2 %collective-permute-start.10 = (bf16[128,1024]{1,0:T(8,128)(2,1)S(1)}, bf16[128,1024]{1,0:T(8,128)(2,1)S(1)}, u32[]{:S(2)}, u32[]{:S(2)}) collective-permute-start(bf16[128,1024]{1,0:T(8,128)(2,1)S(1)} %collective-permute-done.9.refs_11_.refs_13_), channel_id=1, source_target_pairs={{0,4},{1,3},{4,8},{5,1},{8,12},{9,5},{12,14},{13,9},{14,10},{15,13... | collective-permute-start | bytes 786440 | tf_op jit(solution)/shard_map/ppermute | solution.py:271
  22.2 9.2 %collective-permute-start.5 = (bf16[128,1024]{1,0:T(8,128)(2,1)S(1)}, bf16[128,1024]{1,0:T(8,128)(2,1)S(1)}, u32[]{:S(2)}, u32[]{:S(2)}) collective-permute-start(bf16[128,1024]{1,0:T(8,128)(2,1)S(1)} %collective-permute-done.4.refs_6_.refs_7_), channel_id=1, source_target_pairs={{0,4},{1,3},{4,8},{5,1},{8,12},{9,5},{12,14},{13,9},{14,10},{15,13... | collective-permute-start | bytes 786440 | tf_op jit(solution)/shard_map/ppermute | solution.py:271
  24.9 9.4 %collective-permute-start.2 = (bf16[128,1024]{1,0:T(8,128)(2,1)S(1)}, bf16[128,1024]{1,0:T(8,128)(2,1)S(1)}, u32[]{:S(2)}, u32[]{:S(2)}) collective-permute-start(bf16[128,1024]{1,0:T(8,128)(2,1)S(1)} %collective-permute-done.1.refs_2_), channel_id=1, source_target_pairs={{0,4},{1,3},{4,8},{5,1},{8,12},{9,5},{12,14},{13,9},{14,10},{15,13... | collective-permute-start | bytes 786440 | tf_op jit(solution)/shard_map/ppermute | solution.py:271
  25.8 11.4 %collective-permute-start.8 = (bf16[128,1024]{1,0:T(8,128)(2,1)S(1)}, bf16[128,1024]{1,0:T(8,128)(2,1)S(1)}, u32[]{:S(2)}, u32[]{:S(2)}) collective-permute-start(bf16[128,1024]{1,0:T(8,128)(2,1)S(1)} %collective-permute-done.7.refs_9_.refs_11_), channel_id=1, source_target_pairs={{0,4},{1,3},{4,8},{5,1},{8,12},{9,5},{12,14},{13,9},{14,10},{15,13... | collective-permute-start | bytes 786440 | tf_op jit(solution)/shard_map/ppermute | solution.py:271
  28.6 11.2 %collective-permute-start.11 = (bf16[128,1024]{1,0:T(8,128)(2,1)S(1)}, bf16[128,1024]{1,0:T(8,128)(2,1)S(1)}, u32[]{:S(2)}, u32[]{:S(2)}) collective-permute-start(bf16[128,1024]{1,0:T(8,128)(2,1)S(1)} %collective-permute-done.10.refs_12_.refs_14_), channel_id=1, source_target_pairs={{0,4},{1,3},{4,8},{5,1},{8,12},{9,5},{12,14},{13,9},{14,10},{15,13... | collective-permute-start | bytes 786440 | tf_op jit(solution)/shard_map/ppermute | solution.py:271
  31.4 12.1 %collective-permute-start.12 = (bf16[128,1024]{1,0:T(8,128)(2,1)S(1)}, bf16[128,1024]{1,0:T(8,128)(2,1)S(1)}, u32[]{:S(2)}, u32[]{:S(2)}) collective-permute-start(bf16[128,1024]{1,0:T(8,128)(2,1)S(1)} %collective-permute-done.5.refs_7_.refs_8_), channel_id=1, source_target_pairs={{0,4},{1,3},{4,8},{5,1},{8,12},{9,5},{12,14},{13,9},{14,10},{15,13... | collective-permute-start | bytes 786440 | tf_op jit(solution)/shard_map/ppermute | solution.py:271
  34.3 11.2 %collective-permute-start.14 = (bf16[128,1024]{1,0:T(8,128)(2,1)S(1)}, bf16[128,1024]{1,0:T(8,128)(2,1)S(1)}, u32[]{:S(2)}, u32[]{:S(2)}) collective-permute-start(bf16[128,1024]{1,0:T(8,128)(2,1)S(1)} %collective-permute-done.2.refs_3_), channel_id=1, source_target_pairs={{0,4},{1,3},{4,8},{5,1},{8,12},{9,5},{12,14},{13,9},{14,10},{15,13... | collective-permute-start | bytes 786440 | tf_op jit(solution)/shard_map/ppermute | solution.py:271
  39.9 1.0 %copy-start.1 = (bf16[128,1024]{1,0:T(8,128)(2,1)S(1)}, bf16[128,1024]{1,0:T(8,128)(2,1)}, u32[]{:S(2)}) copy-start(bf16[128,1024]{1,0:T(8,128)(2,1)} %refs_0_.3) | copy-start | bytes 786436
  40.8 0.9 %copy-start.3 = (bf16[128,1024]{1,0:T(8,128)(2,1)S(1)}, bf16[128,1024]{1,0:T(8,128)(2,1)}, u32[]{:S(2)}) copy-start(bf16[128,1024]{1,0:T(8,128)(2,1)} %refs_5_.1) | copy-start | bytes 786436
  42.9 5.8 %copy-start.2 = (bf16[128,1024]{1,0:T(8,128)(2,1)S(1)}, bf16[128,1024]{1,0:T(8,128)(2,1)}, u32[]{:S(2)}) copy-start(bf16[128,1024]{1,0:T(8,128)(2,1)} %refs_0_.3) | copy-start | bytes 786436
  42.9 5.8 %copy-start.4 = (bf16[128,1024]{1,0:T(8,128)(2,1)S(1)}, bf16[128,1024]{1,0:T(8,128)(2,1)}, u32[]{:S(2)}) copy-start(bf16[128,1024]{1,0:T(8,128)(2,1)} %refs_5_.1) | copy-start | bytes 786436
  42.9 5.8 %copy-start.5 = (s32[1,96]{1,0:T(1,128)S(1)}, s32[1,96]{1,0:T(1,128)}, u32[]{:S(2)}) copy-start(s32[1,96]{1,0:T(1,128)} %param.12) | copy-start | bytes 1156
  43.0 2.9 %collective-permute-start.13 = (f32[128,128]{1,0:T(8,128)S(1)}, f32[128,128]{1,0:T(8,128)S(1)}, u32[]{:S(2)}, u32[]{:S(2)}) collective-permute-start(f32[128,128]{1,0:T(8,128)S(1)} %get-tuple-element.23), channel_id=1, source_target_pairs={{0,1},{1,0},{2,3},{3,2},{4,5},{5,4},{6,7},{7,6},{8,9},{9,8},{10,11... | collective-permute-start | bytes 196616 | tf_op jit(solution)/shard_map/ppermute | solution.py:272
  43.0 2.7 %collective-permute-start.15 = (f32[128,256]{1,0:T(8,128)S(1)}, f32[128,256]{1,0:T(8,128)S(1)}, u32[]{:S(2)}, u32[]{:S(2)}) collective-permute-start(f32[128,256]{1,0:T(8,128)S(1)} %get-tuple-element.25), channel_id=1, source_target_pairs={{0,1},{1,0},{2,3},{3,2},{4,5},{5,4},{6,7},{7,6},{8,9},{9,8},{10,11... | collective-permute-start | bytes 393224 | tf_op jit(solution)/shard_map/ppermute | solution.py:272
  43.8 4.9 %collective-permute-start.17 = (f32[128,128]{1,0:T(8,128)S(1)}, f32[128,128]{1,0:T(8,128)S(1)}, u32[]{:S(2)}, u32[]{:S(2)}) collective-permute-start(f32[128,128]{1,0:T(8,128)S(1)} %fusion.5), channel_id=1, source_target_pairs={{0,1},{1,0},{2,3},{3,2},{4,5},{5,4},{6,7},{7,6},{8,9},{9,8},{10,11... | collective-permute-start | bytes 196616 | tf_op jit(solution)/shard_map/ppermute | solution.py:272
  45.8 2.8 %collective-permute-start.18 = (f32[128,256]{1,0:T(8,128)S(1)}, f32[128,256]{1,0:T(8,128)S(1)}, u32[]{:S(2)}, u32[]{:S(2)}) collective-permute-start(f32[128,256]{1,0:T(8,128)S(1)} %get-tuple-element.33), channel_id=1, source_target_pairs={{0,1},{1,0},{2,3},{3,2},{4,5},{5,4},{6,7},{7,6},{8,9},{9,8},{10,11... | collective-permute-start | bytes 393224 | tf_op jit(solution)/shard_map/ppermute | solution.py:272
  46.2 6.4 %collective-permute-start.16 = (bf16[128,1024]{1,0:T(8,128)(2,1)S(1)}, bf16[128,1024]{1,0:T(8,128)(2,1)S(1)}, u32[]{:S(2)}, u32[]{:S(2)}) collective-permute-start(bf16[128,1024]{1,0:T(8,128)(2,1)S(1)} %convolution_convert_fusion.1), channel_id=1, source_target_pairs={{0,4},{1,3},{4,8},{5,1},{8,12},{9,5},{12,14},{13,9},{14,10},{15,13... | collective-permute-start | bytes 786440 | tf_op jit(solution)/shard_map/ppermute | solution.py:271
  52.7 20.3 %collective-permute-start.22 = (bf16[96,128,128]{2,1,0:T(8,128)(2,1)S(1)}, bf16[96,128,128]{2,1,0:T(8,128)(2,1)S(1)}, u32[]{:S(2)}, u32[]{:S(2)}) collective-permute-start(bf16[96,128,128]{2,1,0:T(8,128)(2,1)S(1)} %tile_gradients.1.a_ref), channel_id=1, source_target_pairs={{0,1},{1,0},{2,3},{3,2},{4,5},{5,4},{6,7},{7,6},{8,9},{9,8},{10,11... | collective-permute-start | bytes 9437192 | tf_op jit(solution)/shard_map/ppermute | solution.py:272
  53.1 6.4 %collective-permute-start.23 = (bf16[128,1024]{1,0:T(8,128)(2,1)S(1)}, bf16[128,1024]{1,0:T(8,128)(2,1)S(1)}, u32[]{:S(2)}, u32[]{:S(2)}) collective-permute-start(bf16[128,1024]{1,0:T(8,128)(2,1)S(1)} %convolution_convert_fusion), channel_id=1, source_target_pairs={{0,4},{1,3},{4,8},{5,1},{8,12},{9,5},{12,14},{13,9},{14,10},{15,13... | collective-permute-start | bytes 786440 | tf_op jit(solution)/shard_map/ppermute | solution.py:271
  55.8 6.7 %collective-permute-start.19 = (bf16[128,1024]{1,0:T(8,128)(2,1)S(1)}, bf16[128,1024]{1,0:T(8,128)(2,1)S(1)}, u32[]{:S(2)}, u32[]{:S(2)}) collective-permute-start(bf16[128,1024]{1,0:T(8,128)(2,1)S(1)} %fusion), channel_id=1, source_target_pairs={{0,4},{1,3},{4,8},{5,1},{8,12},{9,5},{12,14},{13,9},{14,10},{15,13... | collective-permute-start | bytes 786440 | tf_op jit(solution)/shard_map/ppermute | solution.py:271
  59.8 6.4 %collective-permute-start.24 = (bf16[128,1024]{1,0:T(8,128)(2,1)S(1)}, bf16[128,1024]{1,0:T(8,128)(2,1)S(1)}, u32[]{:S(2)}, u32[]{:S(2)}) collective-permute-start(bf16[128,1024]{1,0:T(8,128)(2,1)S(1)} %fusion.4), channel_id=1, source_target_pairs={{0,4},{1,3},{4,8},{5,1},{8,12},{9,5},{12,14},{13,9},{14,10},{15,13... | collective-permute-start | bytes 786440 | tf_op jit(solution)/shard_map/ppermute | solution.py:271
  62.8 6.4 %collective-permute-start.20 = (bf16[128,1024]{1,0:T(8,128)(2,1)S(1)}, bf16[128,1024]{1,0:T(8,128)(2,1)S(1)}, u32[]{:S(2)}, u32[]{:S(2)}) collective-permute-start(bf16[128,1024]{1,0:T(8,128)(2,1)S(1)} %fusion.2), channel_id=1, source_target_pairs={{0,4},{1,3},{4,8},{5,1},{8,12},{9,5},{12,14},{13,9},{14,10},{15,13... | collective-permute-start | bytes 786440 | tf_op jit(solution)/shard_map/ppermute | solution.py:271
  66.6 6.4 %collective-permute-start.25 = (bf16[128,1024]{1,0:T(8,128)(2,1)S(1)}, bf16[128,1024]{1,0:T(8,128)(2,1)S(1)}, u32[]{:S(2)}, u32[]{:S(2)}) collective-permute-start(bf16[128,1024]{1,0:T(8,128)(2,1)S(1)} %fusion.3), channel_id=1, source_target_pairs={{0,4},{1,3},{4,8},{5,1},{8,12},{9,5},{12,14},{13,9},{14,10},{15,13... | collective-permute-start | bytes 786440 | tf_op jit(solution)/shard_map/ppermute | solution.py:271
  69.6 6.4 %collective-permute-start.21 = (bf16[128,1024]{1,0:T(8,128)(2,1)S(1)}, bf16[128,1024]{1,0:T(8,128)(2,1)S(1)}, u32[]{:S(2)}, u32[]{:S(2)}) collective-permute-start(bf16[128,1024]{1,0:T(8,128)(2,1)S(1)} %fusion.1), channel_id=1, source_target_pairs={{0,4},{1,3},{4,8},{5,1},{8,12},{9,5},{12,14},{13,9},{14,10},{15,13... | collective-permute-start | bytes 786440 | tf_op jit(solution)/shard_map/ppermute | solution.py:271
  73.0 3.0 %collective-permute-start.26 = (bf16[128,1024]{1,0:T(8,128)(2,1)S(1)}, bf16[128,1024]{1,0:T(8,128)(2,1)S(1)}, u32[]{:S(2)}, u32[]{:S(2)}) collective-permute-start(bf16[128,1024]{1,0:T(8,128)(2,1)S(1)} %collective-permute-done.25), channel_id=1, source_target_pairs={{0,1},{1,0},{2,3},{3,2},{4,5},{5,4},{6,7},{7,6},{8,9},{9,8},{10,11... | collective-permute-start | bytes 786440 | tf_op jit(solution)/shard_map/ppermute | solution.py:272

commit v6 on v5

--- a/solution.py
+++ b/solution.py
@@ -292,6 +292,9 @@
         x_m.append(hop(x_m[-1]))
         y_m.append(hop(y_m[-1]))
         if k < half:
+            if k == half - 1:
+                x_s[-1], _ = lax.optimization_barrier((x_s[-1], x_m[-1]))
+                y_s[-1], _ = lax.optimization_barrier((y_s[-1], y_m[-1]))
             x_s.append(hop(x_s[-1]))
             y_s.append(hop(y_s[-1]))
 

time: 77.5 us -> 77.4 us (level)
  waiting for transfers between devices: 12.6 us -> 18.4 us
  starting transfers between devices: 44.3 us -> 38.5 us
    ppermute x19, starting transfers between devices: 41.7 us -> 35.9 us  [ring_plan(): hop = lambda v: lax.ppermute(v, axes, perm)]
    ppermute x19, waiting for transfers between devices: 12.6 us -> 17.8 us  [ring_plan(): hop = lambda v: lax.ppermute(v, axes, perm)]
  transfers between devices with their start and end apart: 27 -> 27, of which waited for: 13 -> 14; matrix products, arithmetic and copies ran while one was open for 4% -> 4% of each run, Pallas kernels for 13% -> 13%
where the time goes in v6:
time: 77.4 us; the launch traced here: 76.9 us
  starting transfers between devices  38.5 us (50%)
  waiting for transfers between devices  18.4 us (24%)
  Pallas kernels  9.77 us (13%)
  local copies, waits for them, and re-layouts  4.07 us (5%)
  matrix products  2.9 us (4%)
  between operations  2.2 us (3%)
  other arithmetic  1.08 us (1%)
    ppermute x19, starting transfers between devices, ring_plan(): hop = lambda v: lax.ppermute(v, axes, perm)  35.9 us
    ppermute x19, waiting for transfers between devices, ring_plan(): hop = lambda v: lax.ppermute(v, axes, perm)  17.8 us
    unnamed x14, local copies, waits for them, and re-layouts  4.07 us
    pallas_call x1, Pallas kernels, place(): pl.pallas_call(functools.partial(place_kernel, n=n, blocks=blocks, edge=e...  3.38 us
    pallas_call x1, Pallas kernels, tile_grads(): pl.pallas_call(functools.partial(grads_kernel, half=half, blocks=blocks,...  3.23 us
    dot_general x8, matrix products, term(): lax.dot_general(dgu, rows, (((1,), (1,)), ((), ())), preferred_element_ty...  2.45 us
    pallas_call x1, Pallas kernels, sum_grads(): pl.pallas_call(sum_kernel, grid=(slots // size,), in_specs=[pl.BlockSpec(...  2.04 us
  transfers between devices with their start and end apart: 27, of which 14 were waited for; matrix products, arithmetic and copies ran while one was open for 4% of the time, Pallas kernels for 13%

profile of v6, /device:TPU:0, one launch (start us, length us, event | category | flops | bytes accessed | tf_op | source)
XLA Modules:
  0.0 76.9 jit_solution(1761673512129812670)
XLA Ops:
  0.6 3.1 %collective-permute-start.3 = (bf16[128,1024]{1,0:T(8,128)(2,1)}, bf16[128,1024]{1,0:T(8,128)(2,1)S(1)}, u32[]{:S(2)}, u32[]{:S(2)}) collective-permute-start(bf16[128,1024]{1,0:T(8,128)(2,1)} %refs_5_.1), channel_id=1, source_target_pairs={{0,4},{1,3},{4,8},{5,1},{8,12},{9,5},{12,14},{13,9},{14,10},{15,13... | collective-permute-start | bytes 786440 | tf_op jit(solution)/shard_map/ppermute | solution.py:271
  3.7 1.6 %collective-permute-start = (bf16[128,1024]{1,0:T(8,128)(2,1)}, bf16[128,1024]{1,0:T(8,128)(2,1)S(1)}, u32[]{:S(2)}, u32[]{:S(2)}) collective-permute-start(bf16[128,1024]{1,0:T(8,128)(2,1)} %refs_0_.3), channel_id=1, source_target_pairs={{0,4},{1,3},{4,8},{5,1},{8,12},{9,5},{12,14},{13,9},{14,10},{15,13... | collective-permute-start | bytes 786440 | tf_op jit(solution)/shard_map/ppermute | solution.py:271
  5.3 0.4 collective-permute-start.6
  5.7 1.4 %collective-permute-start.9 = (bf16[128,1024]{1,0:T(8,128)(2,1)}, bf16[128,1024]{1,0:T(8,128)(2,1)S(1)}, u32[]{:S(2)}, u32[]{:S(2)}) collective-permute-start(bf16[128,1024]{1,0:T(8,128)(2,1)} %refs_5_.1), channel_id=1, source_target_pairs={{1,4},{0,3},{5,8},{4,1},{9,12},{8,5},{13,14},{12,9},{15,10},{14,13... | collective-permute-start | bytes 786440 | tf_op jit(solution)/shard_map/ppermute | solution.py:289
  7.7 0.1 pad_add_fusion.here_ref
  7.8 1.5 %copy-done = bf16[1,56,128,128]{3,2,1,0:T(8,128)(2,1)S(1)} copy-done((bf16[1,56,128,128]{3,2,1,0:T(8,128)(2,1)S(1)}, bf16[1,56,128,128]{3,2,1,0:T(8,128)(2,1)}, u32[]{:S(2)}) %copy-start) | copy-done | bytes 1835032
  9.3 0.7 copy-done.6
  9.9 3.4 %place_weights.1 = (bf16[8192,256]{1,0:T(8,128)(2,1)S(1)}, bf16[8192,128]{1,0:T(8,128)(2,1)S(1)}) custom-call(s32[2]{0:T(128)S(1)} %pad_add_fusion.here_ref, s32[56]{0:T(128)S(1)} %bitcast.14, s32[1]{0:T(128)S(6)} %copy.11.cnt_ref, bf16[56,128,128]{2,1,0:T(8,128)(2,1)S(1)} %bitcast.12), custom_call_target="tpu_custom_call" | custom-call | flops 1 | bytes 1 | tf_op jit(solution)/shard_map/place_weights/pallas_call | solution.py:131
  13.3 2.2 %collective-permute-start.4 = (bf16[128,1024]{1,0:T(8,128)(2,1)S(1)}, bf16[128,1024]{1,0:T(8,128)(2,1)S(1)}, u32[]{:S(2)}, u32[]{:S(2)}) collective-permute-start(bf16[128,1024]{1,0:T(8,128)(2,1)S(1)} %collective-permute-done.3.refs_5_.refs_6_), channel_id=1, source_target_pairs={{0,4},{1,3},{4,8},{5,1},{8,12},{9,5},{12,14},{13,9},{14,10},{15,13... | collective-permute-start | bytes 786440 | tf_op jit(solution)/shard_map/ppermute | solution.py:271
  15.6 0.5 collective-permute-start.1
  16.1 0.5 collective-permute-done.9.refs_11_.refs_13_
  16.6 2.1 %collective-permute-start.10 = (bf16[128,1024]{1,0:T(8,128)(2,1)S(1)}, bf16[128,1024]{1,0:T(8,128)(2,1)S(1)}, u32[]{:S(2)}, u32[]{:S(2)}) collective-permute-start(bf16[128,1024]{1,0:T(8,128)(2,1)S(1)} %collective-permute-done.9.refs_11_.refs_13_), channel_id=1, source_target_pairs={{0,4},{1,3},{4,8},{5,1},{8,12},{9,5},{12,14},{13,9},{14,10},{15,13... | collective-permute-start | bytes 786440 | tf_op jit(solution)/shard_map/ppermute | solution.py:271
  18.7 1.0 %collective-permute-done.4.refs_6_.refs_7_ = bf16[128,1024]{1,0:T(8,128)(2,1)S(1)} collective-permute-done((bf16[128,1024]{1,0:T(8,128)(2,1)S(1)}, bf16[128,1024]{1,0:T(8,128)(2,1)S(1)}, u32[]{:S(2)}, u32[]{:S(2)}) %collective-permute-start.4) | collective-permute-done | bytes 262176 | tf_op jit(solution)/shard_map/ppermute | solution.py:271
  19.7 2.2 %collective-permute-start.5 = (bf16[128,1024]{1,0:T(8,128)(2,1)S(1)}, bf16[128,1024]{1,0:T(8,128)(2,1)S(1)}, u32[]{:S(2)}, u32[]{:S(2)}) collective-permute-start(bf16[128,1024]{1,0:T(8,128)(2,1)S(1)} %collective-permute-done.4.refs_6_.refs_7_), channel_id=1, source_target_pairs={{0,4},{1,3},{4,8},{5,1},{8,12},{9,5},{12,14},{13,9},{14,10},{15,13... | collective-permute-start | bytes 786440 | tf_op jit(solution)/shard_map/ppermute | solution.py:271
  21.9 1.4 %collective-permute-start.7 = (bf16[128,1024]{1,0:T(8,128)(2,1)S(1)}, bf16[128,1024]{1,0:T(8,128)(2,1)S(1)}, u32[]{:S(2)}, u32[]{:S(2)}) collective-permute-start(bf16[128,1024]{1,0:T(8,128)(2,1)S(1)} %collective-permute-done.6.refs_8_.refs_10_), channel_id=1, source_target_pairs={{0,4},{1,3},{4,8},{5,1},{8,12},{9,5},{12,14},{13,9},{14,10},{15,13... | collective-permute-start | bytes 786440 | tf_op jit(solution)/shard_map/ppermute | solution.py:271
  23.3 1.4 %collective-permute-start.2 = (bf16[128,1024]{1,0:T(8,128)(2,1)S(1)}, bf16[128,1024]{1,0:T(8,128)(2,1)S(1)}, u32[]{:S(2)}, u32[]{:S(2)}) collective-permute-start(bf16[128,1024]{1,0:T(8,128)(2,1)S(1)} %collective-permute-done.1.refs_2_), channel_id=1, source_target_pairs={{0,4},{1,3},{4,8},{5,1},{8,12},{9,5},{12,14},{13,9},{14,10},{15,13... | collective-permute-start | bytes 786440 | tf_op jit(solution)/shard_map/ppermute | solution.py:271
  24.7 0.6 collective-permute-done.10.refs_12_.refs_14_
  25.4 2.8 %collective-permute-done.5.refs_7_.refs_8_ = bf16[128,1024]{1,0:T(8,128)(2,1)S(1)} collective-permute-done((bf16[128,1024]{1,0:T(8,128)(2,1)S(1)}, bf16[128,1024]{1,0:T(8,128)(2,1)S(1)}, u32[]{:S(2)}, u32[]{:S(2)}) %collective-permute-start.5) | collective-permute-done | bytes 262176 | tf_op jit(solution)/shard_map/ppermute | solution.py:271
  28.2 2.2 %collective-permute-start.11 = (bf16[128,1024]{1,0:T(8,128)(2,1)S(1)}, bf16[128,1024]{1,0:T(8,128)(2,1)S(1)}, u32[]{:S(2)}, u32[]{:S(2)}) collective-permute-start(bf16[128,1024]{1,0:T(8,128)(2,1)S(1)} %collective-permute-done.10.refs_12_.refs_14_), channel_id=1, source_target_pairs={{0,4},{1,3},{4,8},{5,1},{8,12},{9,5},{12,14},{13,9},{14,10},{15,13... | collective-permute-start | bytes 786440 | tf_op jit(solution)/shard_map/ppermute | solution.py:271
  30.4 0.6 collective-permute-done.7.refs_9_.refs_11_
  31.0 2.8 %collective-permute-done.2.refs_3_ = bf16[128,1024]{1,0:T(8,128)(2,1)S(1)} collective-permute-done((bf16[128,1024]{1,0:T(8,128)(2,1)S(1)}, bf16[128,1024]{1,0:T(8,128)(2,1)S(1)}, u32[]{:S(2)}, u32[]{:S(2)}) %collective-permute-start.2) | collective-permute-done | bytes 262176 | tf_op jit(solution)/shard_map/ppermute | solution.py:271
  33.8 2.2 %collective-permute-start.8 = (bf16[128,1024]{1,0:T(8,128)(2,1)S(1)}, bf16[128,1024]{1,0:T(8,128)(2,1)S(1)}, u32[]{:S(2)}, u32[]{:S(2)}) collective-permute-start(bf16[128,1024]{1,0:T(8,128)(2,1)S(1)} %collective-permute-done.7.refs_9_.refs_11_), channel_id=1, source_target_pairs={{0,4},{1,3},{4,8},{5,1},{8,12},{9,5},{12,14},{13,9},{14,10},{15,13... | collective-permute-start | bytes 786440 | tf_op jit(solution)/shard_map/ppermute | solution.py:271
  36.0 1.2 %collective-permute-start.12 = (bf16[128,1024]{1,0:T(8,128)(2,1)S(1)}, bf16[128,1024]{1,0:T(8,128)(2,1)S(1)}, u32[]{:S(2)}, u32[]{:S(2)}) collective-permute-start(bf16[128,1024]{1,0:T(8,128)(2,1)S(1)} %collective-permute-done.5.refs_7_.refs_8_), channel_id=1, source_target_pairs={{0,4},{1,3},{4,8},{5,1},{8,12},{9,5},{12,14},{13,9},{14,10},{15,13... | collective-permute-start | bytes 786440 | tf_op jit(solution)/shard_map/ppermute | solution.py:271
  37.1 1.6 %collective-permute-start.14 = (bf16[128,1024]{1,0:T(8,128)(2,1)S(1)}, bf16[128,1024]{1,0:T(8,128)(2,1)S(1)}, u32[]{:S(2)}, u32[]{:S(2)}) collective-permute-start(bf16[128,1024]{1,0:T(8,128)(2,1)S(1)} %collective-permute-done.2.refs_3_), channel_id=1, source_target_pairs={{0,4},{1,3},{4,8},{5,1},{8,12},{9,5},{12,14},{13,9},{14,10},{15,13... | collective-permute-start | bytes 786440 | tf_op jit(solution)/shard_map/ppermute | solution.py:271
  39.4 0.8 %collective-permute-done.8.refs_10_.refs_12_ = bf16[128,1024]{1,0:T(8,128)(2,1)S(1)} collective-permute-done((bf16[128,1024]{1,0:T(8,128)(2,1)S(1)}, bf16[128,1024]{1,0:T(8,128)(2,1)S(1)}, u32[]{:S(2)}, u32[]{:S(2)}) %collective-permute-start.8) | collective-permute-done | bytes 262176 | tf_op jit(solution)/shard_map/ppermute | solution.py:271
  40.2 0.9 %copy-done.1 = bf16[128,1024]{1,0:T(8,128)(2,1)S(1)} copy-done((bf16[128,1024]{1,0:T(8,128)(2,1)S(1)}, bf16[128,1024]{1,0:T(8,128)(2,1)}, u32[]{:S(2)}) %copy-start.1) | copy-done | bytes 262168
  41.1 0.9 %copy-done.3 = bf16[128,1024]{1,0:T(8,128)(2,1)S(1)} copy-done((bf16[128,1024]{1,0:T(8,128)(2,1)S(1)}, bf16[128,1024]{1,0:T(8,128)(2,1)}, u32[]{:S(2)}) %copy-start.3) | copy-done | bytes 262168
  42.1 1.1 %forward_terms.1 = (f32[128,256]{1,0:T(8,128)S(1)}, f32[128,128]{1,0:T(8,128)S(1)}, f32[128,256]{1,0:T(8,128)S(1)}, f32[128,128]{1,0:T(8,128)S(1)}) custom-call(bf16[128,1024]{1,0:T(8,128)(2,1)S(1)} %copy-done.1, bf16[128,1024]{1,0:T(8,128)(2,1)S(1)} %collective-permute-done.refs_1_, bf16[128,1024]{1,0:T(8,128)(2,1)S(1)} %collective-permute-done.1.refs_2_, ...), custom_call_target="tpu_custom_call" | custom-call | flops 1 | bytes 1 | tf_op jit(solution)/shard_map/forward_terms/pallas_call | solution.py:171
  43.2 0.0 copy-start.2
  43.2 0.2 fusion.5
  43.5 0.1 collective-permute-start.17
  43.5 0.5 collective-permute-start.13
  44.0 0.1 collective-permute-start.15
  44.1 1.7 %collective-permute-done.14.refs_4_ = bf16[128,1024]{1,0:T(8,128)(2,1)S(1)} collective-permute-done((bf16[128,1024]{1,0:T(8,128)(2,1)S(1)}, bf16[128,1024]{1,0:T(8,128)(2,1)S(1)}, u32[]{:S(2)}, u32[]{:S(2)}) %collective-permute-start.14) | collective-permute-done | bytes 262176 | tf_op jit(solution)/shard_map/ppermute | solution.py:271
  45.8 0.2 fusion.15
  46.1 0.1 collective-permute-start.18
  46.1 0.1 multiply_convert_fusion.5
  46.2 0.3 convolution_convert_fusion.1
  46.5 2.2 %collective-permute-start.16 = (bf16[128,1024]{1,0:T(8,128)(2,1)S(1)}, bf16[128,1024]{1,0:T(8,128)(2,1)S(1)}, u32[]{:S(2)}, u32[]{:S(2)}) collective-permute-start(bf16[128,1024]{1,0:T(8,128)(2,1)S(1)} %convolution_convert_fusion.1), channel_id=1, source_target_pairs={{0,4},{1,3},{4,8},{5,1},{8,12},{9,5},{12,14},{13,9},{14,10},{15,13... | collective-permute-start | bytes 786440 | tf_op jit(solution)/shard_map/ppermute | solution.py:271
  48.8 0.1 multiply_convert_fusion.3
  48.9 3.2 %tile_gradients.1.a_ref = bf16[96,128,128]{2,1,0:T(8,128)(2,1)S(1)} custom-call(s32[2]{0:T(128)S(1)} %pad_add_fusion.here_ref, s32[96]{0:T(128)S(1)} %bitcast.13, s32[1]{0:T(128)S(6)} %copy.12.cnt_ref, bf16[128,1024]{1,0:T(8,128)(2,1)S(1)} %copy-done.2, bf16[128,1024]{1,0:T(8,128)(2,1)S(1)} %collective-permute-done.refs_1_, ...), custom_call_target="tpu_custom_call" | custom-call | flops 1 | bytes 1 | tf_op jit(solution)/shard_map/tile_gradients/pallas_call | solution.py:229
  52.2 0.8 %collective-permute-done.16 = bf16[128,1024]{1,0:T(8,128)(2,1)S(1)} collective-permute-done((bf16[128,1024]{1,0:T(8,128)(2,1)S(1)}, bf16[128,1024]{1,0:T(8,128)(2,1)S(1)}, u32[]{:S(2)}, u32[]{:S(2)}) %collective-permute-start.16) | collective-permute-done | bytes 262176 | tf_op jit(solution)/shard_map/ppermute | solution.py:271
  53.0 0.1 collective-permute-start.22
  53.0 0.3 convolution_convert_fusion
  53.4 2.2 %collective-permute-start.23 = (bf16[128,1024]{1,0:T(8,128)(2,1)S(1)}, bf16[128,1024]{1,0:T(8,128)(2,1)S(1)}, u32[]{:S(2)}, u32[]{:S(2)}) collective-permute-start(bf16[128,1024]{1,0:T(8,128)(2,1)S(1)} %convolution_convert_fusion), channel_id=1, source_target_pairs={{0,4},{1,3},{4,8},{5,1},{8,12},{9,5},{12,14},{13,9},{14,10},{15,13... | collective-permute-start | bytes 786440 | tf_op jit(solution)/shard_map/ppermute | solution.py:271
  55.5 0.3 fusion
  55.8 1.2 %collective-permute-start.19 = (bf16[128,1024]{1,0:T(8,128)(2,1)S(1)}, bf16[128,1024]{1,0:T(8,128)(2,1)S(1)}, u32[]{:S(2)}, u32[]{:S(2)}) collective-permute-start(bf16[128,1024]{1,0:T(8,128)(2,1)S(1)} %fusion), channel_id=1, source_target_pairs={{0,4},{1,3},{4,8},{5,1},{8,12},{9,5},{12,14},{13,9},{14,10},{15,13... | collective-permute-start | bytes 786440 | tf_op jit(solution)/shard_map/ppermute | solution.py:271
  57.1 2.7 %collective-permute-done.23 = bf16[128,1024]{1,0:T(8,128)(2,1)S(1)} collective-permute-done((bf16[128,1024]{1,0:T(8,128)(2,1)S(1)}, bf16[128,1024]{1,0:T(8,128)(2,1)S(1)}, u32[]{:S(2)}, u32[]{:S(2)}) %collective-permute-start.23) | collective-permute-done | bytes 262176 | tf_op jit(solution)/shard_map/ppermute | solution.py:271
  59.8 0.3 fusion.4
  60.1 2.2 %collective-permute-start.24 = (bf16[128,1024]{1,0:T(8,128)(2,1)S(1)}, bf16[128,1024]{1,0:T(8,128)(2,1)S(1)}, u32[]{:S(2)}, u32[]{:S(2)}) collective-permute-start(bf16[128,1024]{1,0:T(8,128)(2,1)S(1)} %fusion.4), channel_id=1, source_target_pairs={{0,4},{1,3},{4,8},{5,1},{8,12},{9,5},{12,14},{13,9},{14,10},{15,13... | collective-permute-start | bytes 786440 | tf_op jit(solution)/shard_map/ppermute | solution.py:271
  62.3 0.3 fusion.6
  62.6 0.0 collective-permute-done.19
  62.6 0.3 fusion.2
  62.9 2.2 %collective-permute-start.20 = (bf16[128,1024]{1,0:T(8,128)(2,1)S(1)}, bf16[128,1024]{1,0:T(8,128)(2,1)S(1)}, u32[]{:S(2)}, u32[]{:S(2)}) collective-permute-start(bf16[128,1024]{1,0:T(8,128)(2,1)S(1)} %fusion.2), channel_id=1, source_target_pairs={{0,4},{1,3},{4,8},{5,1},{8,12},{9,5},{12,14},{13,9},{14,10},{15,13... | collective-permute-start | bytes 786440 | tf_op jit(solution)/shard_map/ppermute | solution.py:271
  65.1 1.4 %collective-permute-done.24 = bf16[128,1024]{1,0:T(8,128)(2,1)S(1)} collective-permute-done((bf16[128,1024]{1,0:T(8,128)(2,1)S(1)}, bf16[128,1024]{1,0:T(8,128)(2,1)S(1)}, u32[]{:S(2)}, u32[]{:S(2)}) %collective-permute-start.24) | collective-permute-done | bytes 262176 | tf_op jit(solution)/shard_map/ppermute | solution.py:271
  66.5 0.3 fusion.3
  66.8 2.2 %collective-permute-start.25 = (bf16[128,1024]{1,0:T(8,128)(2,1)S(1)}, bf16[128,1024]{1,0:T(8,128)(2,1)S(1)}, u32[]{:S(2)}, u32[]{:S(2)}) collective-permute-start(bf16[128,1024]{1,0:T(8,128)(2,1)S(1)} %fusion.3), channel_id=1, source_target_pairs={{0,4},{1,3},{4,8},{5,1},{8,12},{9,5},{12,14},{13,9},{14,10},{15,13... | collective-permute-start | bytes 786440 | tf_op jit(solution)/shard_map/ppermute | solution.py:271
  69.0 0.3 collective-permute-done.20
  69.3 0.3 fusion.1
  69.6 2.2 %collective-permute-start.21 = (bf16[128,1024]{1,0:T(8,128)(2,1)S(1)}, bf16[128,1024]{1,0:T(8,128)(2,1)S(1)}, u32[]{:S(2)}, u32[]{:S(2)}) collective-permute-start(bf16[128,1024]{1,0:T(8,128)(2,1)S(1)} %fusion.1), channel_id=1, source_target_pairs={{0,4},{1,3},{4,8},{5,1},{8,12},{9,5},{12,14},{13,9},{14,10},{15,13... | collective-permute-start | bytes 786440 | tf_op jit(solution)/shard_map/ppermute | solution.py:271
  71.8 1.4 %collective-permute-done.25 = bf16[128,1024]{1,0:T(8,128)(2,1)S(1)} collective-permute-done((bf16[128,1024]{1,0:T(8,128)(2,1)S(1)}, bf16[128,1024]{1,0:T(8,128)(2,1)S(1)}, u32[]{:S(2)}, u32[]{:S(2)}) %collective-permute-start.25) | collective-permute-done | bytes 262176 | tf_op jit(solution)/shard_map/ppermute | solution.py:271
  73.3 2.0 %sum_tile_gradients.1 = bf16[96,128,128]{2,1,0:T(8,128)(2,1)} custom-call(bf16[96,128,128]{2,1,0:T(8,128)(2,1)S(1)} %tile_gradients.1.a_ref, bf16[96,128,128]{2,1,0:T(8,128)(2,1)S(1)} %collective-permute-done.22.b_ref), custom_call_target="tpu_custom_call" | custom-call | flops 1 | bytes 1 | tf_op jit(solution)/shard_map/sum_tile_gradients/pallas_call | solution.py:250
  75.3 0.8 collective-permute-done.21
  76.1 0.8 %add_convert_fusion = bf16[128,1024]{1,0:T(8,128)(2,1)} fusion(bf16[128,1024]{1,0:T(8,128)(2,1)S(1)} %collective-permute-done.26, f32[128,1024]{1,0:T(8,128)S(1)} %fusion.6, bf16[128,1024]{1,0:T(8,128)(2,1)S(1)} %collective-permute-done.21), kind=kLoop, calls=%fused_computation.14 | loop fusion | flops 655360 | bytes 1310720 | tf_op jit(solution)/shard_map/convert_element_type | solution.py:336
  (26 shorter events, 0.1 us)
Async XLA Ops:
  0.6 12.7 %collective-permute-start.3 = (bf16[128,1024]{1,0:T(8,128)(2,1)}, bf16[128,1024]{1,0:T(8,128)(2,1)S(1)}, u32[]{:S(2)}, u32[]{:S(2)}) collective-permute-start(bf16[128,1024]{1,0:T(8,128)(2,1)} %refs_5_.1), channel_id=1, source_target_pairs={{0,4},{1,3},{4,8},{5,1},{8,12},{9,5},{12,14},{13,9},{14,10},{15,13... | collective-permute-start | bytes 786440 | tf_op jit(solution)/shard_map/ppermute | solution.py:271
  3.7 11.9 %collective-permute-start = (bf16[128,1024]{1,0:T(8,128)(2,1)}, bf16[128,1024]{1,0:T(8,128)(2,1)S(1)}, u32[]{:S(2)}, u32[]{:S(2)}) collective-permute-start(bf16[128,1024]{1,0:T(8,128)(2,1)} %refs_0_.3), channel_id=1, source_target_pairs={{0,4},{1,3},{4,8},{5,1},{8,12},{9,5},{12,14},{13,9},{14,10},{15,13... | collective-permute-start | bytes 786440 | tf_op jit(solution)/shard_map/ppermute | solution.py:271
  5.3 16.7 %collective-permute-start.6 = (bf16[128,1024]{1,0:T(8,128)(2,1)}, bf16[128,1024]{1,0:T(8,128)(2,1)S(1)}, u32[]{:S(2)}, u32[]{:S(2)}) collective-permute-start(bf16[128,1024]{1,0:T(8,128)(2,1)} %refs_0_.3), channel_id=1, source_target_pairs={{1,4},{0,3},{5,8},{4,1},{9,12},{8,5},{13,14},{12,9},{15,10},{14,13... | collective-permute-start | bytes 786440 | tf_op jit(solution)/shard_map/ppermute | solution.py:289
  5.7 11.0 %collective-permute-start.9 = (bf16[128,1024]{1,0:T(8,128)(2,1)}, bf16[128,1024]{1,0:T(8,128)(2,1)S(1)}, u32[]{:S(2)}, u32[]{:S(2)}) collective-permute-start(bf16[128,1024]{1,0:T(8,128)(2,1)} %refs_5_.1), channel_id=1, source_target_pairs={{1,4},{0,3},{5,8},{4,1},{9,12},{8,5},{13,14},{12,9},{15,10},{14,13... | collective-permute-start | bytes 786440 | tf_op jit(solution)/shard_map/ppermute | solution.py:289
  7.8 1.5 %copy-start = (bf16[1,56,128,128]{3,2,1,0:T(8,128)(2,1)S(1)}, bf16[1,56,128,128]{3,2,1,0:T(8,128)(2,1)}, u32[]{:S(2)}) copy-start(bf16[1,56,128,128]{3,2,1,0:T(8,128)(2,1)} %param.9) | copy-start | bytes 5505028
  9.3 0.7 copy-start.6
  13.3 6.4 %collective-permute-start.4 = (bf16[128,1024]{1,0:T(8,128)(2,1)S(1)}, bf16[128,1024]{1,0:T(8,128)(2,1)S(1)}, u32[]{:S(2)}, u32[]{:S(2)}) collective-permute-start(bf16[128,1024]{1,0:T(8,128)(2,1)S(1)} %collective-permute-done.3.refs_5_.refs_6_), channel_id=1, source_target_pairs={{0,4},{1,3},{4,8},{5,1},{8,12},{9,5},{12,14},{13,9},{14,10},{15,13... | collective-permute-start | bytes 786440 | tf_op jit(solution)/shard_map/ppermute | solution.py:271
  15.6 7.7 %collective-permute-start.1 = (bf16[128,1024]{1,0:T(8,128)(2,1)S(1)}, bf16[128,1024]{1,0:T(8,128)(2,1)S(1)}, u32[]{:S(2)}, u32[]{:S(2)}) collective-permute-start(bf16[128,1024]{1,0:T(8,128)(2,1)S(1)} %collective-permute-done.refs_1_), channel_id=1, source_target_pairs={{0,4},{1,3},{4,8},{5,1},{8,12},{9,5},{12,14},{13,9},{14,10},{15,13... | collective-permute-start | bytes 786440 | tf_op jit(solution)/shard_map/ppermute | solution.py:271
  16.6 8.7 %collective-permute-start.10 = (bf16[128,1024]{1,0:T(8,128)(2,1)S(1)}, bf16[128,1024]{1,0:T(8,128)(2,1)S(1)}, u32[]{:S(2)}, u32[]{:S(2)}) collective-permute-start(bf16[128,1024]{1,0:T(8,128)(2,1)S(1)} %collective-permute-done.9.refs_11_.refs_13_), channel_id=1, source_target_pairs={{0,4},{1,3},{4,8},{5,1},{8,12},{9,5},{12,14},{13,9},{14,10},{15,13... | collective-permute-start | bytes 786440 | tf_op jit(solution)/shard_map/ppermute | solution.py:271
  19.7 8.4 %collective-permute-start.5 = (bf16[128,1024]{1,0:T(8,128)(2,1)S(1)}, bf16[128,1024]{1,0:T(8,128)(2,1)S(1)}, u32[]{:S(2)}, u32[]{:S(2)}) collective-permute-start(bf16[128,1024]{1,0:T(8,128)(2,1)S(1)} %collective-permute-done.4.refs_6_.refs_7_), channel_id=1, source_target_pairs={{0,4},{1,3},{4,8},{5,1},{8,12},{9,5},{12,14},{13,9},{14,10},{15,13... | collective-permute-start | bytes 786440 | tf_op jit(solution)/shard_map/ppermute | solution.py:271
  21.9 9.0 %collective-permute-start.7 = (bf16[128,1024]{1,0:T(8,128)(2,1)S(1)}, bf16[128,1024]{1,0:T(8,128)(2,1)S(1)}, u32[]{:S(2)}, u32[]{:S(2)}) collective-permute-start(bf16[128,1024]{1,0:T(8,128)(2,1)S(1)} %collective-permute-done.6.refs_8_.refs_10_), channel_id=1, source_target_pairs={{0,4},{1,3},{4,8},{5,1},{8,12},{9,5},{12,14},{13,9},{14,10},{15,13... | collective-permute-start | bytes 786440 | tf_op jit(solution)/shard_map/ppermute | solution.py:271
  23.3 10.5 %collective-permute-start.2 = (bf16[128,1024]{1,0:T(8,128)(2,1)S(1)}, bf16[128,1024]{1,0:T(8,128)(2,1)S(1)}, u32[]{:S(2)}, u32[]{:S(2)}) collective-permute-start(bf16[128,1024]{1,0:T(8,128)(2,1)S(1)} %collective-permute-done.1.refs_2_), channel_id=1, source_target_pairs={{0,4},{1,3},{4,8},{5,1},{8,12},{9,5},{12,14},{13,9},{14,10},{15,13... | collective-permute-start | bytes 786440 | tf_op jit(solution)/shard_map/ppermute | solution.py:271
  28.2 11.2 %collective-permute-start.11 = (bf16[128,1024]{1,0:T(8,128)(2,1)S(1)}, bf16[128,1024]{1,0:T(8,128)(2,1)S(1)}, u32[]{:S(2)}, u32[]{:S(2)}) collective-permute-start(bf16[128,1024]{1,0:T(8,128)(2,1)S(1)} %collective-permute-done.10.refs_12_.refs_14_), channel_id=1, source_target_pairs={{0,4},{1,3},{4,8},{5,1},{8,12},{9,5},{12,14},{13,9},{14,10},{15,13... | collective-permute-start | bytes 786440 | tf_op jit(solution)/shard_map/ppermute | solution.py:271
  33.8 6.4 %collective-permute-start.8 = (bf16[128,1024]{1,0:T(8,128)(2,1)S(1)}, bf16[128,1024]{1,0:T(8,128)(2,1)S(1)}, u32[]{:S(2)}, u32[]{:S(2)}) collective-permute-start(bf16[128,1024]{1,0:T(8,128)(2,1)S(1)} %collective-permute-done.7.refs_9_.refs_11_), channel_id=1, source_target_pairs={{0,4},{1,3},{4,8},{5,1},{8,12},{9,5},{12,14},{13,9},{14,10},{15,13... | collective-permute-start | bytes 786440 | tf_op jit(solution)/shard_map/ppermute | solution.py:271
  36.0 7.2 %collective-permute-start.12 = (bf16[128,1024]{1,0:T(8,128)(2,1)S(1)}, bf16[128,1024]{1,0:T(8,128)(2,1)S(1)}, u32[]{:S(2)}, u32[]{:S(2)}) collective-permute-start(bf16[128,1024]{1,0:T(8,128)(2,1)S(1)} %collective-permute-done.5.refs_7_.refs_8_), channel_id=1, source_target_pairs={{0,4},{1,3},{4,8},{5,1},{8,12},{9,5},{12,14},{13,9},{14,10},{15,13... | collective-permute-start | bytes 786440 | tf_op jit(solution)/shard_map/ppermute | solution.py:271
  37.1 8.6 %collective-permute-start.14 = (bf16[128,1024]{1,0:T(8,128)(2,1)S(1)}, bf16[128,1024]{1,0:T(8,128)(2,1)S(1)}, u32[]{:S(2)}, u32[]{:S(2)}) collective-permute-start(bf16[128,1024]{1,0:T(8,128)(2,1)S(1)} %collective-permute-done.2.refs_3_), channel_id=1, source_target_pairs={{0,4},{1,3},{4,8},{5,1},{8,12},{9,5},{12,14},{13,9},{14,10},{15,13... | collective-permute-start | bytes 786440 | tf_op jit(solution)/shard_map/ppermute | solution.py:271
  40.2 1.0 %copy-start.1 = (bf16[128,1024]{1,0:T(8,128)(2,1)S(1)}, bf16[128,1024]{1,0:T(8,128)(2,1)}, u32[]{:S(2)}) copy-start(bf16[128,1024]{1,0:T(8,128)(2,1)} %refs_0_.3) | copy-start | bytes 786436
  41.1 0.9 %copy-start.3 = (bf16[128,1024]{1,0:T(8,128)(2,1)S(1)}, bf16[128,1024]{1,0:T(8,128)(2,1)}, u32[]{:S(2)}) copy-start(bf16[128,1024]{1,0:T(8,128)(2,1)} %refs_5_.1) | copy-start | bytes 786436
  43.2 5.7 %copy-start.2 = (bf16[128,1024]{1,0:T(8,128)(2,1)S(1)}, bf16[128,1024]{1,0:T(8,128)(2,1)}, u32[]{:S(2)}) copy-start(bf16[128,1024]{1,0:T(8,128)(2,1)} %refs_0_.3) | copy-start | bytes 786436
  43.2 5.7 %copy-start.4 = (bf16[128,1024]{1,0:T(8,128)(2,1)S(1)}, bf16[128,1024]{1,0:T(8,128)(2,1)}, u32[]{:S(2)}) copy-start(bf16[128,1024]{1,0:T(8,128)(2,1)} %refs_5_.1) | copy-start | bytes 786436
  43.2 5.7 %copy-start.5 = (s32[1,96]{1,0:T(1,128)S(1)}, s32[1,96]{1,0:T(1,128)}, u32[]{:S(2)}) copy-start(s32[1,96]{1,0:T(1,128)} %param.12) | copy-start | bytes 1156
  43.5 5.4 %collective-permute-start.17 = (f32[128,128]{1,0:T(8,128)S(1)}, f32[128,128]{1,0:T(8,128)S(1)}, u32[]{:S(2)}, u32[]{:S(2)}) collective-permute-start(f32[128,128]{1,0:T(8,128)S(1)} %fusion.5), channel_id=1, source_target_pairs={{0,1},{1,0},{2,3},{3,2},{4,5},{5,4},{6,7},{7,6},{8,9},{9,8},{10,11... | collective-permute-start | bytes 196616 | tf_op jit(solution)/shard_map/ppermute | solution.py:272
  43.5 2.6 %collective-permute-start.13 = (f32[128,128]{1,0:T(8,128)S(1)}, f32[128,128]{1,0:T(8,128)S(1)}, u32[]{:S(2)}, u32[]{:S(2)}) collective-permute-start(f32[128,128]{1,0:T(8,128)S(1)} %get-tuple-element.27), channel_id=1, source_target_pairs={{0,1},{1,0},{2,3},{3,2},{4,5},{5,4},{6,7},{7,6},{8,9},{9,8},{10,11... | collective-permute-start | bytes 196616 | tf_op jit(solution)/shard_map/ppermute | solution.py:272
  44.0 2.0 %collective-permute-start.15 = (f32[128,256]{1,0:T(8,128)S(1)}, f32[128,256]{1,0:T(8,128)S(1)}, u32[]{:S(2)}, u32[]{:S(2)}) collective-permute-start(f32[128,256]{1,0:T(8,128)S(1)} %get-tuple-element.29), channel_id=1, source_target_pairs={{0,1},{1,0},{2,3},{3,2},{4,5},{5,4},{6,7},{7,6},{8,9},{9,8},{10,11... | collective-permute-start | bytes 393224 | tf_op jit(solution)/shard_map/ppermute | solution.py:272
  46.1 2.7 %collective-permute-start.18 = (f32[128,256]{1,0:T(8,128)S(1)}, f32[128,256]{1,0:T(8,128)S(1)}, u32[]{:S(2)}, u32[]{:S(2)}) collective-permute-start(f32[128,256]{1,0:T(8,128)S(1)} %get-tuple-element.37), channel_id=1, source_target_pairs={{0,1},{1,0},{2,3},{3,2},{4,5},{5,4},{6,7},{7,6},{8,9},{9,8},{10,11... | collective-permute-start | bytes 393224 | tf_op jit(solution)/shard_map/ppermute | solution.py:272
  46.5 6.4 %collective-permute-start.16 = (bf16[128,1024]{1,0:T(8,128)(2,1)S(1)}, bf16[128,1024]{1,0:T(8,128)(2,1)S(1)}, u32[]{:S(2)}, u32[]{:S(2)}) collective-permute-start(bf16[128,1024]{1,0:T(8,128)(2,1)S(1)} %convolution_convert_fusion.1), channel_id=1, source_target_pairs={{0,4},{1,3},{4,8},{5,1},{8,12},{9,5},{12,14},{13,9},{14,10},{15,13... | collective-permute-start | bytes 786440 | tf_op jit(solution)/shard_map/ppermute | solution.py:271
  53.0 20.3 %collective-permute-start.22 = (bf16[96,128,128]{2,1,0:T(8,128)(2,1)S(1)}, bf16[96,128,128]{2,1,0:T(8,128)(2,1)S(1)}, u32[]{:S(2)}, u32[]{:S(2)}) collective-permute-start(bf16[96,128,128]{2,1,0:T(8,128)(2,1)S(1)} %tile_gradients.1.a_ref), channel_id=1, source_target_pairs={{0,1},{1,0},{2,3},{3,2},{4,5},{5,4},{6,7},{7,6},{8,9},{9,8},{10,11... | collective-permute-start | bytes 9437192 | tf_op jit(solution)/shard_map/ppermute | solution.py:272
  53.4 6.4 %collective-permute-start.23 = (bf16[128,1024]{1,0:T(8,128)(2,1)S(1)}, bf16[128,1024]{1,0:T(8,128)(2,1)S(1)}, u32[]{:S(2)}, u32[]{:S(2)}) collective-permute-start(bf16[128,1024]{1,0:T(8,128)(2,1)S(1)} %convolution_convert_fusion), channel_id=1, source_target_pairs={{0,4},{1,3},{4,8},{5,1},{8,12},{9,5},{12,14},{13,9},{14,10},{15,13... | collective-permute-start | bytes 786440 | tf_op jit(solution)/shard_map/ppermute | solution.py:271
  55.8 6.7 %collective-permute-start.19 = (bf16[128,1024]{1,0:T(8,128)(2,1)S(1)}, bf16[128,1024]{1,0:T(8,128)(2,1)S(1)}, u32[]{:S(2)}, u32[]{:S(2)}) collective-permute-start(bf16[128,1024]{1,0:T(8,128)(2,1)S(1)} %fusion), channel_id=1, source_target_pairs={{0,4},{1,3},{4,8},{5,1},{8,12},{9,5},{12,14},{13,9},{14,10},{15,13... | collective-permute-start | bytes 786440 | tf_op jit(solution)/shard_map/ppermute | solution.py:271
  60.1 6.4 %collective-permute-start.24 = (bf16[128,1024]{1,0:T(8,128)(2,1)S(1)}, bf16[128,1024]{1,0:T(8,128)(2,1)S(1)}, u32[]{:S(2)}, u32[]{:S(2)}) collective-permute-start(bf16[128,1024]{1,0:T(8,128)(2,1)S(1)} %fusion.4), channel_id=1, source_target_pairs={{0,4},{1,3},{4,8},{5,1},{8,12},{9,5},{12,14},{13,9},{14,10},{15,13... | collective-permute-start | bytes 786440 | tf_op jit(solution)/shard_map/ppermute | solution.py:271
  62.9 6.4 %collective-permute-start.20 = (bf16[128,1024]{1,0:T(8,128)(2,1)S(1)}, bf16[128,1024]{1,0:T(8,128)(2,1)S(1)}, u32[]{:S(2)}, u32[]{:S(2)}) collective-permute-start(bf16[128,1024]{1,0:T(8,128)(2,1)S(1)} %fusion.2), channel_id=1, source_target_pairs={{0,4},{1,3},{4,8},{5,1},{8,12},{9,5},{12,14},{13,9},{14,10},{15,13... | collective-permute-start | bytes 786440 | tf_op jit(solution)/shard_map/ppermute | solution.py:271
  66.8 6.4 %collective-permute-start.25 = (bf16[128,1024]{1,0:T(8,128)(2,1)S(1)}, bf16[128,1024]{1,0:T(8,128)(2,1)S(1)}, u32[]{:S(2)}, u32[]{:S(2)}) collective-permute-start(bf16[128,1024]{1,0:T(8,128)(2,1)S(1)} %fusion.3), channel_id=1, source_target_pairs={{0,4},{1,3},{4,8},{5,1},{8,12},{9,5},{12,14},{13,9},{14,10},{15,13... | collective-permute-start | bytes 786440 | tf_op jit(solution)/shard_map/ppermute | solution.py:271
  69.6 6.4 %collective-permute-start.21 = (bf16[128,1024]{1,0:T(8,128)(2,1)S(1)}, bf16[128,1024]{1,0:T(8,128)(2,1)S(1)}, u32[]{:S(2)}, u32[]{:S(2)}) collective-permute-start(bf16[128,1024]{1,0:T(8,128)(2,1)S(1)} %fusion.1), channel_id=1, source_target_pairs={{0,4},{1,3},{4,8},{5,1},{8,12},{9,5},{12,14},{13,9},{14,10},{15,13... | collective-permute-start | bytes 786440 | tf_op jit(solution)/shard_map/ppermute | solution.py:271
  73.2 2.8 %collective-permute-start.26 = (bf16[128,1024]{1,0:T(8,128)(2,1)S(1)}, bf16[128,1024]{1,0:T(8,128)(2,1)S(1)}, u32[]{:S(2)}, u32[]{:S(2)}) collective-permute-start(bf16[128,1024]{1,0:T(8,128)(2,1)S(1)} %collective-permute-done.25), channel_id=1, source_target_pairs={{0,1},{1,0},{2,3},{3,2},{4,5},{5,4},{6,7},{7,6},{8,9},{9,8},{10,11... | collective-permute-start | bytes 786440 | tf_op jit(solution)/shard_map/ppermute | solution.py:272

commit v7 on v5

--- a/solution.py
+++ b/solution.py
@@ -292,6 +292,8 @@
         x_m.append(hop(x_m[-1]))
         y_m.append(hop(y_m[-1]))
         if k < half:
+            x_s[-1], _ = lax.optimization_barrier((x_s[-1], x_m[-1]))
+            y_s[-1], _ = lax.optimization_barrier((y_s[-1], y_m[-1]))
             x_s.append(hop(x_s[-1]))
             y_s.append(hop(y_s[-1]))
 

time: 77.5 us -> 77.5 us (level)
  waiting for transfers between devices: 12.6 us -> 18.3 us
  starting transfers between devices: 44.3 us -> 40.4 us
  Pallas kernels: 9.68 us -> 8.26 us
    ppermute x19, waiting for transfers between devices: 12.6 us -> 17.3 us  [ring_plan(): hop = lambda v: lax.ppermute(v, axes, perm)]
    ppermute x19, starting transfers between devices: 41.7 us -> 37.9 us  [ring_plan(): hop = lambda v: lax.ppermute(v, axes, perm)]
    pallas_call x1, Pallas kernels: 3.24 us -> 1.87 us  [place(): pl.pallas_call(functools.partial(place_kernel, n=n, blocks=blocks, edge=e...]
    ppermute x1, waiting for transfers between devices: 0.01 us -> 0.96 us  [ring_plan(): lax.ppermute(cotangent, axes, cross)]
  transfers between devices with their start and end apart: 27 -> 27, of which waited for: 13 -> 13; matrix products, arithmetic and copies ran while one was open for 4% -> 4% of each run, Pallas kernels for 13% -> 11%
where the time goes in v7:
time: 77.5 us; the launch traced here: 77.2 us
  starting transfers between devices  40.4 us (52%)
  waiting for transfers between devices  18.3 us (24%)
  Pallas kernels  8.26 us (11%)
  local copies, waits for them, and re-layouts  4.07 us (5%)
  matrix products  2.91 us (4%)
  between operations  2.2 us (3%)
  other arithmetic  1.08 us (1%)
    ppermute x19, starting transfers between devices, ring_plan(): hop = lambda v: lax.ppermute(v, axes, perm)  37.9 us
    ppermute x19, waiting for transfers between devices, ring_plan(): hop = lambda v: lax.ppermute(v, axes, perm)  17.3 us
    unnamed x14, local copies, waits for them, and re-layouts  4.07 us
    pallas_call x1, Pallas kernels, tile_grads(): pl.pallas_call(functools.partial(grads_kernel, half=half, blocks=blocks,...  3.23 us
    dot_general x8, matrix products, term(): lax.dot_general(dgu, rows, (((1,), (1,)), ((), ())), preferred_element_ty...  2.45 us
    pallas_call x1, Pallas kernels, sum_grads(): pl.pallas_call(sum_kernel, grid=(slots // size,), in_specs=[pl.BlockSpec(...  2.04 us
    pallas_call x1, Pallas kernels, place(): pl.pallas_call(functools.partial(place_kernel, n=n, blocks=blocks, edge=e...  1.87 us
  transfers between devices with their start and end apart: 27, of which 13 were waited for; matrix products, arithmetic and copies ran while one was open for 4% of the time, Pallas kernels for 11%

profile of v7, /device:TPU:0, one launch (start us, length us, event | category | flops | bytes accessed | tf_op | source)
XLA Modules:
  0.0 77.2 jit_solution(12825587287101917643)
XLA Ops:
  0.6 3.1 %collective-permute-start.3 = (bf16[128,1024]{1,0:T(8,128)(2,1)}, bf16[128,1024]{1,0:T(8,128)(2,1)S(1)}, u32[]{:S(2)}, u32[]{:S(2)}) collective-permute-start(bf16[128,1024]{1,0:T(8,128)(2,1)} %refs_5_.1), channel_id=1, source_target_pairs={{0,4},{1,3},{4,8},{5,1},{8,12},{9,5},{12,14},{13,9},{14,10},{15,13... | collective-permute-start | bytes 786440 | tf_op jit(solution)/shard_map/ppermute | solution.py:271
  3.7 1.6 %collective-permute-start = (bf16[128,1024]{1,0:T(8,128)(2,1)}, bf16[128,1024]{1,0:T(8,128)(2,1)S(1)}, u32[]{:S(2)}, u32[]{:S(2)}) collective-permute-start(bf16[128,1024]{1,0:T(8,128)(2,1)} %refs_0_.3), channel_id=1, source_target_pairs={{0,4},{1,3},{4,8},{5,1},{8,12},{9,5},{12,14},{13,9},{14,10},{15,13... | collective-permute-start | bytes 786440 | tf_op jit(solution)/shard_map/ppermute | solution.py:271
  5.3 0.4 collective-permute-start.6
  5.7 1.4 %collective-permute-start.9 = (bf16[128,1024]{1,0:T(8,128)(2,1)}, bf16[128,1024]{1,0:T(8,128)(2,1)S(1)}, u32[]{:S(2)}, u32[]{:S(2)}) collective-permute-start(bf16[128,1024]{1,0:T(8,128)(2,1)} %refs_5_.1), channel_id=1, source_target_pairs={{1,4},{0,3},{5,8},{4,1},{9,12},{8,5},{13,14},{12,9},{15,10},{14,13... | collective-permute-start | bytes 786440 | tf_op jit(solution)/shard_map/ppermute | solution.py:289
  7.7 0.1 pad_add_fusion.here_ref
  7.8 1.5 %copy-done = bf16[1,56,128,128]{3,2,1,0:T(8,128)(2,1)S(1)} copy-done((bf16[1,56,128,128]{3,2,1,0:T(8,128)(2,1)S(1)}, bf16[1,56,128,128]{3,2,1,0:T(8,128)(2,1)}, u32[]{:S(2)}) %copy-start) | copy-done | bytes 1835032
  9.3 0.7 copy-done.6
  9.9 1.9 %place_weights.1 = (bf16[8192,256]{1,0:T(8,128)(2,1)S(1)}, bf16[8192,128]{1,0:T(8,128)(2,1)S(1)}) custom-call(s32[2]{0:T(128)S(1)} %pad_add_fusion.here_ref, s32[56]{0:T(128)S(1)} %bitcast.14, s32[1]{0:T(128)S(6)} %copy.11.cnt_ref, bf16[56,128,128]{2,1,0:T(8,128)(2,1)S(1)} %bitcast.12), custom_call_target="tpu_custom_call" | custom-call | flops 1 | bytes 1 | tf_op jit(solution)/shard_map/place_weights/pallas_call | solution.py:131
  11.8 3.2 %collective-permute-start.4 = (bf16[128,1024]{1,0:T(8,128)(2,1)S(1)}, bf16[128,1024]{1,0:T(8,128)(2,1)S(1)}, u32[]{:S(2)}, u32[]{:S(2)}) collective-permute-start(bf16[128,1024]{1,0:T(8,128)(2,1)S(1)} %collective-permute-done.3.refs_5_.refs_6_), channel_id=1, source_target_pairs={{0,4},{1,3},{4,8},{5,1},{8,12},{9,5},{12,14},{13,9},{14,10},{15,13... | collective-permute-start | bytes 786440 | tf_op jit(solution)/shard_map/ppermute | solution.py:271
  15.0 1.4 %collective-permute-start.1 = (bf16[128,1024]{1,0:T(8,128)(2,1)S(1)}, bf16[128,1024]{1,0:T(8,128)(2,1)S(1)}, u32[]{:S(2)}, u32[]{:S(2)}) collective-permute-start(bf16[128,1024]{1,0:T(8,128)(2,1)S(1)} %collective-permute-done.refs_1_), channel_id=1, source_target_pairs={{0,4},{1,3},{4,8},{5,1},{8,12},{9,5},{12,14},{13,9},{14,10},{15,13... | collective-permute-start | bytes 786440 | tf_op jit(solution)/shard_map/ppermute | solution.py:271
  16.4 1.0 %collective-permute-done.9.refs_11_.refs_13_ = bf16[128,1024]{1,0:T(8,128)(2,1)S(1)} collective-permute-done((bf16[128,1024]{1,0:T(8,128)(2,1)}, bf16[128,1024]{1,0:T(8,128)(2,1)S(1)}, u32[]{:S(2)}, u32[]{:S(2)}) %collective-permute-start.9) | collective-permute-done | bytes 262176 | tf_op jit(solution)/shard_map/ppermute | solution.py:289
  17.4 2.0 %collective-permute-done.4.refs_6_.refs_7_ = bf16[128,1024]{1,0:T(8,128)(2,1)S(1)} collective-permute-done((bf16[128,1024]{1,0:T(8,128)(2,1)S(1)}, bf16[128,1024]{1,0:T(8,128)(2,1)S(1)}, u32[]{:S(2)}, u32[]{:S(2)}) %collective-permute-start.4) | collective-permute-done | bytes 262176 | tf_op jit(solution)/shard_map/ppermute | solution.py:271
  19.4 2.1 %collective-permute-start.10 = (bf16[128,1024]{1,0:T(8,128)(2,1)S(1)}, bf16[128,1024]{1,0:T(8,128)(2,1)S(1)}, u32[]{:S(2)}, u32[]{:S(2)}) collective-permute-start(bf16[128,1024]{1,0:T(8,128)(2,1)S(1)} %collective-permute-done.9.refs_11_.refs_13_), channel_id=1, source_target_pairs={{0,4},{1,3},{4,8},{5,1},{8,12},{9,5},{12,14},{13,9},{14,10},{15,13... | collective-permute-start | bytes 786440 | tf_op jit(solution)/shard_map/ppermute | solution.py:271
  21.5 1.6 %collective-permute-start.5 = (bf16[128,1024]{1,0:T(8,128)(2,1)S(1)}, bf16[128,1024]{1,0:T(8,128)(2,1)S(1)}, u32[]{:S(2)}, u32[]{:S(2)}) collective-permute-start(bf16[128,1024]{1,0:T(8,128)(2,1)S(1)} %collective-permute-done.4.refs_6_.refs_7_), channel_id=1, source_target_pairs={{0,4},{1,3},{4,8},{5,1},{8,12},{9,5},{12,14},{13,9},{14,10},{15,13... | collective-permute-start | bytes 786440 | tf_op jit(solution)/shard_map/ppermute | solution.py:271
  23.1 1.6 %collective-permute-start.7 = (bf16[128,1024]{1,0:T(8,128)(2,1)S(1)}, bf16[128,1024]{1,0:T(8,128)(2,1)S(1)}, u32[]{:S(2)}, u32[]{:S(2)}) collective-permute-start(bf16[128,1024]{1,0:T(8,128)(2,1)S(1)} %collective-permute-done.6.refs_8_.refs_10_), channel_id=1, source_target_pairs={{0,4},{1,3},{4,8},{5,1},{8,12},{9,5},{12,14},{13,9},{14,10},{15,13... | collective-permute-start | bytes 786440 | tf_op jit(solution)/shard_map/ppermute | solution.py:271
  24.7 1.5 %collective-permute-start.2 = (bf16[128,1024]{1,0:T(8,128)(2,1)S(1)}, bf16[128,1024]{1,0:T(8,128)(2,1)S(1)}, u32[]{:S(2)}, u32[]{:S(2)}) collective-permute-start(bf16[128,1024]{1,0:T(8,128)(2,1)S(1)} %collective-permute-done.1.refs_2_), channel_id=1, source_target_pairs={{0,4},{1,3},{4,8},{5,1},{8,12},{9,5},{12,14},{13,9},{14,10},{15,13... | collective-permute-start | bytes 786440 | tf_op jit(solution)/shard_map/ppermute | solution.py:271
  26.2 2.4 %collective-permute-done.5.refs_7_.refs_8_ = bf16[128,1024]{1,0:T(8,128)(2,1)S(1)} collective-permute-done((bf16[128,1024]{1,0:T(8,128)(2,1)S(1)}, bf16[128,1024]{1,0:T(8,128)(2,1)S(1)}, u32[]{:S(2)}, u32[]{:S(2)}) %collective-permute-start.5) | collective-permute-done | bytes 262176 | tf_op jit(solution)/shard_map/ppermute | solution.py:271
  28.6 2.1 %collective-permute-start.11 = (bf16[128,1024]{1,0:T(8,128)(2,1)S(1)}, bf16[128,1024]{1,0:T(8,128)(2,1)S(1)}, u32[]{:S(2)}, u32[]{:S(2)}) collective-permute-start(bf16[128,1024]{1,0:T(8,128)(2,1)S(1)} %collective-permute-done.10.refs_12_.refs_14_), channel_id=1, source_target_pairs={{0,4},{1,3},{4,8},{5,1},{8,12},{9,5},{12,14},{13,9},{14,10},{15,13... | collective-permute-start | bytes 786440 | tf_op jit(solution)/shard_map/ppermute | solution.py:271
  30.7 0.7 collective-permute-done.7.refs_9_.refs_11_
  31.4 2.8 %collective-permute-done.2.refs_3_ = bf16[128,1024]{1,0:T(8,128)(2,1)S(1)} collective-permute-done((bf16[128,1024]{1,0:T(8,128)(2,1)S(1)}, bf16[128,1024]{1,0:T(8,128)(2,1)S(1)}, u32[]{:S(2)}, u32[]{:S(2)}) %collective-permute-start.2) | collective-permute-done | bytes 262176 | tf_op jit(solution)/shard_map/ppermute | solution.py:271
  34.2 2.1 %collective-permute-start.8 = (bf16[128,1024]{1,0:T(8,128)(2,1)S(1)}, bf16[128,1024]{1,0:T(8,128)(2,1)S(1)}, u32[]{:S(2)}, u32[]{:S(2)}) collective-permute-start(bf16[128,1024]{1,0:T(8,128)(2,1)S(1)} %collective-permute-done.7.refs_9_.refs_11_), channel_id=1, source_target_pairs={{0,4},{1,3},{4,8},{5,1},{8,12},{9,5},{12,14},{13,9},{14,10},{15,13... | collective-permute-start | bytes 786440 | tf_op jit(solution)/shard_map/ppermute | solution.py:271
  36.3 1.6 %collective-permute-start.12 = (bf16[128,1024]{1,0:T(8,128)(2,1)S(1)}, bf16[128,1024]{1,0:T(8,128)(2,1)S(1)}, u32[]{:S(2)}, u32[]{:S(2)}) collective-permute-start(bf16[128,1024]{1,0:T(8,128)(2,1)S(1)} %collective-permute-done.5.refs_7_.refs_8_), channel_id=1, source_target_pairs={{0,4},{1,3},{4,8},{5,1},{8,12},{9,5},{12,14},{13,9},{14,10},{15,13... | collective-permute-start | bytes 786440 | tf_op jit(solution)/shard_map/ppermute | solution.py:271
  37.9 1.6 %collective-permute-start.14 = (bf16[128,1024]{1,0:T(8,128)(2,1)S(1)}, bf16[128,1024]{1,0:T(8,128)(2,1)S(1)}, u32[]{:S(2)}, u32[]{:S(2)}) collective-permute-start(bf16[128,1024]{1,0:T(8,128)(2,1)S(1)} %collective-permute-done.2.refs_3_), channel_id=1, source_target_pairs={{0,4},{1,3},{4,8},{5,1},{8,12},{9,5},{12,14},{13,9},{14,10},{15,13... | collective-permute-start | bytes 786440 | tf_op jit(solution)/shard_map/ppermute | solution.py:271
  40.1 0.5 collective-permute-done.8.refs_10_.refs_12_
  40.6 0.9 %copy-done.1 = bf16[128,1024]{1,0:T(8,128)(2,1)S(1)} copy-done((bf16[128,1024]{1,0:T(8,128)(2,1)S(1)}, bf16[128,1024]{1,0:T(8,128)(2,1)}, u32[]{:S(2)}) %copy-start.1) | copy-done | bytes 262168
  41.5 0.9 %copy-done.3 = bf16[128,1024]{1,0:T(8,128)(2,1)S(1)} copy-done((bf16[128,1024]{1,0:T(8,128)(2,1)S(1)}, bf16[128,1024]{1,0:T(8,128)(2,1)}, u32[]{:S(2)}) %copy-start.3) | copy-done | bytes 262168
  42.5 1.1 %forward_terms.1 = (f32[128,256]{1,0:T(8,128)S(1)}, f32[128,128]{1,0:T(8,128)S(1)}, f32[128,256]{1,0:T(8,128)S(1)}, f32[128,128]{1,0:T(8,128)S(1)}) custom-call(bf16[128,1024]{1,0:T(8,128)(2,1)S(1)} %copy-done.1, bf16[128,1024]{1,0:T(8,128)(2,1)S(1)} %collective-permute-done.refs_1_, bf16[128,1024]{1,0:T(8,128)(2,1)S(1)} %collective-permute-done.1.refs_2_, ...), custom_call_target="tpu_custom_call" | custom-call | flops 1 | bytes 1 | tf_op jit(solution)/shard_map/forward_terms/pallas_call | solution.py:171
  43.6 0.0 copy-start.2
  43.6 0.0 copy-start.4
  43.6 0.0 copy-start.5
  43.7 0.2 fusion.5
  43.9 0.1 collective-permute-start.17
  44.0 0.5 collective-permute-start.13
  44.5 0.1 collective-permute-start.15
  44.6 1.7 %collective-permute-done.14.refs_4_ = bf16[128,1024]{1,0:T(8,128)(2,1)S(1)} collective-permute-done((bf16[128,1024]{1,0:T(8,128)(2,1)S(1)}, bf16[128,1024]{1,0:T(8,128)(2,1)S(1)}, u32[]{:S(2)}, u32[]{:S(2)}) %collective-permute-start.14) | collective-permute-done | bytes 262176 | tf_op jit(solution)/shard_map/ppermute | solution.py:271
  46.2 0.2 fusion.15
  46.5 0.1 collective-permute-start.18
  46.6 0.1 multiply_convert_fusion.5
  46.6 0.3 convolution_convert_fusion.1
  47.0 2.2 %collective-permute-start.16 = (bf16[128,1024]{1,0:T(8,128)(2,1)S(1)}, bf16[128,1024]{1,0:T(8,128)(2,1)S(1)}, u32[]{:S(2)}, u32[]{:S(2)}) collective-permute-start(bf16[128,1024]{1,0:T(8,128)(2,1)S(1)} %convolution_convert_fusion.1), channel_id=1, source_target_pairs={{0,4},{1,3},{4,8},{5,1},{8,12},{9,5},{12,14},{13,9},{14,10},{15,13... | collective-permute-start | bytes 786440 | tf_op jit(solution)/shard_map/ppermute | solution.py:271
  49.2 0.1 multiply_convert_fusion.3
  49.3 3.2 %tile_gradients.1.a_ref = bf16[96,128,128]{2,1,0:T(8,128)(2,1)S(1)} custom-call(s32[2]{0:T(128)S(1)} %pad_add_fusion.here_ref, s32[96]{0:T(128)S(1)} %bitcast.13, s32[1]{0:T(128)S(6)} %copy.12.cnt_ref, bf16[128,1024]{1,0:T(8,128)(2,1)S(1)} %copy-done.2, bf16[128,1024]{1,0:T(8,128)(2,1)S(1)} %collective-permute-done.refs_1_, ...), custom_call_target="tpu_custom_call" | custom-call | flops 1 | bytes 1 | tf_op jit(solution)/shard_map/tile_gradients/pallas_call | solution.py:229
  52.5 0.9 %collective-permute-done.16 = bf16[128,1024]{1,0:T(8,128)(2,1)S(1)} collective-permute-done((bf16[128,1024]{1,0:T(8,128)(2,1)S(1)}, bf16[128,1024]{1,0:T(8,128)(2,1)S(1)}, u32[]{:S(2)}, u32[]{:S(2)}) %collective-permute-start.16) | collective-permute-done | bytes 262176 | tf_op jit(solution)/shard_map/ppermute | solution.py:271
  53.4 0.3 convolution_convert_fusion
  53.7 2.2 %collective-permute-start.23 = (bf16[128,1024]{1,0:T(8,128)(2,1)S(1)}, bf16[128,1024]{1,0:T(8,128)(2,1)S(1)}, u32[]{:S(2)}, u32[]{:S(2)}) collective-permute-start(bf16[128,1024]{1,0:T(8,128)(2,1)S(1)} %convolution_convert_fusion), channel_id=1, source_target_pairs={{0,4},{1,3},{4,8},{5,1},{8,12},{9,5},{12,14},{13,9},{14,10},{15,13... | collective-permute-start | bytes 786440 | tf_op jit(solution)/shard_map/ppermute | solution.py:271
  55.9 0.3 fusion
  56.2 1.6 %collective-permute-start.19 = (bf16[128,1024]{1,0:T(8,128)(2,1)S(1)}, bf16[128,1024]{1,0:T(8,128)(2,1)S(1)}, u32[]{:S(2)}, u32[]{:S(2)}) collective-permute-start(bf16[128,1024]{1,0:T(8,128)(2,1)S(1)} %fusion), channel_id=1, source_target_pairs={{0,4},{1,3},{4,8},{5,1},{8,12},{9,5},{12,14},{13,9},{14,10},{15,13... | collective-permute-start | bytes 786440 | tf_op jit(solution)/shard_map/ppermute | solution.py:271
  57.8 2.3 %collective-permute-done.23 = bf16[128,1024]{1,0:T(8,128)(2,1)S(1)} collective-permute-done((bf16[128,1024]{1,0:T(8,128)(2,1)S(1)}, bf16[128,1024]{1,0:T(8,128)(2,1)S(1)}, u32[]{:S(2)}, u32[]{:S(2)}) %collective-permute-start.23) | collective-permute-done | bytes 262176 | tf_op jit(solution)/shard_map/ppermute | solution.py:271
  60.1 0.3 fusion.4
  60.4 2.2 %collective-permute-start.24 = (bf16[128,1024]{1,0:T(8,128)(2,1)S(1)}, bf16[128,1024]{1,0:T(8,128)(2,1)S(1)}, u32[]{:S(2)}, u32[]{:S(2)}) collective-permute-start(bf16[128,1024]{1,0:T(8,128)(2,1)S(1)} %fusion.4), channel_id=1, source_target_pairs={{0,4},{1,3},{4,8},{5,1},{8,12},{9,5},{12,14},{13,9},{14,10},{15,13... | collective-permute-start | bytes 786440 | tf_op jit(solution)/shard_map/ppermute | solution.py:271
  62.6 0.3 fusion.6
  62.9 0.0 collective-permute-done.19
  62.9 0.3 fusion.2
  63.3 2.2 %collective-permute-start.20 = (bf16[128,1024]{1,0:T(8,128)(2,1)S(1)}, bf16[128,1024]{1,0:T(8,128)(2,1)S(1)}, u32[]{:S(2)}, u32[]{:S(2)}) collective-permute-start(bf16[128,1024]{1,0:T(8,128)(2,1)S(1)} %fusion.2), channel_id=1, source_target_pairs={{0,4},{1,3},{4,8},{5,1},{8,12},{9,5},{12,14},{13,9},{14,10},{15,13... | collective-permute-start | bytes 786440 | tf_op jit(solution)/shard_map/ppermute | solution.py:271
  65.4 1.5 %collective-permute-done.24 = bf16[128,1024]{1,0:T(8,128)(2,1)S(1)} collective-permute-done((bf16[128,1024]{1,0:T(8,128)(2,1)S(1)}, bf16[128,1024]{1,0:T(8,128)(2,1)S(1)}, u32[]{:S(2)}, u32[]{:S(2)}) %collective-permute-start.24) | collective-permute-done | bytes 262176 | tf_op jit(solution)/shard_map/ppermute | solution.py:271
  66.9 0.3 fusion.3
  67.2 2.2 %collective-permute-start.25 = (bf16[128,1024]{1,0:T(8,128)(2,1)S(1)}, bf16[128,1024]{1,0:T(8,128)(2,1)S(1)}, u32[]{:S(2)}, u32[]{:S(2)}) collective-permute-start(bf16[128,1024]{1,0:T(8,128)(2,1)S(1)} %fusion.3), channel_id=1, source_target_pairs={{0,4},{1,3},{4,8},{5,1},{8,12},{9,5},{12,14},{13,9},{14,10},{15,13... | collective-permute-start | bytes 786440 | tf_op jit(solution)/shard_map/ppermute | solution.py:271
  69.3 0.3 collective-permute-done.20
  69.7 0.3 fusion.1
  70.0 2.2 %collective-permute-start.21 = (bf16[128,1024]{1,0:T(8,128)(2,1)S(1)}, bf16[128,1024]{1,0:T(8,128)(2,1)S(1)}, u32[]{:S(2)}, u32[]{:S(2)}) collective-permute-start(bf16[128,1024]{1,0:T(8,128)(2,1)S(1)} %fusion.1), channel_id=1, source_target_pairs={{0,4},{1,3},{4,8},{5,1},{8,12},{9,5},{12,14},{13,9},{14,10},{15,13... | collective-permute-start | bytes 786440 | tf_op jit(solution)/shard_map/ppermute | solution.py:271
  72.2 1.5 %collective-permute-done.25 = bf16[128,1024]{1,0:T(8,128)(2,1)S(1)} collective-permute-done((bf16[128,1024]{1,0:T(8,128)(2,1)S(1)}, bf16[128,1024]{1,0:T(8,128)(2,1)S(1)}, u32[]{:S(2)}, u32[]{:S(2)}) %collective-permute-start.25) | collective-permute-done | bytes 262176 | tf_op jit(solution)/shard_map/ppermute | solution.py:271
  73.6 2.0 %sum_tile_gradients.1 = bf16[96,128,128]{2,1,0:T(8,128)(2,1)} custom-call(bf16[96,128,128]{2,1,0:T(8,128)(2,1)S(1)} %tile_gradients.1.a_ref, bf16[96,128,128]{2,1,0:T(8,128)(2,1)S(1)} %collective-permute-done.22.b_ref), custom_call_target="tpu_custom_call" | custom-call | flops 1 | bytes 1 | tf_op jit(solution)/shard_map/sum_tile_gradients/pallas_call | solution.py:250
  75.7 0.8 collective-permute-done.21
  76.4 0.8 %add_convert_fusion = bf16[128,1024]{1,0:T(8,128)(2,1)} fusion(bf16[128,1024]{1,0:T(8,128)(2,1)S(1)} %collective-permute-done.26, f32[128,1024]{1,0:T(8,128)S(1)} %fusion.6, bf16[128,1024]{1,0:T(8,128)(2,1)S(1)} %collective-permute-done.21), kind=kLoop, calls=%fused_computation.14 | loop fusion | flops 655360 | bytes 1310720 | tf_op jit(solution)/shard_map/convert_element_type | solution.py:335
  (26 shorter events, 0.1 us)
Async XLA Ops:
  0.6 11.2 %collective-permute-start.3 = (bf16[128,1024]{1,0:T(8,128)(2,1)}, bf16[128,1024]{1,0:T(8,128)(2,1)S(1)}, u32[]{:S(2)}, u32[]{:S(2)}) collective-permute-start(bf16[128,1024]{1,0:T(8,128)(2,1)} %refs_5_.1), channel_id=1, source_target_pairs={{0,4},{1,3},{4,8},{5,1},{8,12},{9,5},{12,14},{13,9},{14,10},{15,13... | collective-permute-start | bytes 786440 | tf_op jit(solution)/shard_map/ppermute | solution.py:271
  3.7 11.3 %collective-permute-start = (bf16[128,1024]{1,0:T(8,128)(2,1)}, bf16[128,1024]{1,0:T(8,128)(2,1)S(1)}, u32[]{:S(2)}, u32[]{:S(2)}) collective-permute-start(bf16[128,1024]{1,0:T(8,128)(2,1)} %refs_0_.3), channel_id=1, source_target_pairs={{0,4},{1,3},{4,8},{5,1},{8,12},{9,5},{12,14},{13,9},{14,10},{15,13... | collective-permute-start | bytes 786440 | tf_op jit(solution)/shard_map/ppermute | solution.py:271
  5.3 17.8 %collective-permute-start.6 = (bf16[128,1024]{1,0:T(8,128)(2,1)}, bf16[128,1024]{1,0:T(8,128)(2,1)S(1)}, u32[]{:S(2)}, u32[]{:S(2)}) collective-permute-start(bf16[128,1024]{1,0:T(8,128)(2,1)} %refs_0_.3), channel_id=1, source_target_pairs={{1,4},{0,3},{5,8},{4,1},{9,12},{8,5},{13,14},{12,9},{15,10},{14,13... | collective-permute-start | bytes 786440 | tf_op jit(solution)/shard_map/ppermute | solution.py:289
  5.7 11.7 %collective-permute-start.9 = (bf16[128,1024]{1,0:T(8,128)(2,1)}, bf16[128,1024]{1,0:T(8,128)(2,1)S(1)}, u32[]{:S(2)}, u32[]{:S(2)}) collective-permute-start(bf16[128,1024]{1,0:T(8,128)(2,1)} %refs_5_.1), channel_id=1, source_target_pairs={{1,4},{0,3},{5,8},{4,1},{9,12},{8,5},{13,14},{12,9},{15,10},{14,13... | collective-permute-start | bytes 786440 | tf_op jit(solution)/shard_map/ppermute | solution.py:289
  7.8 1.5 %copy-start = (bf16[1,56,128,128]{3,2,1,0:T(8,128)(2,1)S(1)}, bf16[1,56,128,128]{3,2,1,0:T(8,128)(2,1)}, u32[]{:S(2)}) copy-start(bf16[1,56,128,128]{3,2,1,0:T(8,128)(2,1)} %param.9) | copy-start | bytes 5505028
  9.3 0.7 copy-start.6
  11.8 7.6 %collective-permute-start.4 = (bf16[128,1024]{1,0:T(8,128)(2,1)S(1)}, bf16[128,1024]{1,0:T(8,128)(2,1)S(1)}, u32[]{:S(2)}, u32[]{:S(2)}) collective-permute-start(bf16[128,1024]{1,0:T(8,128)(2,1)S(1)} %collective-permute-done.3.refs_5_.refs_6_), channel_id=1, source_target_pairs={{0,4},{1,3},{4,8},{5,1},{8,12},{9,5},{12,14},{13,9},{14,10},{15,13... | collective-permute-start | bytes 786440 | tf_op jit(solution)/shard_map/ppermute | solution.py:271
  15.0 8.1 %collective-permute-start.1 = (bf16[128,1024]{1,0:T(8,128)(2,1)S(1)}, bf16[128,1024]{1,0:T(8,128)(2,1)S(1)}, u32[]{:S(2)}, u32[]{:S(2)}) collective-permute-start(bf16[128,1024]{1,0:T(8,128)(2,1)S(1)} %collective-permute-done.refs_1_), channel_id=1, source_target_pairs={{0,4},{1,3},{4,8},{5,1},{8,12},{9,5},{12,14},{13,9},{14,10},{15,13... | collective-permute-start | bytes 786440 | tf_op jit(solution)/shard_map/ppermute | solution.py:271
  19.4 6.8 %collective-permute-start.10 = (bf16[128,1024]{1,0:T(8,128)(2,1)S(1)}, bf16[128,1024]{1,0:T(8,128)(2,1)S(1)}, u32[]{:S(2)}, u32[]{:S(2)}) collective-permute-start(bf16[128,1024]{1,0:T(8,128)(2,1)S(1)} %collective-permute-done.9.refs_11_.refs_13_), channel_id=1, source_target_pairs={{0,4},{1,3},{4,8},{5,1},{8,12},{9,5},{12,14},{13,9},{14,10},{15,13... | collective-permute-start | bytes 786440 | tf_op jit(solution)/shard_map/ppermute | solution.py:271
  21.5 7.1 %collective-permute-start.5 = (bf16[128,1024]{1,0:T(8,128)(2,1)S(1)}, bf16[128,1024]{1,0:T(8,128)(2,1)S(1)}, u32[]{:S(2)}, u32[]{:S(2)}) collective-permute-start(bf16[128,1024]{1,0:T(8,128)(2,1)S(1)} %collective-permute-done.4.refs_6_.refs_7_), channel_id=1, source_target_pairs={{0,4},{1,3},{4,8},{5,1},{8,12},{9,5},{12,14},{13,9},{14,10},{15,13... | collective-permute-start | bytes 786440 | tf_op jit(solution)/shard_map/ppermute | solution.py:271
  23.1 8.3 %collective-permute-start.7 = (bf16[128,1024]{1,0:T(8,128)(2,1)S(1)}, bf16[128,1024]{1,0:T(8,128)(2,1)S(1)}, u32[]{:S(2)}, u32[]{:S(2)}) collective-permute-start(bf16[128,1024]{1,0:T(8,128)(2,1)S(1)} %collective-permute-done.6.refs_8_.refs_10_), channel_id=1, source_target_pairs={{0,4},{1,3},{4,8},{5,1},{8,12},{9,5},{12,14},{13,9},{14,10},{15,13... | collective-permute-start | bytes 786440 | tf_op jit(solution)/shard_map/ppermute | solution.py:271
  24.7 9.5 %collective-permute-start.2 = (bf16[128,1024]{1,0:T(8,128)(2,1)S(1)}, bf16[128,1024]{1,0:T(8,128)(2,1)S(1)}, u32[]{:S(2)}, u32[]{:S(2)}) collective-permute-start(bf16[128,1024]{1,0:T(8,128)(2,1)S(1)} %collective-permute-done.1.refs_2_), channel_id=1, source_target_pairs={{0,4},{1,3},{4,8},{5,1},{8,12},{9,5},{12,14},{13,9},{14,10},{15,13... | collective-permute-start | bytes 786440 | tf_op jit(solution)/shard_map/ppermute | solution.py:271
  28.6 11.5 %collective-permute-start.11 = (bf16[128,1024]{1,0:T(8,128)(2,1)S(1)}, bf16[128,1024]{1,0:T(8,128)(2,1)S(1)}, u32[]{:S(2)}, u32[]{:S(2)}) collective-permute-start(bf16[128,1024]{1,0:T(8,128)(2,1)S(1)} %collective-permute-done.10.refs_12_.refs_14_), channel_id=1, source_target_pairs={{0,4},{1,3},{4,8},{5,1},{8,12},{9,5},{12,14},{13,9},{14,10},{15,13... | collective-permute-start | bytes 786440 | tf_op jit(solution)/shard_map/ppermute | solution.py:271
  34.2 6.4 %collective-permute-start.8 = (bf16[128,1024]{1,0:T(8,128)(2,1)S(1)}, bf16[128,1024]{1,0:T(8,128)(2,1)S(1)}, u32[]{:S(2)}, u32[]{:S(2)}) collective-permute-start(bf16[128,1024]{1,0:T(8,128)(2,1)S(1)} %collective-permute-done.7.refs_9_.refs_11_), channel_id=1, source_target_pairs={{0,4},{1,3},{4,8},{5,1},{8,12},{9,5},{12,14},{13,9},{14,10},{15,13... | collective-permute-start | bytes 786440 | tf_op jit(solution)/shard_map/ppermute | solution.py:271
  36.3 7.3 %collective-permute-start.12 = (bf16[128,1024]{1,0:T(8,128)(2,1)S(1)}, bf16[128,1024]{1,0:T(8,128)(2,1)S(1)}, u32[]{:S(2)}, u32[]{:S(2)}) collective-permute-start(bf16[128,1024]{1,0:T(8,128)(2,1)S(1)} %collective-permute-done.5.refs_7_.refs_8_), channel_id=1, source_target_pairs={{0,4},{1,3},{4,8},{5,1},{8,12},{9,5},{12,14},{13,9},{14,10},{15,13... | collective-permute-start | bytes 786440 | tf_op jit(solution)/shard_map/ppermute | solution.py:271
  37.9 8.3 %collective-permute-start.14 = (bf16[128,1024]{1,0:T(8,128)(2,1)S(1)}, bf16[128,1024]{1,0:T(8,128)(2,1)S(1)}, u32[]{:S(2)}, u32[]{:S(2)}) collective-permute-start(bf16[128,1024]{1,0:T(8,128)(2,1)S(1)} %collective-permute-done.2.refs_3_), channel_id=1, source_target_pairs={{0,4},{1,3},{4,8},{5,1},{8,12},{9,5},{12,14},{13,9},{14,10},{15,13... | collective-permute-start | bytes 786440 | tf_op jit(solution)/shard_map/ppermute | solution.py:271
  40.6 1.0 %copy-start.1 = (bf16[128,1024]{1,0:T(8,128)(2,1)S(1)}, bf16[128,1024]{1,0:T(8,128)(2,1)}, u32[]{:S(2)}) copy-start(bf16[128,1024]{1,0:T(8,128)(2,1)} %refs_0_.3) | copy-start | bytes 786436
  41.5 0.9 %copy-start.3 = (bf16[128,1024]{1,0:T(8,128)(2,1)S(1)}, bf16[128,1024]{1,0:T(8,128)(2,1)}, u32[]{:S(2)}) copy-start(bf16[128,1024]{1,0:T(8,128)(2,1)} %refs_5_.1) | copy-start | bytes 786436
  43.6 5.6 %copy-start.2 = (bf16[128,1024]{1,0:T(8,128)(2,1)S(1)}, bf16[128,1024]{1,0:T(8,128)(2,1)}, u32[]{:S(2)}) copy-start(bf16[128,1024]{1,0:T(8,128)(2,1)} %refs_0_.3) | copy-start | bytes 786436
  43.6 5.6 %copy-start.4 = (bf16[128,1024]{1,0:T(8,128)(2,1)S(1)}, bf16[128,1024]{1,0:T(8,128)(2,1)}, u32[]{:S(2)}) copy-start(bf16[128,1024]{1,0:T(8,128)(2,1)} %refs_5_.1) | copy-start | bytes 786436
  43.6 5.6 %copy-start.5 = (s32[1,96]{1,0:T(1,128)S(1)}, s32[1,96]{1,0:T(1,128)}, u32[]{:S(2)}) copy-start(s32[1,96]{1,0:T(1,128)} %param.12) | copy-start | bytes 1156
  43.9 5.3 %collective-permute-start.17 = (f32[128,128]{1,0:T(8,128)S(1)}, f32[128,128]{1,0:T(8,128)S(1)}, u32[]{:S(2)}, u32[]{:S(2)}) collective-permute-start(f32[128,128]{1,0:T(8,128)S(1)} %fusion.5), channel_id=1, source_target_pairs={{0,1},{1,0},{2,3},{3,2},{4,5},{5,4},{6,7},{7,6},{8,9},{9,8},{10,11... | collective-permute-start | bytes 196616 | tf_op jit(solution)/shard_map/ppermute | solution.py:272
  44.0 2.6 %collective-permute-start.13 = (f32[128,128]{1,0:T(8,128)S(1)}, f32[128,128]{1,0:T(8,128)S(1)}, u32[]{:S(2)}, u32[]{:S(2)}) collective-permute-start(f32[128,128]{1,0:T(8,128)S(1)} %get-tuple-element.31), channel_id=1, source_target_pairs={{0,1},{1,0},{2,3},{3,2},{4,5},{5,4},{6,7},{7,6},{8,9},{9,8},{10,11... | collective-permute-start | bytes 196616 | tf_op jit(solution)/shard_map/ppermute | solution.py:272
  44.5 2.0 %collective-permute-start.15 = (f32[128,256]{1,0:T(8,128)S(1)}, f32[128,256]{1,0:T(8,128)S(1)}, u32[]{:S(2)}, u32[]{:S(2)}) collective-permute-start(f32[128,256]{1,0:T(8,128)S(1)} %get-tuple-element.33), channel_id=1, source_target_pairs={{0,1},{1,0},{2,3},{3,2},{4,5},{5,4},{6,7},{7,6},{8,9},{9,8},{10,11... | collective-permute-start | bytes 393224 | tf_op jit(solution)/shard_map/ppermute | solution.py:272
  46.5 2.6 %collective-permute-start.18 = (f32[128,256]{1,0:T(8,128)S(1)}, f32[128,256]{1,0:T(8,128)S(1)}, u32[]{:S(2)}, u32[]{:S(2)}) collective-permute-start(f32[128,256]{1,0:T(8,128)S(1)} %get-tuple-element.41), channel_id=1, source_target_pairs={{0,1},{1,0},{2,3},{3,2},{4,5},{5,4},{6,7},{7,6},{8,9},{9,8},{10,11... | collective-permute-start | bytes 393224 | tf_op jit(solution)/shard_map/ppermute | solution.py:272
  47.0 6.4 %collective-permute-start.16 = (bf16[128,1024]{1,0:T(8,128)(2,1)S(1)}, bf16[128,1024]{1,0:T(8,128)(2,1)S(1)}, u32[]{:S(2)}, u32[]{:S(2)}) collective-permute-start(bf16[128,1024]{1,0:T(8,128)(2,1)S(1)} %convolution_convert_fusion.1), channel_id=1, source_target_pairs={{0,4},{1,3},{4,8},{5,1},{8,12},{9,5},{12,14},{13,9},{14,10},{15,13... | collective-permute-start | bytes 786440 | tf_op jit(solution)/shard_map/ppermute | solution.py:271
  53.4 20.2 %collective-permute-start.22 = (bf16[96,128,128]{2,1,0:T(8,128)(2,1)S(1)}, bf16[96,128,128]{2,1,0:T(8,128)(2,1)S(1)}, u32[]{:S(2)}, u32[]{:S(2)}) collective-permute-start(bf16[96,128,128]{2,1,0:T(8,128)(2,1)S(1)} %tile_gradients.1.a_ref), channel_id=1, source_target_pairs={{0,1},{1,0},{2,3},{3,2},{4,5},{5,4},{6,7},{7,6},{8,9},{9,8},{10,11... | collective-permute-start | bytes 9437192 | tf_op jit(solution)/shard_map/ppermute | solution.py:272
  53.7 6.4 %collective-permute-start.23 = (bf16[128,1024]{1,0:T(8,128)(2,1)S(1)}, bf16[128,1024]{1,0:T(8,128)(2,1)S(1)}, u32[]{:S(2)}, u32[]{:S(2)}) collective-permute-start(bf16[128,1024]{1,0:T(8,128)(2,1)S(1)} %convolution_convert_fusion), channel_id=1, source_target_pairs={{0,4},{1,3},{4,8},{5,1},{8,12},{9,5},{12,14},{13,9},{14,10},{15,13... | collective-permute-start | bytes 786440 | tf_op jit(solution)/shard_map/ppermute | solution.py:271
  56.2 6.8 %collective-permute-start.19 = (bf16[128,1024]{1,0:T(8,128)(2,1)S(1)}, bf16[128,1024]{1,0:T(8,128)(2,1)S(1)}, u32[]{:S(2)}, u32[]{:S(2)}) collective-permute-start(bf16[128,1024]{1,0:T(8,128)(2,1)S(1)} %fusion), channel_id=1, source_target_pairs={{0,4},{1,3},{4,8},{5,1},{8,12},{9,5},{12,14},{13,9},{14,10},{15,13... | collective-permute-start | bytes 786440 | tf_op jit(solution)/shard_map/ppermute | solution.py:271
  60.4 6.4 %collective-permute-start.24 = (bf16[128,1024]{1,0:T(8,128)(2,1)S(1)}, bf16[128,1024]{1,0:T(8,128)(2,1)S(1)}, u32[]{:S(2)}, u32[]{:S(2)}) collective-permute-start(bf16[128,1024]{1,0:T(8,128)(2,1)S(1)} %fusion.4), channel_id=1, source_target_pairs={{0,4},{1,3},{4,8},{5,1},{8,12},{9,5},{12,14},{13,9},{14,10},{15,13... | collective-permute-start | bytes 786440 | tf_op jit(solution)/shard_map/ppermute | solution.py:271
  63.3 6.4 %collective-permute-start.20 = (bf16[128,1024]{1,0:T(8,128)(2,1)S(1)}, bf16[128,1024]{1,0:T(8,128)(2,1)S(1)}, u32[]{:S(2)}, u32[]{:S(2)}) collective-permute-start(bf16[128,1024]{1,0:T(8,128)(2,1)S(1)} %fusion.2), channel_id=1, source_target_pairs={{0,4},{1,3},{4,8},{5,1},{8,12},{9,5},{12,14},{13,9},{14,10},{15,13... | collective-permute-start | bytes 786440 | tf_op jit(solution)/shard_map/ppermute | solution.py:271
  67.2 6.4 %collective-permute-start.25 = (bf16[128,1024]{1,0:T(8,128)(2,1)S(1)}, bf16[128,1024]{1,0:T(8,128)(2,1)S(1)}, u32[]{:S(2)}, u32[]{:S(2)}) collective-permute-start(bf16[128,1024]{1,0:T(8,128)(2,1)S(1)} %fusion.3), channel_id=1, source_target_pairs={{0,4},{1,3},{4,8},{5,1},{8,12},{9,5},{12,14},{13,9},{14,10},{15,13... | collective-permute-start | bytes 786440 | tf_op jit(solution)/shard_map/ppermute | solution.py:271
  70.0 6.4 %collective-permute-start.21 = (bf16[128,1024]{1,0:T(8,128)(2,1)S(1)}, bf16[128,1024]{1,0:T(8,128)(2,1)S(1)}, u32[]{:S(2)}, u32[]{:S(2)}) collective-permute-start(bf16[128,1024]{1,0:T(8,128)(2,1)S(1)} %fusion.1), channel_id=1, source_target_pairs={{0,4},{1,3},{4,8},{5,1},{8,12},{9,5},{12,14},{13,9},{14,10},{15,13... | collective-permute-start | bytes 786440 | tf_op jit(solution)/shard_map/ppermute | solution.py:271
  73.6 2.8 %collective-permute-start.26 = (bf16[128,1024]{1,0:T(8,128)(2,1)S(1)}, bf16[128,1024]{1,0:T(8,128)(2,1)S(1)}, u32[]{:S(2)}, u32[]{:S(2)}) collective-permute-start(bf16[128,1024]{1,0:T(8,128)(2,1)S(1)} %collective-permute-done.25), channel_id=1, source_target_pairs={{0,1},{1,0},{2,3},{3,2},{4,5},{5,4},{6,7},{7,6},{8,9},{9,8},{10,11... | collective-permute-start | bytes 786440 | tf_op jit(solution)/shard_map/ppermute | solution.py:272
